TPU v7x, 32 devices: a whole 2x2x4 slice. The times are simulated.
32 devices in a mesh: energy: 8 (over y, x, core), slab: 4 (over z).
Axes of the slice: x: 2, y: 2, z: 4, core: 2. Of those that a mesh axis runs over, the one named last changes fastest.
Arguments:
- green_diag: float32 [4, 256, 2, 128, 128], P('slab', 'energy'), may hold values from -0.375 to 0.375
- green_lower: float32 [4, 256, 2, 128, 128], P('slab', 'energy'), may hold values from -0.375 to 0.375
- green_upper: float32 [4, 256, 2, 128, 128], P('slab', 'energy'), may hold values from -0.375 to 0.375
- sigma_lesser: float32 [4, 256, 2, 128, 128], P('slab', 'energy'), may hold values from -6 to 6
- screened: float32 [4, 256, 2, 128, 128], P('slab', None, None, 'energy'), may hold values from -6 to 6
- pattern: int32 [4, 128], P('slab'), may hold values 0 or 1
Outputs:
- green_lesser: float32 [4, 256, 2, 128, 128], P('slab', 'energy')
All inputs are finite; a program needn't handle non-finite values. No bound on the sum of `pattern` on one device may be relied on, other than what follows from the above.
Results may differ from a plain program's by a relative error of at most 0.0001.
Values sent between devices are 32-bit elements; how exact they have to be, the bound alone decides.
No kernel may reach another device: no remote copies, remote signals or barrier semaphores. Data moves between devices by JAX's collectives and lax.ppermute only.
A program may use at most 128 MiB of HBM per device.

v0:
```python
import math

import jax
import jax.numpy as jnp
from jax import lax
from jax.sharding import PartitionSpec as P


def with_halo(cells, sides, width):
    for axis, dim in sides:
        count = lax.axis_size(axis)
        ends = count - 1
        head = lax.slice_in_dim(cells, 0, width, axis=dim)
        tail = lax.slice_in_dim(cells, cells.shape[dim] - width, cells.shape[dim], axis=dim)
        cells = jnp.concatenate(
            [
                lax.ppermute(tail, axis, [(i, (i + 1) % count) for i in range(ends)]),
                cells,
                lax.ppermute(head, axis, [((i + 1) % count, i) for i in range(ends)]),
            ],
            axis=dim,
        )
    return cells


def matmul_plain(first_op, second_op):
    return jnp.einsum("...ab,...bc->...ac", first_op, second_op, precision=lax.Precision.HIGHEST)


def matmul_adjoint(first_op, second_op):
    return jnp.einsum("...ab,...cb->...ac", first_op, second_op, precision=lax.Precision.HIGHEST)


def sandwich(outer_factor, middle_factor):
    outer_real = outer_factor[..., 0, :, :]
    outer_imag = outer_factor[..., 1, :, :]
    middle_real = middle_factor[..., 0, :, :]
    middle_imag = middle_factor[..., 1, :, :]
    prod_real = matmul_plain(outer_real, middle_real) - matmul_plain(outer_imag, middle_imag)
    prod_imag = matmul_plain(outer_real, middle_imag) + matmul_plain(outer_imag, middle_real)
    final_real = matmul_adjoint(prod_real, outer_real) + matmul_adjoint(prod_imag, outer_imag)
    final_imag = matmul_adjoint(prod_imag, outer_real) - matmul_adjoint(prod_real, outer_imag)
    return jnp.stack([final_real, final_imag], axis=-3)


def lesser_product(green_diag, green_lower, green_upper, sigma_blocks):
    block_count = sigma_blocks.shape[0]
    padded = with_halo(sigma_blocks, (("slab", 0),), 1)
    before = padded[:block_count]
    after = padded[2:]
    own_term = sandwich(green_diag, sigma_blocks)
    return own_term + sandwich(green_lower, before) + sandwich(green_upper, after)


def phase_table(row_count, col_count, period, direction_sign):
    products = (
        lax.broadcasted_iota(jnp.int32, (row_count, col_count), 0)
        * lax.broadcasted_iota(jnp.int32, (row_count, col_count), 1)
        % period
    )
    angles = direction_sign * 2.0 * math.pi / period * products.astype(jnp.float32)
    return (jnp.cos(angles), jnp.sin(angles))


def complex_apply(table, real_part, imag_part, form):
    cosine, sine_part = table
    out_real = jnp.einsum(form, cosine, real_part, precision=lax.Precision.HIGHEST) - jnp.einsum(
        form, sine_part, imag_part, precision=lax.Precision.HIGHEST
    )
    out_imag = jnp.einsum(form, cosine, imag_part, precision=lax.Precision.HIGHEST) + jnp.einsum(
        form, sine_part, real_part, precision=lax.Precision.HIGHEST
    )
    return (out_real, out_imag)


def twiddle(table, real_part, imag_part):
    cosine = table[0][None, :, :, None, None]
    sine_part = table[1][None, :, :, None, None]
    return (real_part * cosine - imag_part * sine_part, real_part * sine_part + imag_part * cosine)


def convolve(moved, screened, groups):
    block_count, total_energy, pair, row_part, width = moved.shape
    local_energy = total_energy // groups
    shaped = moved.reshape(block_count, groups, local_energy, pair, row_part, width)
    real_part = shaped[:, :, :, 0]
    imag_part = shaped[:, :, :, 1]
    real_part, imag_part = complex_apply(
        phase_table(groups, groups, groups, -1.0), real_part, imag_part, "pj,bjlrc->bplrc"
    )
    real_part, imag_part = twiddle(
        phase_table(groups, local_energy, total_energy, -1.0), real_part, imag_part
    )
    real_part, imag_part = complex_apply(
        phase_table(local_energy, local_energy, local_energy, -1.0),
        real_part,
        imag_part,
        "ql,bplrc->bpqrc",
    )
    weights = screened.reshape(block_count, local_energy, groups, pair, row_part, width)
    weight_real = jnp.swapaxes(weights[:, :, :, 0], 1, 2)
    weight_imag = jnp.swapaxes(weights[:, :, :, 1], 1, 2)
    prod_real = real_part * weight_real - imag_part * weight_imag
    prod_imag = real_part * weight_imag + imag_part * weight_real
    prod_real, prod_imag = complex_apply(
        phase_table(local_energy, local_energy, local_energy, 1.0),
        prod_real,
        prod_imag,
        "lq,bpqrc->bplrc",
    )
    prod_real, prod_imag = twiddle(
        phase_table(groups, local_energy, total_energy, 1.0), prod_real, prod_imag
    )
    prod_real, prod_imag = complex_apply(
        phase_table(groups, groups, groups, 1.0), prod_real, prod_imag, "jp,bplrc->bjlrc"
    )
    scale_factor = 1.0 / total_energy
    stacked = jnp.stack([-prod_imag * scale_factor, prod_real * scale_factor], axis=3)
    return stacked.reshape(block_count, total_energy, pair, row_part, width)


def local(green_diag, green_lower, green_upper, sigma_lesser, screened, pattern):
    first_pass = lesser_product(green_diag, green_lower, green_upper, sigma_lesser)
    moved = lax.all_to_all(first_pass, "energy", split_axis=3, concat_axis=1, tiled=True)
    interaction = convolve(moved, screened, lax.axis_size("energy"))
    returned = lax.all_to_all(interaction, "energy", split_axis=1, concat_axis=3, tiled=True)
    mask_float = pattern.astype(jnp.float32)
    kept = mask_float[:, :, None] * mask_float[:, None, :]
    scattering = kept[:, None, None] * returned
    return lesser_product(green_diag, green_lower, green_upper, sigma_lesser + scattering)


def solution(mesh):
    return jax.shard_map(
        local,
        mesh=mesh,
        in_specs=(
            P("slab", "energy", None, None, None),
            P("slab", "energy", None, None, None),
            P("slab", "energy", None, None, None),
            P("slab", "energy", None, None, None),
            P("slab", None, None, "energy", None),
            P("slab", None),
        ),
        out_specs=P("slab", "energy", None, None, None),
        check_vma=False,
    )
```

profile of v0, /device:TPU:18, one launch (start us, length us, event | category | flops | bytes accessed | tf_op | source)
XLA Modules:
  0.0 500.2 jit_solution(8830933661244121831)
XLA Ops:
  18.4 4.5 fusion.76
  23.0 5.0 add_bitcast_fusion.5
  27.9 4.5 fusion.74
  32.4 4.5 subtract_bitcast_fusion.5
  37.0 60.4 %collective-permute-done.1 = f32[1,32,2,128,128]{4,3,1,2,0:T(8,128)S(1)} collective-permute-done((f32[1,32,2,128,128]{4,3,1,2,0:T(8,128)S(1)}, f32[1,32,2,128,128]{4,3,1,2,0:T(8,128)S(1)}, u32[]{:S(2)}, u32[]{:S(2)}) %collective-permute-start.1) | collective-permute-done | bytes 4194336 | tf_op jit(solution)/shard_map/ppermute | solution.py:19
  102.1 4.5 fusion.12
  115.7 4.7 fusion.10
  129.6 4.5 fusion.44
  139.1 4.5 fusion.42
  148.1 4.7 subtract_bitcast_fusion.4
  158.3 5.0 all-to-all-start
  167.6 43.4 %all-to-all-done = f32[1,32,2,128,128]{4,1,2,0,3:T(8,128)} async-done(((f32[1,32,2,128,128]{4,1,2,0,3:T(8,128)}), f32[1,32,2,128,128]{4,1,2,0,3:T(8,128)}, u32[]{:S(2)}, u32[]{:S(2)}) %all-to-all-start) | async-done | bytes 4194336 | tf_op jit(solution)/shard_map/all_to_all | solution.py:124
  211.0 4.6 copy.293
  233.8 5.8 %fusion.108 = (f32[1,8,32,16,128]{4,2,3,1,0:T(8,128)S(1)}, f32[8,32,16,128]{3,1,2,0:T(8,128)S(1)}) fusion(f32[8,16,128,32]{2,3,1,0:T(8,128)S(1)} %fusion.133, f32[1,32,8,1,16,128]{5,4,3,2,1,0:T(8,128)S(1)} %copy-done.7, f32[1,32,8,1,16,128]{5,4,3,2,1,0:T(8,128)S(1)} %get-tuple-element.11, f32[8,16,128,32]{2,3,1,0:T(8,128)S(1)} %fusion.125, ...), kind=kOutput, calls=%fused_computation.135 | convolution fusion | flops 205010944 | bytes 14680064 | tf_op jit(solution)/shard_map/ql,bplrc->bpqrc/dot_general | solution.py:70
  267.3 6.0 %all-to-all-start.1 = ((f32[1,256,2,16,128]{4,3,2,0,1:T(8,128)}), f32[1,256,2,16,128]{4,3,2,0,1:T(8,128)}, u32[]{:S(2)}, u32[]{:S(2)}) async-start(f32[1,256,2,16,128]{4,3,2,0,1:T(8,128)} %copy.197), calls=%async_computation.1 | async-start | bytes 8388608 | tf_op jit(solution)/shard_map/all_to_all | solution.py:126
  273.2 5.6 %copy.200 = f32[1,32,2,128,128]{3,4,1,2,0:T(8,128)} copy(f32[1,32,2,128,128]{4,3,2,1,0:T(8,128)} %param.9) | data formatting | bytes 8388608 | tf_op args[3]
  278.9 42.0 %all-to-all-done.1 = f32[1,256,2,16,128]{4,3,2,0,1:T(8,128)} async-done(((f32[1,256,2,16,128]{4,3,2,0,1:T(8,128)}), f32[1,256,2,16,128]{4,3,2,0,1:T(8,128)}, u32[]{:S(2)}, u32[]{:S(2)}) %all-to-all-start.1) | async-done | bytes 4194336 | tf_op jit(solution)/shard_map/all_to_all | solution.py:126
  320.9 4.8 copy.198
  325.7 5.6 %copy.199 = f32[1,32,2,128,128]{3,4,1,2,0:T(8,128)} copy(f32[1,32,2,128,128]{4,3,2,1,0:T(8,128)} %bitcast.486) | data formatting | bytes 8388608 | tf_op jit(solution)/shard_map/all_to_all | solution.py:126
  342.1 4.5 fusion.70
  346.6 4.5 fusion.72
  351.1 4.5 fusion.166
  355.7 4.5 fusion.161
  375.2 55.0 %collective-permute-done.3 = f32[1,32,2,128,128]{3,4,1,2,0:T(8,128)S(1)} collective-permute-done((f32[1,32,2,128,128]{3,4,1,2,0:T(8,128)S(1)}, f32[1,32,2,128,128]{3,4,1,2,0:T(8,128)S(1)}, u32[]{:S(2)}, u32[]{:S(2)}) %collective-permute-start.3) | collective-permute-done | bytes 4194336 | tf_op jit(solution)/shard_map/ppermute | solution.py:19
  430.2 4.5 fusion.6
  434.8 4.5 fusion.206
  442.9 4.6 fusion.8
  447.5 4.5 fusion.201
  463.2 4.5 fusion.38
  467.7 4.5 fusion.186
  476.3 4.5 fusion.40
  480.8 4.5 fusion.181
  (84 shorter events, 165.5 us)
Async XLA Ops:
  0.0 9.2 %copy-start.6 = (f32[1,32,2,128,128]{4,3,2,1,0:T(8,128)S(1)}, f32[1,32,2,128,128]{4,3,2,1,0:T(8,128)}, u32[]{:S(2)}) copy-start(f32[1,32,2,128,128]{4,3,2,1,0:T(8,128)} %param.9) | copy-start | bytes 12582916
  0.0 9.2 %copy-start = (f32[1,32,2,128,128]{4,3,2,1,0:T(8,128)S(1)}, f32[1,32,2,128,128]{4,3,2,1,0:T(8,128)}, u32[]{:S(2)}) copy-start(f32[1,32,2,128,128]{4,3,2,1,0:T(8,128)} %param.6) | copy-start | bytes 12582916
  2.8 94.5 %collective-permute-start.1 = (f32[1,32,2,128,128]{4,3,1,2,0:T(8,128)S(1)}, f32[1,32,2,128,128]{4,3,1,2,0:T(8,128)S(1)}, u32[]{:S(2)}, u32[]{:S(2)}) collective-permute-start(f32[1,32,2,128,128]{4,3,1,2,0:T(8,128)S(1)} %copy.171), channel_id=1, source_target_pairs={{1,0},{2,1},{3,2},{5,4},{6,5},{7,6},{9,8},{10,9},{11,10},{13,12},{... | collective-permute-start | bytes 12582920 | tf_op jit(solution)/shard_map/ppermute | solution.py:19
  5.5 119.5 %collective-permute-start = (f32[1,32,2,128,128]{4,3,1,2,0:T(8,128)S(1)}, f32[1,32,2,128,128]{4,3,1,2,0:T(8,128)S(1)}, u32[]{:S(2)}, u32[]{:S(2)}) collective-permute-start(f32[1,32,2,128,128]{4,3,1,2,0:T(8,128)S(1)} %copy.171), channel_id=1, source_target_pairs={{0,1},{1,2},{2,3},{4,5},{5,6},{6,7},{8,9},{9,10},{10,11},{12,13},{... | collective-permute-start | bytes 12582920 | tf_op jit(solution)/shard_map/ppermute | solution.py:17
  32.4 64.9 %copy-start.2 = (f32[1,32,2,128,128]{4,3,2,1,0:T(8,128)S(1)}, f32[1,32,2,128,128]{4,3,2,1,0:T(8,128)}, u32[]{:S(2)}) copy-start(f32[1,32,2,128,128]{4,3,2,1,0:T(8,128)} %param.8) | copy-start | bytes 12582916
  120.4 4.5 copy-start.4
  158.3 52.7 %all-to-all-start = ((f32[1,32,2,128,128]{4,1,2,0,3:T(8,128)}), f32[1,32,2,128,128]{4,1,2,0,3:T(8,128)}, u32[]{:S(2)}, u32[]{:S(2)}) async-start(f32[1,32,2,128,128]{4,1,2,0,3:T(8,128)} %copy.180), calls=%async_computation | async-start | bytes 8388608 | tf_op jit(solution)/shard_map/all_to_all | solution.py:124
  230.5 3.3 copy-start.7
  267.3 53.7 %all-to-all-start.1 = ((f32[1,256,2,16,128]{4,3,2,0,1:T(8,128)}), f32[1,256,2,16,128]{4,3,2,0,1:T(8,128)}, u32[]{:S(2)}, u32[]{:S(2)}) async-start(f32[1,256,2,16,128]{4,3,2,0,1:T(8,128)} %copy.197), calls=%async_computation.1 | async-start | bytes 8388608 | tf_op jit(solution)/shard_map/all_to_all | solution.py:126
  273.2 5.6 %copy-start.8 = (s32[1,128]{1,0:T(1,128)S(1)}, s32[1,128]{1,0:T(1,128)}, u32[]{:S(2)}) copy-start(s32[1,128]{1,0:T(1,128)} %param.11) | copy-start | bytes 1540
  331.4 10.8 %copy-start.1 = (f32[1,32,2,128,128]{4,3,2,1,0:T(8,128)S(1)}, f32[1,32,2,128,128]{4,3,2,1,0:T(8,128)}, u32[]{:S(2)}) copy-start(f32[1,32,2,128,128]{4,3,2,1,0:T(8,128)} %param.6) | copy-start | bytes 12582916
  335.8 94.4 %collective-permute-start.3 = (f32[1,32,2,128,128]{3,4,1,2,0:T(8,128)S(1)}, f32[1,32,2,128,128]{3,4,1,2,0:T(8,128)S(1)}, u32[]{:S(2)}, u32[]{:S(2)}) collective-permute-start(f32[1,32,2,128,128]{3,4,1,2,0:T(8,128)S(1)} %multiply_add_fusion), channel_id=1, source_target_pairs={{1,0},{2,1},{3,2},{5,4},{6,5},{7,6},{9,8},{10,9},{11,10},{13,12},{... | collective-permute-start | bytes 12582920 | tf_op jit(solution)/shard_map/ppermute | solution.py:19
  338.2 125.0 %collective-permute-start.2 = (f32[1,32,2,128,128]{3,4,1,2,0:T(8,128)S(1)}, f32[1,32,2,128,128]{3,4,1,2,0:T(8,128)S(1)}, u32[]{:S(2)}, u32[]{:S(2)}) collective-permute-start(f32[1,32,2,128,128]{3,4,1,2,0:T(8,128)S(1)} %multiply_add_fusion), channel_id=1, source_target_pairs={{0,1},{1,2},{2,3},{4,5},{5,6},{6,7},{8,9},{9,10},{10,11},{12,13},{... | collective-permute-start | bytes 12582920 | tf_op jit(solution)/shard_map/ppermute | solution.py:17
  371.2 59.1 %copy-start.3 = (f32[1,32,2,128,128]{4,3,2,1,0:T(8,128)S(1)}, f32[1,32,2,128,128]{4,3,2,1,0:T(8,128)}, u32[]{:S(2)}) copy-start(f32[1,32,2,128,128]{4,3,2,1,0:T(8,128)} %param.8) | copy-start | bytes 12582916
  459.3 3.9 copy-start.5
where the time goes:
time: 510 us; the launch traced here: 500 us
  matrix products  230 us (45%)
  waiting for transfers between devices  201 us (39%)
  local copies, waits for them, and re-layouts  37.9 us (7%)
  starting transfers between devices  23.6 us (5%)
  other arithmetic  7.1 us (1%)
    ppermute x2, waiting for transfers between devices, with_halo(): lax.ppermute(head, axis, [((i + 1) % count, i) for i in range(ends)])  115 us
    dot_general x24, matrix products, matmul_adjoint(): jnp.einsum('...ab,...cb->...ac', first_op, second_op, precision=lax.Preci...  99.8 us
    dot_general x24, matrix products, matmul_plain(): jnp.einsum('...ab,...bc->...ac', first_op, second_op, precision=lax.Preci...  82.6 us
    all_to_all x1, waiting for transfers between devices, local(): lax.all_to_all(first_pass, 'energy', split_axis=3, concat_axis=1, tiled=T...  43.4 us
    all_to_all x1, waiting for transfers between devices, local(): lax.all_to_all(interaction, 'energy', split_axis=1, concat_axis=3, tiled=...  42 us
    dot_general x4, matrix products, complex_apply(): jnp.einsum(form, sine_part, real_part, precision=lax.Precision.HIGHEST)  13.5 us
    dot_general x4, matrix products, complex_apply(): jnp.einsum(form, cosine, imag_part, precision=lax.Precision.HIGHEST)  11.8 us
    dot_general x4, matrix products, complex_apply(): jnp.einsum(form, sine_part, imag_part, precision=lax.Precision.HIGHEST)  11.7 us
  transfers between devices with their start and end apart: 6, of which 4 were waited for; matrix products, arithmetic and copies ran while one was open for 26% of the time, Pallas kernels for 0%

commit v1 on v0

v1 whole, which is shorter than its diff:
```python
import functools

import jax
import jax.numpy as jnp
import numpy as np
from jax import lax
from jax.experimental import pallas as pl
from jax.experimental.pallas import tpu as pltpu
from jax.sharding import PartitionSpec as P

F32 = jnp.float32
BF16 = jnp.bfloat16
VMEM_LIMIT = 56 * 1024 * 1024


def params():
    return pltpu.CompilerParams(vmem_limit_bytes=VMEM_LIMIT)


def split(value):
    high = value.astype(BF16)
    return high, (value - high.astype(F32)).astype(BF16)


def dot(first, second, transposed=False):
    dims = (((1,), (1,)), ((), ())) if transposed else (((1,), (0,)), ((), ()))
    return lax.dot_general(first, second, dims, preferred_element_type=F32)


def dot3(first, second, transposed=False):
    rows = first[0].shape[0]
    both = dot(jnp.concatenate(first, axis=0), second[0], transposed)
    return both[:rows] + (both[rows:] + dot(first[0], second[1], transposed))


def complex_rows(pair):
    width = pair.shape[1] // 2
    turned = jnp.concatenate([-pair[:, width:], pair[:, :width]], axis=1)
    return jnp.concatenate([pair, turned], axis=0)


def load_matrix(ref, index):
    lead = (0,) * (len(ref.shape) - 4)
    return jnp.concatenate([ref[lead + (index, 0)], ref[lead + (index, 1)]], axis=1)


def load_rows(ref, index):
    groups, _, double, _ = ref.shape
    rows = double // 2
    parts = [jnp.concatenate([ref[r, index, p * rows : (p + 1) * rows, :] for r in range(groups)], axis=0) for p in (0, 1)]
    return jnp.concatenate(parts, axis=1)


def store_matrix(ref, index, value):
    width = value.shape[1] // 2
    lead = (0,) * (len(ref.shape) - 4)
    ref[lead + (index, 0)] = value[:, :width]
    ref[lead + (index, 1)] = value[:, width:]


def store_rows(ref, index, value):
    groups, _, double, width = ref.shape
    rows = double // 2
    for r in range(groups):
        for p in (0, 1):
            ref[r, index, p * rows : (p + 1) * rows, :] = value[r * rows : (r + 1) * rows, p * width : (p + 1) * width]


def sandwich(green, middle):
    green_pair = split(green)
    middle_pair = split(middle)
    first = dot3(green_pair, [complex_rows(part) for part in middle_pair])
    return dot3(split(first), [complex_rows(part) for part in green_pair], transposed=True)


def terms_kernel(count, load_base, load_middle, store, step, *refs):
    base = refs[0] if load_base is not None else None
    rest = refs[1:] if load_base is not None else refs
    greens, middles, out = rest[:count], rest[count : 2 * count], rest[-1]
    for index in range(step):
        total = load_base(base, index) if load_base is not None else None
        for green, middle in zip(greens, middles):
            term = sandwich(load_matrix(green, index), load_middle(middle, index))
            total = term if total is None else total + term
        store(out, index, total)


def matrix_spec(step, offset, width, lead):
    shape = (1,) * lead + (step, 2, width, width)
    return pl.BlockSpec(shape, lambda i: (0,) * lead + (i + offset, 0, 0, 0))


def rows_spec(step, groups, rows, width):
    return pl.BlockSpec((groups, step, 2 * rows, width), lambda i: (0, i, 0, 0))


def cost(energies, count, width):
    return pl.CostEstimate(
        flops=energies * count * 12 * 4 * width**3,
        bytes_accessed=energies * (2 * count + 2) * 8 * width * width,
        transcendentals=0,
    )


def own_terms(green, sigma, step):
    _, energies, _, width, _ = green.shape
    return pl.pallas_call(
        functools.partial(terms_kernel, 1, None, load_matrix, store_matrix, step),
        grid=(energies // step,),
        in_specs=[matrix_spec(step, 0, width, 1)] * 2,
        out_specs=matrix_spec(step, 0, width, 0),
        out_shape=jax.ShapeDtypeStruct((energies, 2, width, width), F32),
        compiler_params=params(),
        cost_estimate=cost(energies, 1, width),
        name="own_terms",
    )(green, sigma)


def side_terms(own, lower, upper, before, after, begin, size, groups, step):
    energies, _, width, _ = own.shape
    rows = width // groups
    at = begin // step
    return pl.pallas_call(
        functools.partial(terms_kernel, 2, load_matrix, load_matrix, store_rows, step),
        grid=(size // step,),
        in_specs=[matrix_spec(step, at, width, 0)] + [matrix_spec(step, at, width, 1)] * 2 + [matrix_spec(step, 0, width, 1)] * 2,
        out_specs=rows_spec(step, groups, rows, width),
        out_shape=jax.ShapeDtypeStruct((groups, size, 2 * rows, width), F32),
        compiler_params=params(),
        cost_estimate=cost(size, 2, width),
        name="side_terms",
    )(own, lower, upper, before, after)


def own_again(first, green, scattered, begin, step):
    groups, size, double, width = first.shape
    return pl.pallas_call(
        functools.partial(terms_kernel, 1, load_rows, load_rows, store_matrix, step),
        grid=(size // step,),
        in_specs=[
            rows_spec(step, groups, double // 2, width),
            matrix_spec(step, begin // step, width, 1),
            rows_spec(step, groups, double // 2, width),
        ],
        out_specs=matrix_spec(step, 0, width, 0),
        out_shape=jax.ShapeDtypeStruct((size, 2, width, width), F32),
        compiler_params=params(),
        cost_estimate=cost(size, 1, width),
        name="own_again",
    )(first, green, scattered)


def side_again_kernel(step, aliased, *refs):
    refs = refs[1:] if aliased else refs
    terms_kernel(2, load_matrix, load_rows, store_matrix, step, *refs)


def side_again(result, partial, lower, upper, before, after, begin, step):
    size, _, width, _ = partial.shape
    groups, _, double, _ = before.shape
    at = begin // step
    aliased = result is not None
    return pl.pallas_call(
        functools.partial(side_again_kernel, step, aliased),
        grid=(size // step,),
        in_specs=([pl.BlockSpec(memory_space=pl.ANY)] if aliased else [])
        + [matrix_spec(step, 0, width, 0)]
        + [matrix_spec(step, at, width, 1)] * 2
        + [rows_spec(step, groups, double // 2, width)] * 2,
        out_specs=matrix_spec(step, at, width, 1),
        out_shape=jax.ShapeDtypeStruct(lower.shape, F32),
        input_output_aliases={0: 0} if aliased else {},
        compiler_params=params(),
        cost_estimate=cost(size, 2, width),
        name="side_again",
    )(*([result] if aliased else []), partial, lower, upper, before, after)


def convolve_kernel(chunks, groups, rows, table_ref, mask_ref, weight_ref, *refs):
    count = len(chunks)
    inputs, outputs = refs[:count], refs[count:]
    total = table_ref.shape[1]
    width = weight_ref.shape[-1]
    stride = 2 * rows
    weight = weight_ref.reshape(total * stride, width)
    arrived = [ref.reshape(groups * size * stride, width) for ref, (_, size) in zip(inputs, chunks)]
    leaving = [ref.reshape(groups * size * stride, width) for ref, (_, size) in zip(outputs, chunks)]

    def apply(value):
        high, low = split(value)
        both = dot(table_ref[...], high)
        out = both[: 2 * total] + (both[2 * total :] + dot(table_ref[: 2 * total], low))
        return out[:total], out[total:]

    def one_row(row, carry):
        parts = []
        for p in (0, 1):
            pieces = [
                arrived[c][pl.ds(j * size * stride + p * rows + row, size, stride=stride), :]
                for j in range(groups)
                for c, (_, size) in enumerate(chunks)
            ]
            parts.append(jnp.concatenate(pieces, axis=0))
        cosine, sine = apply(jnp.concatenate(parts, axis=1))
        real = cosine[:, :width] + sine[:, width:]
        imag = cosine[:, width:] - sine[:, :width]
        weight_real = weight[pl.ds(row, total, stride=stride), :]
        weight_imag = weight[pl.ds(rows + row, total, stride=stride), :]
        cosine, sine = apply(
            jnp.concatenate([real * weight_real - imag * weight_imag, real * weight_imag + imag * weight_real], axis=1)
        )
        kept = mask_ref[pl.ds(row, 1), :] * (1.0 / total)
        results = (-(cosine[:, width:] + sine[:, :width]) * kept, (cosine[:, :width] - sine[:, width:]) * kept)
        for p in (0, 1):
            for j in range(groups):
                for c, (begin, size) in enumerate(chunks):
                    at = j * (total // groups) + begin
                    leaving[c][pl.ds(j * size * stride + p * rows + row, size, stride=stride), :] = results[p][at : at + size]
        return carry

    lax.fori_loop(0, rows, one_row, 0)


def convolve(arrived, weights, mask, chunks):
    groups, _, double, width = arrived[0].shape
    total = weights.shape[0]
    rows = double // 2
    phase = np.arange(total)[:, None] * np.arange(total)[None, :] % total
    angle = 2.0 * np.pi / total * phase
    table = np.concatenate([np.cos(angle), np.sin(angle)], axis=0).astype(np.float32)
    high = table.astype(jnp.bfloat16)
    low = (table - high.astype(np.float32)).astype(jnp.bfloat16)
    both = jnp.asarray(np.concatenate([high, low], axis=0))
    whole = pl.BlockSpec(memory_space=pltpu.VMEM)
    return pl.pallas_call(
        functools.partial(convolve_kernel, chunks, groups, rows),
        in_specs=[whole] * (3 + len(chunks)),
        out_specs=[whole] * len(chunks),
        out_shape=[jax.ShapeDtypeStruct(part.shape, F32) for part in arrived],
        compiler_params=params(),
        cost_estimate=pl.CostEstimate(
            flops=2 * 6 * 2 * total * total * 2 * rows * width, bytes_accessed=3 * total * double * width * 4, transcendentals=0
        ),
        name="convolve",
    )(both, mask, weights, *arrived)


def neighbours(value, count):
    up = [(i, i + 1) for i in range(count - 1)]
    down = [(i + 1, i) for i in range(count - 1)]
    return lax.ppermute(value, "slab", up), lax.ppermute(value, "slab", down)


def exchange(value):
    return lax.all_to_all(value, "energy", split_axis=0, concat_axis=0, tiled=True)


def local(green_diag, green_lower, green_upper, sigma_lesser, screened, pattern):
    groups = lax.axis_size("energy")
    slabs = lax.axis_size("slab")
    _, energies, _, width, _ = sigma_lesser.shape
    rows = width // groups
    total = screened.shape[1]
    step = 2
    parts = 4
    size = energies // parts
    chunks = [(at, size) for at in range(0, energies, size)]

    halos = [neighbours(sigma_lesser[:, at : at + size], slabs) for at, size in chunks]
    own = own_terms(green_diag, sigma_lesser, step)
    firsts = [
        side_terms(own, green_lower, green_upper, *halo, at, size, groups, step) for halo, (at, size) in zip(halos, chunks)
    ]
    arrived = [exchange(first) for first in firsts]

    kept = pattern[0].astype(F32)
    own_rows = lax.dynamic_slice_in_dim(kept, lax.axis_index("energy") * rows, rows)
    mask = own_rows[:, None] * kept[None, :]
    leaving = convolve(arrived, screened.reshape(total, 2 * rows, width), mask, chunks)

    scattered = [exchange(part) for part in leaving]
    halos = [neighbours(part, slabs) for part in scattered]
    partials = [own_again(first, green_diag, part, at, step) for first, part, (at, _) in zip(firsts, scattered, chunks)]
    result = None
    for partial, halo, (at, _) in zip(partials, halos, chunks):
        result = side_again(result, partial, green_lower, green_upper, *halo, at, step)
    return result


def solution(mesh):
    return jax.shard_map(
        local,
        mesh=mesh,
        in_specs=(
            P("slab", "energy", None, None, None),
            P("slab", "energy", None, None, None),
            P("slab", "energy", None, None, None),
            P("slab", "energy", None, None, None),
            P("slab", None, None, "energy", None),
            P("slab", None),
        ),
        out_specs=P("slab", "energy", None, None, None),
        check_vma=False,
    )
```

time: 510 us -> 308 us (0.60)
  the two profiles are of different devices: /device:TPU:18 before, /device:TPU:0 now
where the time goes in v1:
time: 308 us; the launch traced here: 305 us
  Pallas kernels  113 us (37%)
  waiting for transfers between devices  74.6 us (24%)
  starting transfers between devices  71.8 us (23%)
  blocking collectives  38.4 us (12%)
  local copies, waits for them, and re-layouts  6.63 us (2%)
    ppermute x16, waiting for transfers between devices, neighbours(): return (lax.ppermute(value, 'slab', up), lax.ppermute(value, 'slab', down))  50.2 us
    ppermute x16, starting transfers between devices, neighbours(): return (lax.ppermute(value, 'slab', up), lax.ppermute(value, 'slab', down))  49.7 us
    all_to_all x2, blocking collectives, exchange(): lax.all_to_all(value, 'energy', split_axis=0, concat_axis=0, tiled=True)  38.4 us
    pallas_call x1, Pallas kernels, convolve(): pl.pallas_call(functools.partial(convolve_kernel, chunks, groups, rows),...  27.9 us
    pallas_call x4, Pallas kernels, side_terms(): pl.pallas_call(functools.partial(terms_kernel, 2, load_matrix, load_matri...  25.5 us
    pallas_call x4, Pallas kernels, side_again(): pl.pallas_call(functools.partial(side_again_kernel, step, aliased), grid=...  25.4 us
    all_to_all x6, waiting for transfers between devices, exchange(): lax.all_to_all(value, 'energy', split_axis=0, concat_axis=0, tiled=True)  24.4 us
    all_to_all x6, starting transfers between devices, exchange(): lax.all_to_all(value, 'energy', split_axis=0, concat_axis=0, tiled=True)  22.1 us
  transfers between devices with their start and end apart: 22, of which 15 were waited for; matrix products, arithmetic and copies ran while one was open for 0% of the time, Pallas kernels for 26%

profile of v1, /device:TPU:0, one launch (start us, length us, event | category | flops | bytes accessed | tf_op | source)
XLA Modules:
  0.0 305.5 jit_solution(6837582281167575618)
XLA Ops:
  3.6 5.0 %collective-permute-start.4 = (f32[1,8,2,128,128]{4,3,2,1,0:T(8,128)S(1)}, f32[1,8,2,128,128]{4,3,2,1,0:T(8,128)S(1)}, u32[]{:S(2)}, u32[]{:S(2)}) collective-permute-start(f32[1,8,2,128,128]{4,3,2,1,0:T(8,128)S(1)} %get-tuple-element.16), channel_id=1, source_target_pairs={{0,1},{1,2},{2,3},{4,5},{5,6},{6,7},{8,9},{9,10},{10,11},{12,13},{... | collective-permute-start | bytes 3145736 | tf_op jit(solution)/shard_map/ppermute | solution.py:251
  9.8 5.6 %collective-permute-start.6 = (f32[1,8,2,128,128]{4,3,2,1,0:T(8,128)S(1)}, f32[1,8,2,128,128]{4,3,2,1,0:T(8,128)}, u32[]{:S(2)}, u32[]{:S(2)}) collective-permute-start(f32[1,8,2,128,128]{4,3,2,1,0:T(8,128)S(1)} %get-tuple-element.13), channel_id=1, source_target_pairs={{0,1},{1,2},{2,3},{4,5},{5,6},{6,7},{8,9},{9,10},{10,11},{12,13},{... | collective-permute-start | bytes 3145736 | tf_op jit(solution)/shard_map/ppermute | solution.py:251
  16.7 15.0 %own_terms.1.refs_0_ = f32[32,2,128,128]{3,2,1,0:T(8,128)} custom-call(f32[1,32,2,128,128]{4,3,2,1,0:T(8,128)} %refs_1_.19, f32[1,32,2,128,128]{4,3,2,1,0:T(8,128)} %refs_1_.10), custom_call_target="tpu_custom_call" | custom-call | flops 3221225472 | bytes 16777216 | tf_op jit(solution)/shard_map/own_terms/pallas_call | solution.py:107
  32.0 4.5 %collective-permute-done.5.refs_4_ = f32[1,8,2,128,128]{4,3,2,1,0:T(8,128)S(1)} collective-permute-done((f32[1,8,2,128,128]{4,3,2,1,0:T(8,128)S(1)}, f32[1,8,2,128,128]{4,3,2,1,0:T(8,128)S(1)}, u32[]{:S(2)}, u32[]{:S(2)}) %collective-permute-start.5) | collective-permute-done | bytes 1048608 | tf_op jit(solution)/shard_map/ppermute | solution.py:251
  37.5 6.4 %side_terms.6.refs_0_ = f32[8,8,32,128]{3,2,1,0:T(8,128)} custom-call(f32[32,2,128,128]{3,2,1,0:T(8,128)} %own_terms.1.refs_0_, f32[1,32,2,128,128]{4,3,2,1,0:T(8,128)} %refs_2_.15, f32[1,32,2,128,128]{4,3,2,1,0:T(8,128)} %refs_3_.5, f32[1,8,2,128,128]{4,3,2,1,0:T(8,128)} %copy-done.9, f32[1,8,2,128,128]{4,3,2,1,0:T(8,128)} %copy-done.10), custom_call_target="tpu_custom_call" | custom-call | flops 1610612736 | bytes 6291456 | tf_op jit(solution)/shard_map/side_terms/pallas_call | solution.py:123
  47.6 4.4 %collective-permute-start.2 = (f32[1,8,2,128,128]{4,3,2,1,0:T(8,128)}, f32[1,8,2,128,128]{4,3,2,1,0:T(8,128)}, u32[]{:S(2)}, u32[]{:S(2)}) collective-permute-start(f32[1,8,2,128,128]{4,3,2,1,0:T(8,128)} %get-tuple-element.14), channel_id=1, source_target_pairs={{0,1},{1,2},{2,3},{4,5},{5,6},{6,7},{8,9},{9,10},{10,11},{12,13},{... | collective-permute-start | bytes 3145736 | tf_op jit(solution)/shard_map/ppermute | solution.py:251
  58.1 6.3 %side_terms.7.refs_0_ = f32[8,8,32,128]{3,2,1,0:T(8,128)} custom-call(f32[32,2,128,128]{3,2,1,0:T(8,128)} %own_terms.1.refs_0_, f32[1,32,2,128,128]{4,3,2,1,0:T(8,128)} %refs_2_.15, f32[1,32,2,128,128]{4,3,2,1,0:T(8,128)} %refs_3_.5, f32[1,8,2,128,128]{4,3,2,1,0:T(8,128)} %collective-permute-done.6.refs_3_, f32[1,8,2,128,128]{4,3,2,1,0:T(8,128)} %collective-permute-done.7.refs_4_), custom_call_target="tpu_custom_call" | custom-call | flops 1610612736 | bytes 6291456 | tf_op jit(solution)/shard_map/side_terms/pallas_call | solution.py:123
  68.1 5.3 %collective-permute-start = (f32[1,8,2,128,128]{4,3,2,1,0:T(8,128)S(1)}, f32[1,8,2,128,128]{4,3,2,1,0:T(8,128)}, u32[]{:S(2)}, u32[]{:S(2)}) collective-permute-start(f32[1,8,2,128,128]{4,3,2,1,0:T(8,128)S(1)} %get-tuple-element.15), channel_id=1, source_target_pairs={{0,1},{1,2},{2,3},{4,5},{5,6},{6,7},{8,9},{9,10},{10,11},{12,13},{... | collective-permute-start | bytes 3145736 | tf_op jit(solution)/shard_map/ppermute | solution.py:251
  80.6 6.4 %side_terms.5.refs_0_ = f32[8,8,32,128]{3,2,1,0:T(8,128)} custom-call(f32[32,2,128,128]{3,2,1,0:T(8,128)} %own_terms.1.refs_0_, f32[1,32,2,128,128]{4,3,2,1,0:T(8,128)} %refs_2_.15, f32[1,32,2,128,128]{4,3,2,1,0:T(8,128)} %refs_3_.5, f32[1,8,2,128,128]{4,3,2,1,0:T(8,128)} %collective-permute-done.2.refs_3_, f32[1,8,2,128,128]{4,3,2,1,0:T(8,128)} %collective-permute-done.3.refs_4_), custom_call_target="tpu_custom_call" | custom-call | flops 1610612736 | bytes 6291456 | tf_op jit(solution)/shard_map/side_terms/pallas_call | solution.py:123
  90.9 7.4 %collective-permute-done.refs_3_ = f32[1,8,2,128,128]{4,3,2,1,0:T(8,128)} collective-permute-done((f32[1,8,2,128,128]{4,3,2,1,0:T(8,128)S(1)}, f32[1,8,2,128,128]{4,3,2,1,0:T(8,128)}, u32[]{:S(2)}, u32[]{:S(2)}) %collective-permute-start) | collective-permute-done | bytes 1048608 | tf_op jit(solution)/shard_map/ppermute | solution.py:251
  98.3 4.3 %collective-permute-done.1.refs_4_ = f32[1,8,2,128,128]{4,3,2,1,0:T(8,128)} collective-permute-done((f32[1,8,2,128,128]{4,3,2,1,0:T(8,128)S(1)}, f32[1,8,2,128,128]{4,3,2,1,0:T(8,128)}, u32[]{:S(2)}, u32[]{:S(2)}) %collective-permute-start.1) | collective-permute-done | bytes 1048608 | tf_op jit(solution)/shard_map/ppermute | solution.py:251
  102.6 6.4 %side_terms.4.refs_0_ = f32[8,8,32,128]{3,2,1,0:T(8,128)} custom-call(f32[32,2,128,128]{3,2,1,0:T(8,128)} %own_terms.1.refs_0_, f32[1,32,2,128,128]{4,3,2,1,0:T(8,128)} %refs_2_.15, f32[1,32,2,128,128]{4,3,2,1,0:T(8,128)} %refs_3_.5, f32[1,8,2,128,128]{4,3,2,1,0:T(8,128)} %collective-permute-done.refs_3_, f32[1,8,2,128,128]{4,3,2,1,0:T(8,128)} %collective-permute-done.1.refs_4_), custom_call_target="tpu_custom_call" | custom-call | flops 1610612736 | bytes 6291456 | tf_op jit(solution)/shard_map/side_terms/pallas_call | solution.py:123
  113.5 14.6 %all-to-all-done.refs_0_ = f32[8,8,32,128]{3,2,1,0:T(8,128)S(1)} async-done(((f32[8,8,32,128]{3,2,1,0:T(8,128)}), f32[8,8,32,128]{3,2,1,0:T(8,128)S(1)}, u32[]{:S(2)}, u32[]{:S(2)}) %all-to-all-start) | async-done | bytes 1048608 | tf_op jit(solution)/shard_map/all_to_all | solution.py:255
  129.1 27.9 %convolve.1 = (f32[8,8,32,128]{3,2,1,0:T(8,128)}, f32[8,8,32,128]{3,2,1,0:T(8,128)}, f32[8,8,32,128]{3,2,1,0:T(8,128)}, f32[8,8,32,128]{3,2,1,0:T(8,128)}) custom-call(bf16[1024,256]{1,0:T(8,128)(2,1)} %constant.15.clone.table_ref, f32[16,128]{1,0:T(8,128)} %broadcast_multiply_fusion.mask_ref, f32[256,32,128]{2,1,0:T(8,128)} %bitcast.5, ...), custom_call_target="tpu_custom_call" | custom-call | flops 6442450944 | bytes 12582912 | tf_op jit(solution)/shard_map/convolve/pallas_call | solution.py:235
  157.0 19.6 %all_to_all.40.refs_2_ = f32[8,8,32,128]{3,2,1,0:T(8,128)} all-to-all(f32[8,8,32,128]{3,2,1,0:T(8,128)} %get-tuple-element.9), channel_id=1, replica_groups=mesh['energy'=8,'slab'=4] {'energy'}, dimensions={0} | all-to-all | bytes 2097152 | tf_op jit(solution)/shard_map/all_to_all | solution.py:255
  176.6 18.8 %all_to_all.41.refs_2_ = f32[8,8,32,128]{3,2,1,0:T(8,128)S(1)} all-to-all(f32[8,8,32,128]{3,2,1,0:T(8,128)} %get-tuple-element.10), channel_id=1, replica_groups=mesh['energy'=8,'slab'=4] {'energy'}, dimensions={0} | all-to-all | bytes 2097152 | tf_op jit(solution)/shard_map/all_to_all | solution.py:255
  199.0 4.5 %collective-permute-start.8 = (f32[8,8,32,128]{3,2,1,0:T(8,128)}, f32[8,8,32,128]{3,2,1,0:T(8,128)}, u32[]{:S(2)}, u32[]{:S(2)}) collective-permute-start(f32[8,8,32,128]{3,2,1,0:T(8,128)} %all_to_all.40.refs_2_), channel_id=1, source_target_pairs={{0,1},{1,2},{2,3},{4,5},{5,6},{6,7},{8,9},{9,10},{10,11},{12,13},{... | collective-permute-start | bytes 3145736 | tf_op jit(solution)/shard_map/ppermute | solution.py:251
  204.8 5.6 %collective-permute-start.10 = (f32[8,8,32,128]{3,2,1,0:T(8,128)S(1)}, f32[8,8,32,128]{3,2,1,0:T(8,128)}, u32[]{:S(2)}, u32[]{:S(2)}) collective-permute-start(f32[8,8,32,128]{3,2,1,0:T(8,128)S(1)} %all_to_all.41.refs_2_), channel_id=1, source_target_pairs={{0,1},{1,2},{2,3},{4,5},{5,6},{6,7},{8,9},{9,10},{10,11},{12,13},{... | collective-permute-start | bytes 3145736 | tf_op jit(solution)/shard_map/ppermute | solution.py:251
  210.3 4.0 %all-to-all-done.6.refs_2_ = f32[8,8,32,128]{3,2,1,0:T(8,128)S(1)} async-done(((f32[8,8,32,128]{3,2,1,0:T(8,128)}), f32[8,8,32,128]{3,2,1,0:T(8,128)S(1)}, u32[]{:S(2)}, u32[]{:S(2)}) %all-to-all-start.6) | async-done | bytes 1048608 | tf_op jit(solution)/shard_map/all_to_all | solution.py:255
  219.2 5.7 %collective-permute-start.12 = (f32[8,8,32,128]{3,2,1,0:T(8,128)S(1)}, f32[8,8,32,128]{3,2,1,0:T(8,128)}, u32[]{:S(2)}, u32[]{:S(2)}) collective-permute-start(f32[8,8,32,128]{3,2,1,0:T(8,128)S(1)} %all-to-all-done.6.refs_2_), channel_id=1, source_target_pairs={{0,1},{1,2},{2,3},{4,5},{5,6},{6,7},{8,9},{9,10},{10,11},{12,13},{... | collective-permute-start | bytes 3145736 | tf_op jit(solution)/shard_map/ppermute | solution.py:251
  227.5 5.7 %all-to-all-done.7.refs_2_ = f32[8,8,32,128]{3,2,1,0:T(8,128)S(1)} async-done(((f32[8,8,32,128]{3,2,1,0:T(8,128)}), f32[8,8,32,128]{3,2,1,0:T(8,128)S(1)}, u32[]{:S(2)}, u32[]{:S(2)}) %all-to-all-start.7) | async-done | bytes 1048608 | tf_op jit(solution)/shard_map/all_to_all | solution.py:255
  236.7 11.9 %collective-permute-done.10.refs_4_ = f32[8,8,32,128]{3,2,1,0:T(8,128)} collective-permute-done((f32[8,8,32,128]{3,2,1,0:T(8,128)S(1)}, f32[8,8,32,128]{3,2,1,0:T(8,128)}, u32[]{:S(2)}, u32[]{:S(2)}) %collective-permute-start.10) | collective-permute-done | bytes 1048608 | tf_op jit(solution)/shard_map/ppermute | solution.py:251
  249.9 4.8 %own_again.4.refs_0_ = f32[8,2,128,128]{3,2,1,0:T(8,128)} custom-call(f32[8,8,32,128]{3,2,1,0:T(8,128)} %side_terms.4.refs_0_, f32[1,32,2,128,128]{4,3,2,1,0:T(8,128)} %refs_1_.19, f32[8,8,32,128]{3,2,1,0:T(8,128)} %all_to_all.40.refs_2_), custom_call_target="tpu_custom_call" | custom-call | flops 805306368 | bytes 4194304 | tf_op jit(solution)/shard_map/own_again/pallas_call | solution.py:137
  254.8 4.9 %own_again.5.refs_1_ = f32[8,2,128,128]{3,2,1,0:T(8,128)} custom-call(f32[8,8,32,128]{3,2,1,0:T(8,128)} %side_terms.5.refs_0_, f32[1,32,2,128,128]{4,3,2,1,0:T(8,128)} %refs_1_.19, f32[8,8,32,128]{3,2,1,0:T(8,128)} %copy-done.1), custom_call_target="tpu_custom_call" | custom-call | flops 805306368 | bytes 4194304 | tf_op jit(solution)/shard_map/own_again/pallas_call | solution.py:137
  259.6 4.8 %own_again.6.refs_1_ = f32[8,2,128,128]{3,2,1,0:T(8,128)} custom-call(f32[8,8,32,128]{3,2,1,0:T(8,128)} %side_terms.6.refs_0_, f32[1,32,2,128,128]{4,3,2,1,0:T(8,128)} %refs_1_.19, f32[8,8,32,128]{3,2,1,0:T(8,128)} %copy-done), custom_call_target="tpu_custom_call" | custom-call | flops 805306368 | bytes 4194304 | tf_op jit(solution)/shard_map/own_again/pallas_call | solution.py:137
  264.4 4.8 %own_again.7.refs_1_ = f32[8,2,128,128]{3,2,1,0:T(8,128)} custom-call(f32[8,8,32,128]{3,2,1,0:T(8,128)} %side_terms.7.refs_0_, f32[1,32,2,128,128]{4,3,2,1,0:T(8,128)} %refs_1_.19, f32[8,8,32,128]{3,2,1,0:T(8,128)} %copy-done.2), custom_call_target="tpu_custom_call" | custom-call | flops 805306368 | bytes 4194304 | tf_op jit(solution)/shard_map/own_again/pallas_call | solution.py:137
  269.3 6.3 %side_again.4.refs_0_ = f32[1,32,2,128,128]{4,3,2,1,0:T(8,128)} custom-call(f32[8,2,128,128]{3,2,1,0:T(8,128)} %own_again.4.refs_0_, f32[1,32,2,128,128]{4,3,2,1,0:T(8,128)} %refs_2_.15, f32[1,32,2,128,128]{4,3,2,1,0:T(8,128)} %refs_3_.5, f32[8,8,32,128]{3,2,1,0:T(8,128)} %collective-permute-done.8.refs_3_, f32[8,8,32,128]{3,2,1,0:T(8,128)} %collective-permute-done.9.refs_4_), custom_call_target="tpu_custom_call" | custom-call | flops 1610612736 | bytes 6291456 | tf_op jit(solution)/shard_map/side_again/pallas_call | solution.py:163
  275.6 6.4 %side_again.5.refs_0_ = f32[1,32,2,128,128]{4,3,2,1,0:T(8,128)} custom-call(f32[1,32,2,128,128]{4,3,2,1,0:T(8,128)} %side_again.4.refs_0_, f32[8,2,128,128]{3,2,1,0:T(8,128)} %own_again.5.refs_1_, f32[1,32,2,128,128]{4,3,2,1,0:T(8,128)} %refs_2_.15, f32[1,32,2,128,128]{4,3,2,1,0:T(8,128)} %refs_3_.5, ...), custom_call_target="tpu_custom_call", output_to_operand_aliasing={{}: (0, {})} | custom-call | flops 1610612736 | bytes 6291456 | tf_op jit(solution)/shard_map/side_again/pallas_call | solution.py:163
  282.0 6.4 %side_again.6.refs_0_ = f32[1,32,2,128,128]{4,3,2,1,0:T(8,128)} custom-call(f32[1,32,2,128,128]{4,3,2,1,0:T(8,128)} %side_again.5.refs_0_, f32[8,2,128,128]{3,2,1,0:T(8,128)} %own_again.6.refs_1_, f32[1,32,2,128,128]{4,3,2,1,0:T(8,128)} %refs_2_.15, f32[1,32,2,128,128]{4,3,2,1,0:T(8,128)} %refs_3_.5, ...), custom_call_target="tpu_custom_call", output_to_operand_aliasing={{}: (0, {})} | custom-call | flops 1610612736 | bytes 6291456 | tf_op jit(solution)/shard_map/side_again/pallas_call | solution.py:163
  288.4 4.6 %collective-permute-done.14.refs_4_ = f32[8,8,32,128]{3,2,1,0:T(8,128)S(1)} collective-permute-done((f32[8,8,32,128]{3,2,1,0:T(8,128)S(1)}, f32[8,8,32,128]{3,2,1,0:T(8,128)S(1)}, u32[]{:S(2)}, u32[]{:S(2)}) %collective-permute-start.14) | collective-permute-done | bytes 1048608 | tf_op jit(solution)/shard_map/ppermute | solution.py:251
  293.0 5.1 %collective-permute-done.15.refs_5_ = f32[8,8,32,128]{3,2,1,0:T(8,128)S(1)} collective-permute-done((f32[8,8,32,128]{3,2,1,0:T(8,128)S(1)}, f32[8,8,32,128]{3,2,1,0:T(8,128)S(1)}, u32[]{:S(2)}, u32[]{:S(2)}) %collective-permute-start.15) | collective-permute-done | bytes 1048608 | tf_op jit(solution)/shard_map/ppermute | solution.py:251
  299.1 6.4 %side_again.7 = f32[1,32,2,128,128]{4,3,2,1,0:T(8,128)} custom-call(f32[1,32,2,128,128]{4,3,2,1,0:T(8,128)} %side_again.6.refs_0_, f32[8,2,128,128]{3,2,1,0:T(8,128)} %own_again.7.refs_1_, f32[1,32,2,128,128]{4,3,2,1,0:T(8,128)} %refs_2_.15, f32[1,32,2,128,128]{4,3,2,1,0:T(8,128)} %refs_3_.5, ...), custom_call_target="tpu_custom_call", output_to_operand_aliasing={{}: (0, {})} | custom-call | flops 1610612736 | bytes 6291456 | tf_op jit(solution)/shard_map/side_again/pallas_call | solution.py:163
  (56 shorter events, 55.5 us)
Async XLA Ops:
  3.6 28.5 %collective-permute-start.4 = (f32[1,8,2,128,128]{4,3,2,1,0:T(8,128)S(1)}, f32[1,8,2,128,128]{4,3,2,1,0:T(8,128)S(1)}, u32[]{:S(2)}, u32[]{:S(2)}) collective-permute-start(f32[1,8,2,128,128]{4,3,2,1,0:T(8,128)S(1)} %get-tuple-element.16), channel_id=1, source_target_pairs={{0,1},{1,2},{2,3},{4,5},{5,6},{6,7},{8,9},{9,10},{10,11},{12,13},{... | collective-permute-start | bytes 3145736 | tf_op jit(solution)/shard_map/ppermute | solution.py:251
  8.5 28.0 %collective-permute-start.5 = (f32[1,8,2,128,128]{4,3,2,1,0:T(8,128)S(1)}, f32[1,8,2,128,128]{4,3,2,1,0:T(8,128)S(1)}, u32[]{:S(2)}, u32[]{:S(2)}) collective-permute-start(f32[1,8,2,128,128]{4,3,2,1,0:T(8,128)S(1)} %get-tuple-element.16), channel_id=1, source_target_pairs={{1,0},{2,1},{3,2},{5,4},{6,5},{7,6},{9,8},{10,9},{11,10},{13,12},{... | collective-permute-start | bytes 3145736 | tf_op jit(solution)/shard_map/ppermute | solution.py:251
  9.8 44.7 %collective-permute-start.6 = (f32[1,8,2,128,128]{4,3,2,1,0:T(8,128)S(1)}, f32[1,8,2,128,128]{4,3,2,1,0:T(8,128)}, u32[]{:S(2)}, u32[]{:S(2)}) collective-permute-start(f32[1,8,2,128,128]{4,3,2,1,0:T(8,128)S(1)} %get-tuple-element.13), channel_id=1, source_target_pairs={{0,1},{1,2},{2,3},{4,5},{5,6},{6,7},{8,9},{9,10},{10,11},{12,13},{... | collective-permute-start | bytes 3145736 | tf_op jit(solution)/shard_map/ppermute | solution.py:251
  15.4 42.7 %collective-permute-start.7 = (f32[1,8,2,128,128]{4,3,2,1,0:T(8,128)S(1)}, f32[1,8,2,128,128]{4,3,2,1,0:T(8,128)}, u32[]{:S(2)}, u32[]{:S(2)}) collective-permute-start(f32[1,8,2,128,128]{4,3,2,1,0:T(8,128)S(1)} %get-tuple-element.13), channel_id=1, source_target_pairs={{1,0},{2,1},{3,2},{5,4},{6,5},{7,6},{9,8},{10,9},{11,10},{13,12},{... | collective-permute-start | bytes 3145736 | tf_op jit(solution)/shard_map/ppermute | solution.py:251
  32.0 4.5 %copy-start.9 = (f32[1,8,2,128,128]{4,3,2,1,0:T(8,128)}, f32[1,8,2,128,128]{4,3,2,1,0:T(8,128)S(1)}, u32[]{:S(2)}) copy-start(f32[1,8,2,128,128]{4,3,2,1,0:T(8,128)S(1)} %collective-permute-done.4.refs_3_) | copy-start | bytes 3145732
  43.9 20.6 %all-to-all-start.2 = ((f32[8,8,32,128]{3,2,1,0:T(8,128)}), f32[8,8,32,128]{3,2,1,0:T(8,128)S(1)}, u32[]{:S(2)}, u32[]{:S(2)}) async-start(f32[8,8,32,128]{3,2,1,0:T(8,128)} %side_terms.6.refs_0_), calls=%async_computation.2 | async-start | bytes 2097152 | tf_op jit(solution)/shard_map/all_to_all | solution.py:255
  47.6 29.4 %collective-permute-start.2 = (f32[1,8,2,128,128]{4,3,2,1,0:T(8,128)}, f32[1,8,2,128,128]{4,3,2,1,0:T(8,128)}, u32[]{:S(2)}, u32[]{:S(2)}) collective-permute-start(f32[1,8,2,128,128]{4,3,2,1,0:T(8,128)} %get-tuple-element.14), channel_id=1, source_target_pairs={{0,1},{1,2},{2,3},{4,5},{5,6},{6,7},{8,9},{9,10},{10,11},{12,13},{... | collective-permute-start | bytes 3145736 | tf_op jit(solution)/shard_map/ppermute | solution.py:251
  52.0 28.6 %collective-permute-start.3 = (f32[1,8,2,128,128]{4,3,2,1,0:T(8,128)}, f32[1,8,2,128,128]{4,3,2,1,0:T(8,128)}, u32[]{:S(2)}, u32[]{:S(2)}) collective-permute-start(f32[1,8,2,128,128]{4,3,2,1,0:T(8,128)} %get-tuple-element.14), channel_id=1, source_target_pairs={{1,0},{2,1},{3,2},{5,4},{6,5},{7,6},{9,8},{10,9},{11,10},{13,12},{... | collective-permute-start | bytes 3145736 | tf_op jit(solution)/shard_map/ppermute | solution.py:251
  64.5 22.5 %copy-start.5 = (f32[8,8,32,128]{3,2,1,0:T(8,128)}, f32[8,8,32,128]{3,2,1,0:T(8,128)S(1)}, u32[]{:S(2)}) copy-start(f32[8,8,32,128]{3,2,1,0:T(8,128)S(1)} %all-to-all-done.2.refs_2_) | copy-start | bytes 3145732
  64.5 22.5 %all-to-all-start.3 = ((f32[8,8,32,128]{3,2,1,0:T(8,128)}), f32[8,8,32,128]{3,2,1,0:T(8,128)S(1)}, u32[]{:S(2)}, u32[]{:S(2)}) async-start(f32[8,8,32,128]{3,2,1,0:T(8,128)} %side_terms.7.refs_0_), calls=%async_computation.3 | async-start | bytes 2097152 | tf_op jit(solution)/shard_map/all_to_all | solution.py:255
  68.1 30.2 %collective-permute-start = (f32[1,8,2,128,128]{4,3,2,1,0:T(8,128)S(1)}, f32[1,8,2,128,128]{4,3,2,1,0:T(8,128)}, u32[]{:S(2)}, u32[]{:S(2)}) collective-permute-start(f32[1,8,2,128,128]{4,3,2,1,0:T(8,128)S(1)} %get-tuple-element.15), channel_id=1, source_target_pairs={{0,1},{1,2},{2,3},{4,5},{5,6},{6,7},{8,9},{9,10},{10,11},{12,13},{... | collective-permute-start | bytes 3145736 | tf_op jit(solution)/shard_map/ppermute | solution.py:251
  73.4 29.1 %collective-permute-start.1 = (f32[1,8,2,128,128]{4,3,2,1,0:T(8,128)S(1)}, f32[1,8,2,128,128]{4,3,2,1,0:T(8,128)}, u32[]{:S(2)}, u32[]{:S(2)}) collective-permute-start(f32[1,8,2,128,128]{4,3,2,1,0:T(8,128)S(1)} %get-tuple-element.15), channel_id=1, source_target_pairs={{1,0},{2,1},{3,2},{5,4},{6,5},{7,6},{9,8},{10,9},{11,10},{13,12},{... | collective-permute-start | bytes 3145736 | tf_op jit(solution)/shard_map/ppermute | solution.py:251
  87.0 21.9 %copy-start.6 = (f32[8,8,32,128]{3,2,1,0:T(8,128)}, f32[8,8,32,128]{3,2,1,0:T(8,128)S(1)}, u32[]{:S(2)}) copy-start(f32[8,8,32,128]{3,2,1,0:T(8,128)S(1)} %all-to-all-done.3.refs_3_) | copy-start | bytes 3145732
  87.0 21.9 %all-to-all-start.1 = ((f32[8,8,32,128]{3,2,1,0:T(8,128)}), f32[8,8,32,128]{3,2,1,0:T(8,128)S(1)}, u32[]{:S(2)}, u32[]{:S(2)}) async-start(f32[8,8,32,128]{3,2,1,0:T(8,128)} %side_terms.5.refs_0_), calls=%async_computation.1 | async-start | bytes 2097152 | tf_op jit(solution)/shard_map/all_to_all | solution.py:255
  90.9 21.8 %copy-start.11 = (s32[1,128]{1,0:T(1,128)S(1)}, s32[1,128]{1,0:T(1,128)}, u32[]{:S(2)}) copy-start(s32[1,128]{1,0:T(1,128)} %param.12) | copy-start | bytes 1540
  109.0 19.2 %copy-start.7 = (f32[8,8,32,128]{3,2,1,0:T(8,128)}, f32[8,8,32,128]{3,2,1,0:T(8,128)S(1)}, u32[]{:S(2)}) copy-start(f32[8,8,32,128]{3,2,1,0:T(8,128)S(1)} %all-to-all-done.1.refs_1_) | copy-start | bytes 3145732
  109.0 19.1 %all-to-all-start = ((f32[8,8,32,128]{3,2,1,0:T(8,128)}), f32[8,8,32,128]{3,2,1,0:T(8,128)S(1)}, u32[]{:S(2)}, u32[]{:S(2)}) async-start(f32[8,8,32,128]{3,2,1,0:T(8,128)} %side_terms.4.refs_0_), calls=%async_computation | async-start | bytes 2097152 | tf_op jit(solution)/shard_map/all_to_all | solution.py:255
  195.4 59.3 %copy-start.1 = (f32[8,8,32,128]{3,2,1,0:T(8,128)}, f32[8,8,32,128]{3,2,1,0:T(8,128)S(1)}, u32[]{:S(2)}) copy-start(f32[8,8,32,128]{3,2,1,0:T(8,128)S(1)} %all_to_all.41.refs_2_) | copy-start | bytes 3145732
  195.4 18.9 %all-to-all-start.6 = ((f32[8,8,32,128]{3,2,1,0:T(8,128)}), f32[8,8,32,128]{3,2,1,0:T(8,128)S(1)}, u32[]{:S(2)}, u32[]{:S(2)}) async-start(f32[8,8,32,128]{3,2,1,0:T(8,128)} %get-tuple-element.11), calls=%async_computation.6 | async-start | bytes 2097152 | tf_op jit(solution)/shard_map/all_to_all | solution.py:255
  199.0 27.2 %collective-permute-start.8 = (f32[8,8,32,128]{3,2,1,0:T(8,128)}, f32[8,8,32,128]{3,2,1,0:T(8,128)}, u32[]{:S(2)}, u32[]{:S(2)}) collective-permute-start(f32[8,8,32,128]{3,2,1,0:T(8,128)} %all_to_all.40.refs_2_), channel_id=1, source_target_pairs={{0,1},{1,2},{2,3},{4,5},{5,6},{6,7},{8,9},{9,10},{10,11},{12,13},{... | collective-permute-start | bytes 3145736 | tf_op jit(solution)/shard_map/ppermute | solution.py:251
  203.5 29.8 %collective-permute-start.9 = (f32[8,8,32,128]{3,2,1,0:T(8,128)}, f32[8,8,32,128]{3,2,1,0:T(8,128)}, u32[]{:S(2)}, u32[]{:S(2)}) collective-permute-start(f32[8,8,32,128]{3,2,1,0:T(8,128)} %all_to_all.40.refs_2_), channel_id=1, source_target_pairs={{1,0},{2,1},{3,2},{5,4},{6,5},{7,6},{9,8},{10,9},{11,10},{13,12},{... | collective-permute-start | bytes 3145736 | tf_op jit(solution)/shard_map/ppermute | solution.py:251
  204.8 43.9 %collective-permute-start.10 = (f32[8,8,32,128]{3,2,1,0:T(8,128)S(1)}, f32[8,8,32,128]{3,2,1,0:T(8,128)}, u32[]{:S(2)}, u32[]{:S(2)}) collective-permute-start(f32[8,8,32,128]{3,2,1,0:T(8,128)S(1)} %all_to_all.41.refs_2_), channel_id=1, source_target_pairs={{0,1},{1,2},{2,3},{4,5},{5,6},{6,7},{8,9},{9,10},{10,11},{12,13},{... | collective-permute-start | bytes 3145736 | tf_op jit(solution)/shard_map/ppermute | solution.py:251
  214.3 40.4 %copy-start = (f32[8,8,32,128]{3,2,1,0:T(8,128)}, f32[8,8,32,128]{3,2,1,0:T(8,128)S(1)}, u32[]{:S(2)}) copy-start(f32[8,8,32,128]{3,2,1,0:T(8,128)S(1)} %all-to-all-done.6.refs_2_) | copy-start | bytes 3145732
  214.4 18.9 %all-to-all-start.7 = ((f32[8,8,32,128]{3,2,1,0:T(8,128)}), f32[8,8,32,128]{3,2,1,0:T(8,128)S(1)}, u32[]{:S(2)}, u32[]{:S(2)}) async-start(f32[8,8,32,128]{3,2,1,0:T(8,128)} %get-tuple-element.12), calls=%async_computation.7 | async-start | bytes 2097152 | tf_op jit(solution)/shard_map/all_to_all | solution.py:255
  217.9 57.7 %collective-permute-start.11 = (f32[8,8,32,128]{3,2,1,0:T(8,128)S(1)}, f32[8,8,32,128]{3,2,1,0:T(8,128)}, u32[]{:S(2)}, u32[]{:S(2)}) collective-permute-start(f32[8,8,32,128]{3,2,1,0:T(8,128)S(1)} %all_to_all.41.refs_2_), channel_id=1, source_target_pairs={{1,0},{2,1},{3,2},{5,4},{6,5},{7,6},{9,8},{10,9},{11,10},{13,12},{... | collective-permute-start | bytes 3145736 | tf_op jit(solution)/shard_map/ppermute | solution.py:251
  219.2 62.8 %collective-permute-start.12 = (f32[8,8,32,128]{3,2,1,0:T(8,128)S(1)}, f32[8,8,32,128]{3,2,1,0:T(8,128)}, u32[]{:S(2)}, u32[]{:S(2)}) collective-permute-start(f32[8,8,32,128]{3,2,1,0:T(8,128)S(1)} %all-to-all-done.6.refs_2_), channel_id=1, source_target_pairs={{0,1},{1,2},{2,3},{4,5},{5,6},{6,7},{8,9},{9,10},{10,11},{12,13},{... | collective-permute-start | bytes 3145736 | tf_op jit(solution)/shard_map/ppermute | solution.py:251
  226.3 55.7 %collective-permute-start.13 = (f32[8,8,32,128]{3,2,1,0:T(8,128)S(1)}, f32[8,8,32,128]{3,2,1,0:T(8,128)}, u32[]{:S(2)}, u32[]{:S(2)}) collective-permute-start(f32[8,8,32,128]{3,2,1,0:T(8,128)S(1)} %all-to-all-done.6.refs_2_), channel_id=1, source_target_pairs={{1,0},{2,1},{3,2},{5,4},{6,5},{7,6},{9,8},{10,9},{11,10},{13,12},{... | collective-permute-start | bytes 3145736 | tf_op jit(solution)/shard_map/ppermute | solution.py:251
  233.3 26.4 %copy-start.2 = (f32[8,8,32,128]{3,2,1,0:T(8,128)}, f32[8,8,32,128]{3,2,1,0:T(8,128)S(1)}, u32[]{:S(2)}) copy-start(f32[8,8,32,128]{3,2,1,0:T(8,128)S(1)} %all-to-all-done.7.refs_2_) | copy-start | bytes 3145732
  233.3 59.8 %collective-permute-start.14 = (f32[8,8,32,128]{3,2,1,0:T(8,128)S(1)}, f32[8,8,32,128]{3,2,1,0:T(8,128)S(1)}, u32[]{:S(2)}, u32[]{:S(2)}) collective-permute-start(f32[8,8,32,128]{3,2,1,0:T(8,128)S(1)} %all-to-all-done.7.refs_2_), channel_id=1, source_target_pairs={{0,1},{1,2},{2,3},{4,5},{5,6},{6,7},{8,9},{9,10},{10,11},{12,13},{... | collective-permute-start | bytes 3145736 | tf_op jit(solution)/shard_map/ppermute | solution.py:251
  248.6 49.5 %collective-permute-start.15 = (f32[8,8,32,128]{3,2,1,0:T(8,128)S(1)}, f32[8,8,32,128]{3,2,1,0:T(8,128)S(1)}, u32[]{:S(2)}, u32[]{:S(2)}) collective-permute-start(f32[8,8,32,128]{3,2,1,0:T(8,128)S(1)} %all-to-all-done.7.refs_2_), channel_id=1, source_target_pairs={{1,0},{2,1},{3,2},{5,4},{6,5},{7,6},{9,8},{10,9},{11,10},{13,12},{... | collective-permute-start | bytes 3145736 | tf_op jit(solution)/shard_map/ppermute | solution.py:251
  293.0 5.1 %copy-start.3 = (f32[8,8,32,128]{3,2,1,0:T(8,128)}, f32[8,8,32,128]{3,2,1,0:T(8,128)S(1)}, u32[]{:S(2)}) copy-start(f32[8,8,32,128]{3,2,1,0:T(8,128)S(1)} %collective-permute-done.14.refs_4_) | copy-start | bytes 3145732
  298.1 1.0 copy-start.4
  (2 other events, 2.0 us)

commit v2 on v1

v2 whole, which is shorter than its diff:
```python
import functools

import jax
import jax.numpy as jnp
import numpy as np
from jax import lax
from jax.experimental import pallas as pl
from jax.experimental.pallas import tpu as pltpu
from jax.sharding import PartitionSpec as P

F32 = jnp.float32
BF16 = jnp.bfloat16
MIB = 1024 * 1024


def params(mebibytes=16):
    return pltpu.CompilerParams(vmem_limit_bytes=mebibytes * MIB)


def split(value):
    high = value.astype(BF16)
    return high, (value - high.astype(F32)).astype(BF16)


def dot(first, second, transposed=False):
    dims = (((1,), (1,)), ((), ())) if transposed else (((1,), (0,)), ((), ()))
    return lax.dot_general(first, second, dims, preferred_element_type=F32)


def stack(*parts):
    return jnp.concatenate(parts, axis=0)


def beside(*parts):
    return jnp.concatenate(parts, axis=1)


def dot_stacked(first, second):
    rows = first.shape[0] // 2
    both = dot(first, second[0])
    return both[:rows] + (both[rows:] + dot(first[:rows], second[1]))


def sandwich(green, middle, turn):
    rows = green.shape[0] // 2
    first = dot_stacked(green, middle)
    out = dot(stack(*split(first), *split(turn(first))), green, transposed=True)
    real, real_low, imag, imag_low = (out[i * rows : (i + 1) * rows] for i in range(4))
    return beside(real[:, :rows] + (real[:, rows:] + real_low[:, :rows]), imag[:, :rows] + (imag[:, rows:] + imag_low[:, :rows]))


def turn_halves(value):
    width = value.shape[1] // 2
    return beside(value[:, width:], -value[:, :width])


def lane_of(value):
    return lax.broadcasted_iota(jnp.int32, value.shape, 1)


def turn_packed(value, extra):
    width = value.shape[1] // 2
    wide, narrow = value[:, :width], value[:, width:]
    lane = lane_of(wide)
    sign = jnp.where(lane < width // 2, 1.0, -1.0)
    wide = pltpu.roll(wide, width // 2, axis=1) * sign
    narrow = jnp.where(lane % (2 * extra) < extra, pltpu.roll(narrow, width - extra, axis=1), -pltpu.roll(narrow, extra, axis=1))
    return beside(wide, narrow)


def load_matrix(ref, index):
    lead = (0,) * (len(ref.shape) - 4)
    return beside(ref[lead + (index, 0)], ref[lead + (index, 1)])


def load_flat(ref, index):
    width = ref.shape[1]
    at = 2 * index * width
    return beside(ref[at : at + width, :], ref[at + width : at + 2 * width, :])


def load_rows(ref, index):
    groups, _, double, _ = ref.shape
    rows = double // 2
    return beside(*[stack(*[ref[r, index, p * rows : (p + 1) * rows, :] for r in range(groups)]) for p in (0, 1)])


def store_matrix(ref, index, value):
    width = value.shape[1] // 2
    lead = (0,) * (len(ref.shape) - 4)
    ref[lead + (index, 0)] = value[:, :width]
    ref[lead + (index, 1)] = value[:, width:]


def store_rows(ref, index, value):
    groups, _, double, width = ref.shape
    rows = double // 2
    for r in range(groups):
        for p in (0, 1):
            ref[r, index, p * rows : (p + 1) * rows, :] = value[r * rows : (r + 1) * rows, p * width : (p + 1) * width]


def whole_term(green, middle):
    pairs = [stack(part, beside(-part[:, part.shape[1] // 2 :], part[:, : part.shape[1] // 2])) for part in split(middle)]
    return sandwich(stack(*split(green)), pairs, turn_halves)


def packed_term(green, middle_ref, index, size, extra):
    width = green.shape[1] // 2
    share = width // (2 * extra)
    middle = beside(middle_ref[index], middle_ref[size + index // share])
    pairs = []
    for part, turned in zip(split(middle), split(-turn_packed(middle, extra))):
        half = width // 2
        pairs.append(stack(part[:half], turned[:half], *([part[half:], turned[half:]] * share)))
    return sandwich(green, pairs, functools.partial(turn_packed, extra=extra))


def matrix_spec(step, offset, width, lead):
    shape = (1,) * lead + (step, 2, width, width)
    return pl.BlockSpec(shape, lambda i: (0,) * lead + (i + offset, 0, 0, 0))


def flat_spec(step, width):
    return pl.BlockSpec((2 * step * width, width), lambda i: (i, 0))


def rows_spec(step, groups, rows, width):
    return pl.BlockSpec((groups, step, 2 * rows, width), lambda i: (0, i, 0, 0))


def in_any():
    return pl.BlockSpec(memory_space=pl.ANY)


def cost(energies, count, width):
    return pl.CostEstimate(
        flops=energies * count * width**2,
        bytes_accessed=energies * count * width,
        transcendentals=0,
    )


def own_terms_kernel(step, green, sigma, out):
    for index in range(step):
        store_matrix(out, index, whole_term(load_matrix(green, index), load_matrix(sigma, index)))


def own_terms(green, sigma, step):
    _, energies, _, width, _ = green.shape
    return pl.pallas_call(
        functools.partial(own_terms_kernel, step),
        grid=(energies // step,),
        in_specs=[matrix_spec(step, 0, width, 1)] * 2,
        out_specs=matrix_spec(step, 0, width, 0),
        out_shape=jax.ShapeDtypeStruct((energies, 2, width, width), F32),
        compiler_params=params(60),
        cost_estimate=cost(energies, 1, width),
        name="own_terms",
    )(green, sigma)


def side_terms_kernel(step, total, lower, upper, before, after, out, send):
    for index in range(step):
        value = load_matrix(total, index)
        value = value + whole_term(load_matrix(lower, index), load_flat(before, index))
        value = value + whole_term(load_matrix(upper, index), load_flat(after, index))
        store_matrix(out, index, value)
        store_rows(send, index, value)


def side_terms(total, lower, upper, before, after, begin, size, groups, step):
    width = total.shape[-1]
    rows = width // groups
    at = begin // step
    return pl.pallas_call(
        functools.partial(side_terms_kernel, step),
        grid=(size // step,),
        in_specs=[matrix_spec(step, at, width, 0)] + [matrix_spec(step, at, width, 1)] * 2 + [flat_spec(step, width)] * 2,
        out_specs=[matrix_spec(step, 0, width, 0), rows_spec(step, groups, rows, width)],
        out_shape=[
            jax.ShapeDtypeStruct((size, 2, width, width), F32),
            jax.ShapeDtypeStruct((groups, size, 2 * rows, width), F32),
        ],
        compiler_params=params(60),
        cost_estimate=cost(size, 2, width),
        name="side_terms",
    )(total, lower, upper, before, after)


def whole_again_kernel(step, count, aliased, *refs):
    refs = refs[1:] if aliased else refs
    base, greens, middles, out = refs[0], refs[1 : 1 + count], refs[1 + count : 1 + 2 * count], refs[-1]
    for index in range(step):
        value = load_matrix(base, index)
        for green, middle in zip(greens, middles):
            value = value + whole_term(load_matrix(green, index), load_rows(middle, index))
        store_matrix(out, index, value)


def whole_again(result, base, base_begin, greens, middles, begin, step, shape):
    groups, size, double, width = middles[0].shape
    count = len(greens)
    at = begin // step
    aliased = result is not None
    return pl.pallas_call(
        functools.partial(whole_again_kernel, step, count, aliased),
        grid=(size // step,),
        in_specs=[in_any()] * aliased
        + [matrix_spec(step, base_begin // step, width, 0)]
        + [matrix_spec(step, at, width, 1)] * count
        + [rows_spec(step, groups, double // 2, width)] * count,
        out_specs=matrix_spec(step, at if len(shape) == 5 else 0, width, len(shape) - 4),
        out_shape=jax.ShapeDtypeStruct(shape, F32),
        input_output_aliases={0: 0} if aliased else {},
        compiler_params=params(),
        cost_estimate=cost(size, count, width),
        name="whole_again",
    )(*([result] * aliased), base, *greens, *middles)


def packed_again_kernel(step, bases, count, size, extra, aliased, *refs):
    refs = refs[1:] if aliased else refs
    base_refs, refs = refs[: len(bases)], refs[len(bases) :]
    greens, middles, out = refs[:count], refs[count : 2 * count], refs[-1]
    here = pl.program_id(0)
    for index in range(step):
        value = load_matrix(base_refs[0], index)
        for (begin, _), ref in zip(bases[1:], base_refs[1:]):
            value = jnp.where(here >= begin, load_matrix(ref, index), value)
        for green, middle in zip(greens, middles):
            value = value + packed_term(green[index], middle, here * step + index, size, extra)
        store_matrix(out, index, value)


def packed_again(result, bases, greens, middles, begin, size, step, shape, extra):
    span, cap, width = middles[0].shape
    count = len(greens)
    at = begin // step
    aliased = result is not None
    places = chunks_of([base.shape[0] // step for base in bases])
    specs = [
        pl.BlockSpec((step, 2, width, width), lambda i, start=start, steps=steps: (jnp.clip(i - start, 0, steps - 1), 0, 0, 0))
        for start, steps in places
    ]
    return pl.pallas_call(
        functools.partial(packed_again_kernel, step, places, count, size, extra, aliased),
        grid=(size // step,),
        in_specs=[in_any()] * aliased
        + specs
        + [pl.BlockSpec((step, 2 * width, 2 * width), lambda i: (i + at, 0, 0))] * count
        + [pl.BlockSpec((span, cap, width), lambda i: (0, 0, 0))] * count,
        out_specs=matrix_spec(step, at if len(shape) == 5 else 0, width, len(shape) - 4),
        out_shape=jax.ShapeDtypeStruct(shape, F32),
        input_output_aliases={0: 0} if aliased else {},
        compiler_params=params(),
        cost_estimate=cost(size, count, width),
        name="packed_again",
    )(*([result] * aliased), *bases, *greens, *middles)


def pack_green_kernel(step, extra, place, *refs):
    count = len(refs) // 2
    width = place.shape[1] // 2
    share = width // (2 * extra)
    for green, out, which in zip(refs[:count], refs[count:], range(count)):
        for index in range(step):
            both = dot(stack(*split(load_matrix(green, index))), place[which])
            lane = lane_of(both) - width
            other = (lane >= 0) & (lane // (2 * extra) != index % share)
            out[index] = jnp.where(other, 0.0, both).astype(BF16)


def pack_green(greens, places, step, extra):
    _, energies, _, width, _ = greens[0].shape
    count = len(greens)
    return pl.pallas_call(
        functools.partial(pack_green_kernel, step, extra),
        grid=(energies // step,),
        in_specs=[pl.BlockSpec(places.shape, lambda i: (0, 0, 0))] + [matrix_spec(step, 0, width, 1)] * count,
        out_specs=[pl.BlockSpec((step, 2 * width, 2 * width), lambda i: (i, 0, 0))] * count,
        out_shape=[jax.ShapeDtypeStruct((energies, 2 * width, 2 * width), BF16)] * count,
        compiler_params=params(60),
        cost_estimate=pl.CostEstimate(
            flops=count * energies * 16 * width**3, bytes_accessed=count * energies * 16 * width**2, transcendentals=0
        ),
        name="pack_green",
    )(places, *greens)


def pack_rows_kernel(rows, chosen, part, out):
    groups, _, _ = part.shape
    for at in range(out.shape[0]):
        block = stack(*[part[r, at * rows : (at + 1) * rows, :] for r in range(groups)])
        high, low = split(block)
        out[at] = dot(chosen[...], high) + dot(chosen[...], low)


def pack_rows(chosen, part, rows):
    groups, height, width = part.shape
    cap = chosen.shape[0]
    whole = pl.BlockSpec(memory_space=pltpu.VMEM)
    return pl.pallas_call(
        functools.partial(pack_rows_kernel, rows),
        in_specs=[whole, whole],
        out_specs=whole,
        out_shape=jax.ShapeDtypeStruct((height // rows, cap, width), F32),
        compiler_params=params(),
        cost_estimate=pl.CostEstimate(
            flops=height // rows * 4 * cap * width**2, bytes_accessed=2 * groups * height * width * 4, transcendentals=0
        ),
        name="pack_rows",
    )(chosen, part)


def apply_table(table, value, size):
    both = dot(table, value[0])
    return both[:size] + (both[size:] + dot(table[:size], value[1]))


def forward_kernel(first, groups, rows, tables, weight_ref, *refs):
    inputs, out = refs[: len(first)], refs[-1]
    total, double, width = weight_ref.shape
    half = total // 2
    weight = weight_ref.reshape(total * double, width)
    arrived = [ref.reshape(groups * size * double, width) for ref, (_, size) in zip(inputs, first)]

    def load(row, p):
        pieces = [
            arrived[c][pl.ds(j * size * double + p * rows + row, size, stride=double), :]
            for j in range(groups)
            for c, (_, size) in enumerate(first)
        ]
        return stack(*pieces)

    def two_rows(pair, carry):
        at = (2 * pair, 2 * pair + 1)
        values = [[load(row, p) for row in at] for p in (0, 1)]
        for odd in (0, 1):
            sign = 1.0 - 2.0 * odd
            folded = [beside(*[value[:half] + sign * value[half:] for value in part]) for part in values]
            spectrum = apply_table(tables[odd], split(stack(*folded)), total)
            real, imag = spectrum[:half], spectrum[half:]
            weights = [
                beside(*[weight[pl.ds(odd * double + p * rows + row, half, stride=2 * double), :] for row in at]) for p in (0, 1)
            ]
            weighed = split(stack(real * weights[0] - imag * weights[1], real * weights[1] + imag * weights[0]))
            for part in (0, 1):
                out[pair, odd, part] = weighed[part]
        return carry

    lax.fori_loop(0, rows // 2, two_rows, 0)


def forward(arrived, weights, first):
    groups, _, double, width = arrived[0].shape
    total = weights.shape[0]
    whole = pl.BlockSpec(memory_space=pltpu.VMEM)
    shape = (double // 4, 2, 2, total, 2 * width)
    return pl.pallas_call(
        functools.partial(forward_kernel, first, groups, double // 2),
        in_specs=[whole] * (2 + len(first)),
        out_specs=whole,
        out_shape=jax.ShapeDtypeStruct(shape, BF16),
        compiler_params=params(60),
        cost_estimate=pl.CostEstimate(
            flops=6 * total * total * double * width, bytes_accessed=3 * total * double * width * 4, transcendentals=0
        ),
        name="forward",
    )(transform_tables(total, None), weights, *arrived)


def backward_kernel(size, groups, extra, tables, weighed, final_ref, out_ref, *scratch):
    pairs, _, _, total, double = weighed.shape
    width = double // 2
    rows = 2 * pairs
    count = groups * size
    share = width // (2 * extra) if extra else 0
    span = (size + size // share) * rows if extra else size * 2 * rows
    out = out_ref.reshape(groups * span, width)

    def store_whole(row, real, imag):
        kept = final_ref[pl.ds(row, 1), :] * (1.0 / total)
        for p, value in enumerate((-imag * kept, real * kept)):
            for j in range(groups):
                out[pl.ds(j * span + p * rows + row, size, stride=2 * rows), :] = value[j * size : (j + 1) * size]

    def store_packed(row, real, imag):
        value = beside(-imag, real) * (1.0 / total)
        both = dot(stack(*split(value)), final_ref[...])
        both = both[:count] + both[count:]
        scratch[0][...] = both[:, width:]
        quarter = [scratch[0][pl.ds(q, count // share, stride=share), :] for q in range(share)]
        lane = lane_of(quarter[0]) // (2 * extra)
        narrow = quarter[0]
        for q in range(1, share):
            narrow = jnp.where(lane == q, quarter[q], narrow)
        for j in range(groups):
            out[pl.ds(j * span + row, size, stride=rows), :] = both[j * size : (j + 1) * size, :width]
            short = size // share
            out[pl.ds(j * span + size * rows + row, short, stride=rows), :] = narrow[j * short : (j + 1) * short]

    def two_rows(pair, carry):
        backs = [apply_table(tables[odd], (weighed[pair, odd, 0], weighed[pair, odd, 1]), count) for odd in (0, 1)]
        early, late = backs[0] + backs[1], backs[0] - backs[1]
        for index in (0, 1):
            lanes = slice(index * width, (index + 1) * width)
            real = stack(early[: count // 2, lanes], late[: count // 2, lanes])
            imag = stack(early[count // 2 :, lanes], late[count // 2 :, lanes])
            (store_packed if extra else store_whole)(2 * pair + index, real, imag)
        return carry

    lax.fori_loop(0, pairs, two_rows, 0)


def backward(weighed, final, begin, size, groups, extra):
    pairs, _, _, total, double = weighed.shape
    width = double // 2
    rows = 2 * pairs
    local = total // groups
    chosen = [j * local + begin + l for j in range(groups // 2) for l in range(size)]
    if extra:
        share = width // (2 * extra)
        shape = (groups, (size + size // share) * rows, width)
        scratch = [pltpu.VMEM((groups * size, width), F32)]
    else:
        shape = (groups, size, 2 * rows, width)
        scratch = []
    whole = pl.BlockSpec(memory_space=pltpu.VMEM)
    return pl.pallas_call(
        functools.partial(backward_kernel, size, groups, extra),
        in_specs=[whole] * 3,
        out_specs=whole,
        out_shape=jax.ShapeDtypeStruct(shape, F32),
        scratch_shapes=scratch,
        compiler_params=params(28),
        cost_estimate=pl.CostEstimate(
            flops=6 * total * groups * size * 2 * rows * width,
            bytes_accessed=(total + groups * size) * 2 * rows * width * 4,
            transcendentals=0,
        ),
        name="backward",
    )(transform_tables(total, chosen), weighed, final)


def transform_tables(total, chosen):
    half = total // 2
    tables = []
    for odd in (0, 1):
        phase = (2 * np.arange(half)[:, None] + odd) * np.arange(half)[None, :] % total
        cosine, sine = np.cos(2.0 * np.pi / total * phase), np.sin(2.0 * np.pi / total * phase)
        if chosen is None:
            table = np.block([[cosine, sine], [-sine, cosine]])
        else:
            cosine, sine = cosine.T[chosen], sine.T[chosen]
            table = np.block([[cosine, -sine], [sine, cosine]])
        tables.append(table.astype(np.float32))
    high = [table.astype(jnp.bfloat16) for table in tables]
    low = [(table - part.astype(np.float32)).astype(jnp.bfloat16) for table, part in zip(tables, high)]
    return jnp.asarray(np.stack([np.concatenate(parts, axis=0) for parts in zip(high, low)]))


def neighbours(value, count):
    up = [(i, i + 1) for i in range(count - 1)]
    down = [(i + 1, i) for i in range(count - 1)]
    return lax.ppermute(value, "slab", up), lax.ppermute(value, "slab", down)


def exchange(value):
    return lax.all_to_all(value, "energy", split_axis=0, concat_axis=0, tiled=True)


def tied(value, earlier):
    return lax.optimization_barrier((value, earlier))[0]


def chunks_of(sizes):
    return [(sum(sizes[:i]), size) for i, size in enumerate(sizes)]


def placement(pattern, rank, extra):
    width = pattern.shape[0]
    lane = jnp.arange(2 * width)
    narrow = lane - width
    imag = jnp.where(lane < width, lane // (width // 2), narrow % (2 * extra) // extra)
    slot = jnp.where(lane < width, lane % (width // 2), width // 2 + narrow % extra)
    source = jnp.arange(2 * width)
    hit = (source[:, None] // width == imag[None, :]) & (jnp.tile(rank, 2)[:, None] == slot[None, :])
    return (hit & (jnp.tile(pattern, 2)[:, None] > 0)).astype(BF16)


def local(green_diag, green_lower, green_upper, sigma_lesser, screened, pattern):
    groups = lax.axis_size("energy")
    slabs = lax.axis_size("slab")
    _, energies, _, width, _ = sigma_lesser.shape
    rows = width // groups
    total = screened.shape[1]
    step = 4
    extra = width // 8
    cap = width // 2 + extra
    first = chunks_of([energies // 4] * 4)
    second = chunks_of([energies // 2] + [energies // 4] * 2)

    mine = pattern[0].astype(F32)
    sent = [sigma_lesser[0, at : at + size].reshape(2 * size * width, width) for at, size in first]
    edge = sent[0].shape[0]
    sent[0] = stack(sent[0], jnp.broadcast_to(mine, (8, width)))
    own = own_terms(green_diag, sigma_lesser, step)
    halos, bases, arrived = [neighbours(part, slabs) for part in sent[:2]], [], []
    patterns = jnp.stack([mine, halos[0][0][edge], halos[0][1][edge]])
    ranks = jnp.cumsum(patterns, axis=1).astype(jnp.int32) - 1
    places = jnp.stack([placement(patterns[side], ranks[side], extra) for side in range(3)])
    packed_greens = pack_green([green_diag, green_lower, green_upper], places, step, extra)
    for index, (at, size) in enumerate(first):
        if index + 2 < len(first):
            halos.append(neighbours(tied(sent[index + 2], (halos[index], own)), slabs))
        halo = halos[index]
        if index:
            halo = tied(halo, (arrived[max(index - 2, 0)], packed_greens))
        base, send = side_terms(own, green_lower, green_upper, *halo, at, size, groups, step)
        bases.append(base)
        arrived.append(exchange(send))

    fits = lax.pmax(tied(jnp.sum(mine), bases[-1]), "slab") <= cap
    chosen = ((ranks[0][None, :] == jnp.arange(cap)[:, None]) & (mine[None, :] > 0)).astype(BF16)
    own_rows = lax.dynamic_slice_in_dim(mine, lax.axis_index("energy") * rows, rows)
    mask = own_rows[:, None] * mine[None, :]
    weighed = forward(arrived, screened.reshape(total, 2 * rows, width), first)

    def within(begin, size):
        return [base for base, (at, _) in zip(bases, first) if begin <= at < begin + size]

    def packed_rest(weighed):
        packed, halos = [], []
        parts = [backward(weighed, places[0], at, size, groups, extra) for at, size in second]
        for index, part in enumerate(parts):
            part = exchange(tied(part, packed[-1]) if index else part)
            packed.append(pack_rows(chosen, part if index else tied(part, parts), rows))
            halos.append(neighbours(packed[-1], slabs))
        partials = [
            packed_again(None, within(at, size), packed_greens[:1], [part], at, size, step, (size, 2, width, width), extra)
            for part, (at, size) in zip(packed, second)
        ]
        result = None
        for partial, halo, (at, size) in zip(partials, halos, second):
            result = packed_again(result, [partial], packed_greens[1:], halo, at, size, step, green_lower.shape, extra)
        return result

    def whole_rest(weighed):
        base = jnp.concatenate(bases, axis=0)
        middles = [exchange(backward(weighed, mask, at, size, groups, 0)) for at, size in second]
        halos = [neighbours(part, slabs) for part in middles]
        partials = [
            whole_again(None, base, at, [green_diag], [part], at, step, (size, 2, width, width))
            for part, (at, size) in zip(middles, second)
        ]
        result = None
        for partial, halo, (at, _) in zip(partials, halos, second):
            result = whole_again(result, partial, 0, [green_lower, green_upper], halo, at, step, green_lower.shape)
        return result

    return lax.cond(fits, packed_rest, whole_rest, weighed)


def solution(mesh):
    return jax.shard_map(
        local,
        mesh=mesh,
        in_specs=(
            P("slab", "energy", None, None, None),
            P("slab", "energy", None, None, None),
            P("slab", "energy", None, None, None),
            P("slab", "energy", None, None, None),
            P("slab", None, None, "energy", None),
            P("slab", None),
        ),
        out_specs=P("slab", "energy", None, None, None),
        check_vma=False,
    )
```

time: 308 us -> 246 us (0.80)
  blocking collectives: 38.4 us -> 9.45 us
  waiting for transfers between devices: 74.6 us -> 50.3 us
  starting transfers between devices: 71.8 us -> 63.8 us
    all_to_all x2 -> x0, blocking collectives: 38.4 us -> none  [exchange(): lax.all_to_all(value, 'energy', split_axis=0, concat_axis=0, tiled=True)]
    ppermute x16 -> x14, waiting for transfers between devices: 50.2 us -> 21.7 us  [neighbours(): return (lax.ppermute(value, 'slab', up), lax.ppermute(value, 'slab', down))]
    ppermute x16 -> x14, starting transfers between devices: 49.7 us -> 38.2 us  [neighbours(): return (lax.ppermute(value, 'slab', up), lax.ppermute(value, 'slab', down))]
    pmax x0 -> x1, blocking collectives: none -> 9.45 us  [local(): fits = lax.pmax(tied(jnp.sum(mine), bases[-1]), 'slab') <= cap]
    all_to_all x6 -> x7, waiting for transfers between devices: 24.4 us -> 28.6 us  [exchange(): lax.all_to_all(value, 'energy', split_axis=0, concat_axis=0, tiled=True)]
    all_to_all x6 -> x7, starting transfers between devices: 22.1 us -> 25.5 us  [exchange(): lax.all_to_all(value, 'energy', split_axis=0, concat_axis=0, tiled=True)]
    pallas_call x14 -> x19, Pallas kernels: 113 us -> 111 us  [the longest x6 30.2 us: packed_again(): pl.pallas_call(functools.partial(packed_again_kernel, step, places, count...]
  transfers between devices with their start and end apart: 22 -> 21, of which waited for: 15 -> 10; matrix products, arithmetic and copies ran while one was open for 0% -> 1% of each run, Pallas kernels for 26% -> 35%
where the time goes in v2:
time: 246 us; the launch traced here: 244 us
  Pallas kernels  111 us (45%)
  starting transfers between devices  63.8 us (26%)
  waiting for transfers between devices  50.3 us (20%)
  blocking collectives  9.45 us (4%)
  local copies, waits for them, and re-layouts  5.08 us (2%)
  other arithmetic  3.65 us (1%)
    ppermute x14, starting transfers between devices, neighbours(): return (lax.ppermute(value, 'slab', up), lax.ppermute(value, 'slab', down))  38.2 us
    pallas_call x6, Pallas kernels, packed_again(): pl.pallas_call(functools.partial(packed_again_kernel, step, places, count...  30.2 us
    all_to_all x7, waiting for transfers between devices, exchange(): lax.all_to_all(value, 'energy', split_axis=0, concat_axis=0, tiled=True)  28.6 us
    all_to_all x7, starting transfers between devices, exchange(): lax.all_to_all(value, 'energy', split_axis=0, concat_axis=0, tiled=True)  25.5 us
    pallas_call x4, Pallas kernels, side_terms(): pl.pallas_call(functools.partial(side_terms_kernel, step), grid=(size //...  24.5 us
    ppermute x14, waiting for transfers between devices, neighbours(): return (lax.ppermute(value, 'slab', up), lax.ppermute(value, 'slab', down))  21.7 us
    pallas_call x3, Pallas kernels, backward(): pl.pallas_call(functools.partial(backward_kernel, size, groups, extra), i...  17.8 us
    pallas_call x1, Pallas kernels, forward(): pl.pallas_call(functools.partial(forward_kernel, first, groups, double //...  13.6 us
  transfers between devices with their start and end apart: 21, of which 10 were waited for; matrix products, arithmetic and copies ran while one was open for 1% of the time, Pallas kernels for 35%

profile of v2, /device:TPU:0, one launch (start us, length us, event | category | flops | bytes accessed | tf_op | source)
XLA Modules:
  0.0 244.3 jit_solution(16365203551101182517)
XLA Ops:
  0.0 4.0 %fusion.13 = (f32[1,8,2,128,128]{4,3,2,1,0:T(8,128)}, f32[1,8,2,128,128]{4,3,2,1,0:T(8,128)}, f32[1,8,2,128,128]{4,3,2,1,0:T(8,128)}, f32[1,8,2,128,128]{4,3,2,1,0:T(8,128)S(1)}) fusion(f32[1,32,2,128,128]{4,3,2,1,0:T(8,128)} %sigma.1), kind=kLoop, calls=%fused_computation.60 | loop fusion | bytes 8388608 | tf_op jit(solution)/shard_map/slice | solution.py:505
  4.1 5.0 %collective-permute-start.16 = (f32[2056,128]{1,0:T(8,128)S(1)}, f32[2056,128]{1,0:T(8,128)S(1)}, u32[]{:S(2)}, u32[]{:S(2)}) collective-permute-start(f32[2056,128]{1,0:T(8,128)S(1)} %pad_maximum_fusion), channel_id=1, source_target_pairs={{0,1},{1,2},{2,3},{4,5},{5,6},{6,7},{8,9},{9,10},{10,11},{12,13},{... | collective-permute-start | bytes 3158024 | tf_op jit(solution)/shard_map/ppermute | solution.py:466
  10.4 5.5 %collective-permute-start.12 = (f32[2048,128]{1,0:T(8,128)}, f32[2048,128]{1,0:T(8,128)}, u32[]{:S(2)}, u32[]{:S(2)}) collective-permute-start(f32[2048,128]{1,0:T(8,128)} %bitcast.1), channel_id=1, source_target_pairs={{0,1},{1,2},{2,3},{4,5},{5,6},{6,7},{8,9},{9,10},{10,11},{12,13},{... | collective-permute-start | bytes 3145736 | tf_op jit(solution)/shard_map/ppermute | solution.py:466
  17.2 11.3 %own_terms.1.total = f32[32,2,128,128]{3,2,1,0:T(8,128)} custom-call(f32[1,32,2,128,128]{4,3,2,1,0:T(8,128)} %refs_0_.1, f32[1,32,2,128,128]{4,3,2,1,0:T(8,128)} %sigma.1), custom_call_target="tpu_custom_call" | custom-call | flops 524288 | bytes 4096 | tf_op jit(solution)/shard_map/own_terms/pallas_call | solution.py:151
  28.6 4.1 %collective-permute-done.16.before = f32[2056,128]{1,0:T(8,128)S(1)} collective-permute-done((f32[2056,128]{1,0:T(8,128)S(1)}, f32[2056,128]{1,0:T(8,128)S(1)}, u32[]{:S(2)}, u32[]{:S(2)}) %collective-permute-start.16) | collective-permute-done | bytes 1052704 | tf_op jit(solution)/shard_map/ppermute | solution.py:466
  32.7 4.5 %collective-permute-done.17.after = f32[2056,128]{1,0:T(8,128)S(1)} collective-permute-done((f32[2056,128]{1,0:T(8,128)S(1)}, f32[2056,128]{1,0:T(8,128)S(1)}, u32[]{:S(2)}, u32[]{:S(2)}) %collective-permute-start.17) | collective-permute-done | bytes 1052704 | tf_op jit(solution)/shard_map/ppermute | solution.py:466
  37.1 4.4 %collective-permute-start.18 = (f32[2048,128]{1,0:T(8,128)}, f32[2048,128]{1,0:T(8,128)}, u32[]{:S(2)}, u32[]{:S(2)}) collective-permute-start(f32[2048,128]{1,0:T(8,128)} %bitcast.34), channel_id=1, source_target_pairs={{0,1},{1,2},{2,3},{4,5},{5,6},{6,7},{8,9},{9,10},{10,11},{12,13},{... | collective-permute-start | bytes 3145736 | tf_op jit(solution)/shard_map/ppermute | solution.py:466
  43.2 6.0 %side_terms.4 = (f32[8,2,128,128]{3,2,1,0:T(8,128)}, f32[8,8,32,128]{3,2,1,0:T(8,128)}) custom-call(f32[32,2,128,128]{3,2,1,0:T(8,128)} %own_terms.1.total, f32[1,32,2,128,128]{4,3,2,1,0:T(8,128)} %lower.7, f32[1,32,2,128,128]{4,3,2,1,0:T(8,128)} %upper.7, f32[2056,128]{1,0:T(8,128)} %copy-done.18, f32[2056,128]{1,0:T(8,128)} %copy-done.19), custom_call_target="tpu_custom_call" | custom-call | flops 262144 | bytes 2048 | tf_op jit(solution)/shard_map/side_terms/pallas_call | solution.py:176
  49.2 3.7 %all-to-all-start.6 = ((f32[8,8,32,128]{3,2,1,0:T(8,128)}), f32[8,8,32,128]{3,2,1,0:T(8,128)S(1)}, u32[]{:S(2)}, u32[]{:S(2)}) async-start(f32[8,8,32,128]{3,2,1,0:T(8,128)} %get-tuple-element.124), calls=%async_computation.6 | async-start | bytes 2097152 | tf_op jit(solution)/shard_map/all_to_all | solution.py:470
  54.8 12.2 %pack_green.1 = (bf16[32,256,256]{2,1,0:T(8,128)(2,1)}, bf16[32,256,256]{2,1,0:T(8,128)(2,1)}, bf16[32,256,256]{2,1,0:T(8,128)(2,1)}) custom-call(bf16[3,256,256]{2,1,0:T(8,128)(2,1)} %add_convert_fusion.place, f32[1,32,2,128,128]{4,3,2,1,0:T(8,128)} %refs_0_.1, f32[1,32,2,128,128]{4,3,2,1,0:T(8,128)} %lower.7, f32[1,32,2,128,128]{4,3,2,1,0:T(8,128)} %upper.7), custom_call_target="tpu_custom_call" | custom-call | flops 3221225472 | bytes 25165824 | tf_op jit(solution)/shard_map/pack_green/pallas_call | solution.py:277
  68.4 6.4 %side_terms.5 = (f32[8,2,128,128]{3,2,1,0:T(8,128)}, f32[8,8,32,128]{3,2,1,0:T(8,128)}) custom-call(f32[32,2,128,128]{3,2,1,0:T(8,128)} %own_terms.1.total, f32[1,32,2,128,128]{4,3,2,1,0:T(8,128)} %lower.7, f32[1,32,2,128,128]{4,3,2,1,0:T(8,128)} %upper.7, f32[2048,128]{1,0:T(8,128)} %collective-permute-done.12.before, f32[2048,128]{1,0:T(8,128)} %collective-permute-done.13.after), custom_call_target="tpu_custom_call" | custom-call | flops 262144 | bytes 2048 | tf_op jit(solution)/shard_map/side_terms/pallas_call | solution.py:176
  78.3 4.6 %collective-permute-start.14 = (f32[2048,128]{1,0:T(8,128)}, f32[2048,128]{1,0:T(8,128)S(1)}, u32[]{:S(2)}, u32[]{:S(2)}) collective-permute-start(f32[2048,128]{1,0:T(8,128)} %bitcast), channel_id=1, source_target_pairs={{0,1},{1,2},{2,3},{4,5},{5,6},{6,7},{8,9},{9,10},{10,11},{12,13},{... | collective-permute-start | bytes 3145736 | tf_op jit(solution)/shard_map/ppermute | solution.py:466
  84.3 6.1 %side_terms.7 = (f32[8,2,128,128]{3,2,1,0:T(8,128)}, f32[8,8,32,128]{3,2,1,0:T(8,128)}) custom-call(f32[32,2,128,128]{3,2,1,0:T(8,128)} %own_terms.1.total, f32[1,32,2,128,128]{4,3,2,1,0:T(8,128)} %lower.7, f32[1,32,2,128,128]{4,3,2,1,0:T(8,128)} %upper.7, f32[2048,128]{1,0:T(8,128)} %collective-permute-done.18.before, f32[2048,128]{1,0:T(8,128)} %collective-permute-done.19.after), custom_call_target="tpu_custom_call" | custom-call | flops 262144 | bytes 2048 | tf_op jit(solution)/shard_map/side_terms/pallas_call | solution.py:176
  97.2 8.9 %collective-permute-done.14.before = f32[2048,128]{1,0:T(8,128)S(1)} collective-permute-done((f32[2048,128]{1,0:T(8,128)}, f32[2048,128]{1,0:T(8,128)S(1)}, u32[]{:S(2)}, u32[]{:S(2)}) %collective-permute-start.14) | collective-permute-done | bytes 1048608 | tf_op jit(solution)/shard_map/ppermute | solution.py:466
  106.2 4.2 %collective-permute-done.15.after = f32[2048,128]{1,0:T(8,128)} collective-permute-done((f32[2048,128]{1,0:T(8,128)}, f32[2048,128]{1,0:T(8,128)}, u32[]{:S(2)}, u32[]{:S(2)}) %collective-permute-start.15) | collective-permute-done | bytes 1048608 | tf_op jit(solution)/shard_map/ppermute | solution.py:466
  110.4 6.0 %side_terms.6 = (f32[8,2,128,128]{3,2,1,0:T(8,128)}, f32[8,8,32,128]{3,2,1,0:T(8,128)}) custom-call(f32[32,2,128,128]{3,2,1,0:T(8,128)} %own_terms.1.total, f32[1,32,2,128,128]{4,3,2,1,0:T(8,128)} %lower.7, f32[1,32,2,128,128]{4,3,2,1,0:T(8,128)} %upper.7, f32[2048,128]{1,0:T(8,128)} %copy-done.20, f32[2048,128]{1,0:T(8,128)} %collective-permute-done.15.after), custom_call_target="tpu_custom_call" | custom-call | flops 262144 | bytes 2048 | tf_op jit(solution)/shard_map/side_terms/pallas_call | solution.py:176
  116.4 3.9 %all-to-all-start.9 = ((f32[8,8,32,128]{3,2,1,0:T(8,128)}), f32[8,8,32,128]{3,2,1,0:T(8,128)S(1)}, u32[]{:S(2)}, u32[]{:S(2)}) async-start(f32[8,8,32,128]{3,2,1,0:T(8,128)} %get-tuple-element.142), calls=%async_computation.9 | async-start | bytes 2097152 | tf_op jit(solution)/shard_map/all_to_all | solution.py:470
  121.7 9.5 %pmax.7 = f32[]{:T(128)} all-reduce(f32[]{:T(128)} %convert_reduce_fusion), channel_id=1, replica_groups=mesh['energy'=8,'slab'=4] {'slab'}, use_global_device_ids=true, to_apply=%region_2.3 | all-reduce | flops 1 | bytes 8 | tf_op jit(solution)/shard_map/pmax | solution.py:524
  131.8 3.9 %all-to-all-done.9.refs_3_ = f32[8,8,32,128]{3,2,1,0:T(8,128)S(1)} async-done(((f32[8,8,32,128]{3,2,1,0:T(8,128)}), f32[8,8,32,128]{3,2,1,0:T(8,128)S(1)}, u32[]{:S(2)}, u32[]{:S(2)}) %all-to-all-start.9) | async-done | bytes 1048608 | tf_op jit(solution)/shard_map/all_to_all | solution.py:470
  136.7 13.6 %forward.1 = bf16[8,2,2,256,256]{4,3,2,1,0:T(8,128)(2,1)} custom-call(bf16[2,512,256]{2,1,0:T(8,128)(2,1)} %constant.141.clone.tables, f32[256,32,128]{2,1,0:T(8,128)} %bitcast.32, f32[8,8,32,128]{3,2,1,0:T(8,128)} %copy-done.14, f32[8,8,32,128]{3,2,1,0:T(8,128)} %copy-done.15, f32[8,8,32,128]{3,2,1,0:T(8,128)} %copy-done.16, f32[8,8,32,128]{3,2,1,0:T(8,128)} %copy-done.17), custom_call_target="tpu_custom_call" | custom-call | flops 1610612736 | bytes 12582912 | tf_op jit(solution)/shard_map/forward/pallas_call | solution.py:360
  150.3 94.0 %conditional.1 = (f32[1,32,2,128,128]{4,3,2,1,0:T(8,128)}) conditional(s32[]{:T(128)} %convert_element_type.46, (f32[8,2,128,128]{3,2,1,0:T(8,128)}, f32[8,2,128,128]{3,2,1,0:T(8,128)}, f32[8,2,128,128]{3,2,1,0:T(8,128)}, f32[8,2,128,128]{3,2,1,0:T(8,128)}, s32[]{:T(128)}, /*index=5*/f32[128]{0:T(128)S(1)}, bf16[2,256,256]{2,1,0:T(8,128)(2,1)S(1)}, ...), branch_computations={%region_3.4_spmd, %region_4.5_spmd} | conditional | flops 1821900800 | bytes 154162496 | solution.py:562
  150.3 7.3 %backward.9 = f32[8,320,128]{2,1,0:T(8,128)} custom-call(bf16[2,256,256]{2,1,0:T(8,128)(2,1)S(1)} %get-tuple-element.91.tables, bf16[8,2,2,256,256]{4,3,2,1,0:T(8,128)(2,1)} %get-tuple-element.92.weighed, bf16[256,256]{1,0:T(8,128)(2,1)S(1)} %get-tuple-element.93.final_ref), custom_call_target="tpu_custom_call" | custom-call | flops 805306368 | bytes 6291456 | tf_op jit(solution)/shard_map/cond/branch_1_fun/backward/pallas_call | solution.py:430
  161.4 6.4 %backward.10 = f32[8,160,128]{2,1,0:T(8,128)} custom-call(bf16[2,128,256]{2,1,0:T(8,128)(2,1)S(1)} %copy-done.23, bf16[8,2,2,256,256]{4,3,2,1,0:T(8,128)(2,1)} %get-tuple-element.92.weighed, bf16[256,256]{1,0:T(8,128)(2,1)S(1)} %get-tuple-element.93.final_ref), custom_call_target="tpu_custom_call" | custom-call | flops 402653184 | bytes 5242880 | tf_op jit(solution)/shard_map/cond/branch_1_fun/backward/pallas_call | solution.py:430
  167.8 4.1 %backward.11 = f32[8,160,128]{2,1,0:T(8,128)} custom-call(bf16[2,128,256]{2,1,0:T(8,128)(2,1)S(1)} %copy-done.25, bf16[8,2,2,256,256]{4,3,2,1,0:T(8,128)(2,1)S(1)} %copy-done.5, bf16[256,256]{1,0:T(8,128)(2,1)S(1)} %get-tuple-element.93.final_ref), custom_call_target="tpu_custom_call" | custom-call | flops 402653184 | bytes 5242880 | tf_op jit(solution)/shard_map/cond/branch_1_fun/backward/pallas_call | solution.py:430
  171.9 7.6 %all-to-all-done.part = f32[8,320,128]{2,1,0:T(8,128)S(1)} async-done(((f32[8,320,128]{2,1,0:T(8,128)}), f32[8,320,128]{2,1,0:T(8,128)S(1)}, u32[]{:S(2)}, u32[]{:S(2)}) %all-to-all-start) | async-done | bytes 1310752 | tf_op jit(solution)/shard_map/cond/branch_1_fun/all_to_all | solution.py:470
  186.2 8.5 %all-to-all-done.1.part = f32[8,160,128]{2,1,0:T(8,128)S(1)} async-done(((f32[8,160,128]{2,1,0:T(8,128)}), f32[8,160,128]{2,1,0:T(8,128)S(1)}, u32[]{:S(2)}, u32[]{:S(2)}) %all-to-all-start.1) | async-done | bytes 655392 | tf_op jit(solution)/shard_map/cond/branch_1_fun/all_to_all | solution.py:470
  200.0 4.6 %collective-permute-start.2 = (f32[10,80,128]{2,1,0:T(8,128)S(1)}, f32[10,80,128]{2,1,0:T(8,128)S(1)}, u32[]{:S(2)}, u32[]{:S(2)}) collective-permute-start(f32[10,80,128]{2,1,0:T(8,128)S(1)} %pack_rows.4.refs_2_), channel_id=1, source_target_pairs={{0,1},{1,2},{2,3},{4,5},{5,6},{6,7},{8,9},{9,10},{10,11},{12,13},{... | collective-permute-start | bytes 1228808 | tf_op jit(solution)/shard_map/cond/branch_1_fun/ppermute | solution.py:466
  205.9 3.9 %all-to-all-done.2.part = f32[8,160,128]{2,1,0:T(8,128)S(1)} async-done(((f32[8,160,128]{2,1,0:T(8,128)}), f32[8,160,128]{2,1,0:T(8,128)S(1)}, u32[]{:S(2)}, u32[]{:S(2)}) %all-to-all-start.2) | async-done | bytes 655392 | tf_op jit(solution)/shard_map/cond/branch_1_fun/all_to_all | solution.py:470
  214.0 6.5 %packed_again.6.refs_0_ = f32[16,2,128,128]{3,2,1,0:T(8,128)S(1)} custom-call(f32[8,2,128,128]{3,2,1,0:T(8,128)} %get-tuple-element.87.refs_0_, f32[8,2,128,128]{3,2,1,0:T(8,128)} %get-tuple-element.88.refs_1_, bf16[32,256,256]{2,1,0:T(8,128)(2,1)} %get-tuple-element.89.refs_2_.refs_1_, f32[20,80,128]{2,1,0:T(8,128)S(1)} %pack_rows.3.refs_3_), custom_call_target="tpu_custom_call" | custom-call | flops 262144 | bytes 2048 | tf_op jit(solution)/shard_map/cond/branch_1_fun/packed_again/pallas_call | solution.py:246
  222.8 9.2 %packed_again.7.refs_0_ = f32[1,32,2,128,128]{4,3,2,1,0:T(8,128)} custom-call(f32[16,2,128,128]{3,2,1,0:T(8,128)S(1)} %packed_again.6.refs_0_, bf16[32,256,256]{2,1,0:T(8,128)(2,1)S(1)} %copy-done.8, bf16[32,256,256]{2,1,0:T(8,128)(2,1)S(1)} %copy-done.9, f32[20,80,128]{2,1,0:T(8,128)S(1)} %collective-permute-done.refs_3_, ...), custom_call_target="tpu_custom_call" | custom-call | flops 524288 | bytes 4096 | tf_op jit(solution)/shard_map/cond/branch_1_fun/packed_again/pallas_call | solution.py:246
  232.1 5.5 %packed_again.9.refs_0_ = f32[1,32,2,128,128]{4,3,2,1,0:T(8,128)} custom-call(f32[1,32,2,128,128]{4,3,2,1,0:T(8,128)} %packed_again.7.refs_0_, f32[8,2,128,128]{3,2,1,0:T(8,128)S(1)} %packed_again.8.refs_1_, bf16[32,256,256]{2,1,0:T(8,128)(2,1)S(1)} %copy-done.8, bf16[32,256,256]{2,1,0:T(8,128)(2,1)S(1)} %copy-done.9, ...), custom_call_target="tpu_custom_call", output_to_operand_aliasing={{}: (0, {})} | custom-call | flops 262144 | bytes 2048 | tf_op jit(solution)/shard_map/cond/branch_1_fun/packed_again/pallas_call | solution.py:246
  239.8 4.4 %packed_again.11 = f32[1,32,2,128,128]{4,3,2,1,0:T(8,128)} custom-call(f32[1,32,2,128,128]{4,3,2,1,0:T(8,128)} %packed_again.9.refs_0_, f32[8,2,128,128]{3,2,1,0:T(8,128)S(1)} %packed_again.10.refs_1_, bf16[32,256,256]{2,1,0:T(8,128)(2,1)S(1)} %copy-done.8, bf16[32,256,256]{2,1,0:T(8,128)(2,1)S(1)} %copy-done.9, ...), custom_call_target="tpu_custom_call", output_to_operand_aliasing={{}: (0, {})} | custom-call | flops 262144 | bytes 2048 | tf_op jit(solution)/shard_map/cond/branch_1_fun/packed_again/pallas_call | solution.py:246
  (93 shorter events, 47.2 us)
Async XLA Ops:
  4.1 28.6 %collective-permute-start.16 = (f32[2056,128]{1,0:T(8,128)S(1)}, f32[2056,128]{1,0:T(8,128)S(1)}, u32[]{:S(2)}, u32[]{:S(2)}) collective-permute-start(f32[2056,128]{1,0:T(8,128)S(1)} %pad_maximum_fusion), channel_id=1, source_target_pairs={{0,1},{1,2},{2,3},{4,5},{5,6},{6,7},{8,9},{9,10},{10,11},{12,13},{... | collective-permute-start | bytes 3158024 | tf_op jit(solution)/shard_map/ppermute | solution.py:466
  9.1 28.1 %collective-permute-start.17 = (f32[2056,128]{1,0:T(8,128)S(1)}, f32[2056,128]{1,0:T(8,128)S(1)}, u32[]{:S(2)}, u32[]{:S(2)}) collective-permute-start(f32[2056,128]{1,0:T(8,128)S(1)} %pad_maximum_fusion), channel_id=1, source_target_pairs={{1,0},{2,1},{3,2},{5,4},{6,5},{7,6},{9,8},{10,9},{11,10},{13,12},{... | collective-permute-start | bytes 3158024 | tf_op jit(solution)/shard_map/ppermute | solution.py:466
  10.4 56.6 %collective-permute-start.12 = (f32[2048,128]{1,0:T(8,128)}, f32[2048,128]{1,0:T(8,128)}, u32[]{:S(2)}, u32[]{:S(2)}) collective-permute-start(f32[2048,128]{1,0:T(8,128)} %bitcast.1), channel_id=1, source_target_pairs={{0,1},{1,2},{2,3},{4,5},{5,6},{6,7},{8,9},{9,10},{10,11},{12,13},{... | collective-permute-start | bytes 3145736 | tf_op jit(solution)/shard_map/ppermute | solution.py:466
  15.9 51.1 %collective-permute-start.13 = (f32[2048,128]{1,0:T(8,128)}, f32[2048,128]{1,0:T(8,128)}, u32[]{:S(2)}, u32[]{:S(2)}) collective-permute-start(f32[2048,128]{1,0:T(8,128)} %bitcast.1), channel_id=1, source_target_pairs={{1,0},{2,1},{3,2},{5,4},{6,5},{7,6},{9,8},{10,9},{11,10},{13,12},{... | collective-permute-start | bytes 3145736 | tf_op jit(solution)/shard_map/ppermute | solution.py:466
  32.6 10.6 %copy-start.18 = (f32[2056,128]{1,0:T(8,128)}, f32[2056,128]{1,0:T(8,128)S(1)}, u32[]{:S(2)}) copy-start(f32[2056,128]{1,0:T(8,128)S(1)} %collective-permute-done.16.before) | copy-start | bytes 3158020
  37.1 47.1 %collective-permute-start.18 = (f32[2048,128]{1,0:T(8,128)}, f32[2048,128]{1,0:T(8,128)}, u32[]{:S(2)}, u32[]{:S(2)}) collective-permute-start(f32[2048,128]{1,0:T(8,128)} %bitcast.34), channel_id=1, source_target_pairs={{0,1},{1,2},{2,3},{4,5},{5,6},{6,7},{8,9},{9,10},{10,11},{12,13},{... | collective-permute-start | bytes 3145736 | tf_op jit(solution)/shard_map/ppermute | solution.py:466
  41.5 42.8 %collective-permute-start.19 = (f32[2048,128]{1,0:T(8,128)}, f32[2048,128]{1,0:T(8,128)}, u32[]{:S(2)}, u32[]{:S(2)}) collective-permute-start(f32[2048,128]{1,0:T(8,128)} %bitcast.35), channel_id=1, source_target_pairs={{1,0},{2,1},{3,2},{5,4},{6,5},{7,6},{9,8},{10,9},{11,10},{13,12},{... | collective-permute-start | bytes 3145736 | tf_op jit(solution)/shard_map/ppermute | solution.py:466
  49.2 19.1 %all-to-all-start.6 = ((f32[8,8,32,128]{3,2,1,0:T(8,128)}), f32[8,8,32,128]{3,2,1,0:T(8,128)S(1)}, u32[]{:S(2)}, u32[]{:S(2)}) async-start(f32[8,8,32,128]{3,2,1,0:T(8,128)} %get-tuple-element.124), calls=%async_computation.6 | async-start | bytes 2097152 | tf_op jit(solution)/shard_map/all_to_all | solution.py:470
  74.8 18.9 %all-to-all-start.7 = ((f32[8,8,32,128]{3,2,1,0:T(8,128)}), f32[8,8,32,128]{3,2,1,0:T(8,128)S(1)}, u32[]{:S(2)}, u32[]{:S(2)}) async-start(f32[8,8,32,128]{3,2,1,0:T(8,128)} %get-tuple-element.130), calls=%async_computation.7 | async-start | bytes 2097152 | tf_op jit(solution)/shard_map/all_to_all | solution.py:470
  78.3 27.8 %collective-permute-start.14 = (f32[2048,128]{1,0:T(8,128)}, f32[2048,128]{1,0:T(8,128)S(1)}, u32[]{:S(2)}, u32[]{:S(2)}) collective-permute-start(f32[2048,128]{1,0:T(8,128)} %bitcast), channel_id=1, source_target_pairs={{0,1},{1,2},{2,3},{4,5},{5,6},{6,7},{8,9},{9,10},{10,11},{12,13},{... | collective-permute-start | bytes 3145736 | tf_op jit(solution)/shard_map/ppermute | solution.py:466
  83.0 27.4 %collective-permute-start.15 = (f32[2048,128]{1,0:T(8,128)}, f32[2048,128]{1,0:T(8,128)}, u32[]{:S(2)}, u32[]{:S(2)}) collective-permute-start(f32[2048,128]{1,0:T(8,128)} %bitcast), channel_id=1, source_target_pairs={{1,0},{2,1},{3,2},{5,4},{6,5},{7,6},{9,8},{10,9},{11,10},{13,12},{... | collective-permute-start | bytes 3145736 | tf_op jit(solution)/shard_map/ppermute | solution.py:466
  93.7 22.7 %copy-start.15 = (f32[8,8,32,128]{3,2,1,0:T(8,128)}, f32[8,8,32,128]{3,2,1,0:T(8,128)S(1)}, u32[]{:S(2)}) copy-start(f32[8,8,32,128]{3,2,1,0:T(8,128)S(1)} %all-to-all-done.7.refs_1_) | copy-start | bytes 3145732
  93.7 22.7 %all-to-all-start.8 = ((f32[8,8,32,128]{3,2,1,0:T(8,128)}), f32[8,8,32,128]{3,2,1,0:T(8,128)S(1)}, u32[]{:S(2)}, u32[]{:S(2)}) async-start(f32[8,8,32,128]{3,2,1,0:T(8,128)} %get-tuple-element.141), calls=%async_computation.8 | async-start | bytes 2097152 | tf_op jit(solution)/shard_map/all_to_all | solution.py:470
  116.4 19.3 %copy-start.16 = (f32[8,8,32,128]{3,2,1,0:T(8,128)}, f32[8,8,32,128]{3,2,1,0:T(8,128)S(1)}, u32[]{:S(2)}) copy-start(f32[8,8,32,128]{3,2,1,0:T(8,128)S(1)} %all-to-all-done.8.refs_2_) | copy-start | bytes 3145732
  116.4 19.3 %all-to-all-start.9 = ((f32[8,8,32,128]{3,2,1,0:T(8,128)}), f32[8,8,32,128]{3,2,1,0:T(8,128)S(1)}, u32[]{:S(2)}, u32[]{:S(2)}) async-start(f32[8,8,32,128]{3,2,1,0:T(8,128)} %get-tuple-element.142), calls=%async_computation.9 | async-start | bytes 2097152 | tf_op jit(solution)/shard_map/all_to_all | solution.py:470
  136.7 13.6 %copy-start.21 = (bf16[2,256,256]{2,1,0:T(8,128)(2,1)S(1)}, bf16[2,256,256]{2,1,0:T(8,128)(2,1)}, u32[]{:S(2)}) copy-start(bf16[2,256,256]{2,1,0:T(8,128)(2,1)} %constant.142.clone) | copy-start | bytes 786436
  150.3 11.1 %copy-start.23 = (bf16[2,128,256]{2,1,0:T(8,128)(2,1)S(1)}, bf16[2,128,256]{2,1,0:T(8,128)(2,1)}, u32[]{:S(2)}) copy-start(bf16[2,128,256]{2,1,0:T(8,128)(2,1)} %get-tuple-element.94.tables) | copy-start | bytes 393220 | tf_op jit(solution)/shard_map/cond
  157.7 10.2 %copy-start.25 = (bf16[2,128,256]{2,1,0:T(8,128)(2,1)S(1)}, bf16[2,128,256]{2,1,0:T(8,128)(2,1)}, u32[]{:S(2)}) copy-start(bf16[2,128,256]{2,1,0:T(8,128)(2,1)} %get-tuple-element.95.tables) | copy-start | bytes 393220 | tf_op jit(solution)/shard_map/cond
  157.7 21.9 %all-to-all-start = ((f32[8,320,128]{2,1,0:T(8,128)}), f32[8,320,128]{2,1,0:T(8,128)S(1)}, u32[]{:S(2)}, u32[]{:S(2)}) async-start(f32[8,320,128]{2,1,0:T(8,128)} %backward.9), calls=%async_computation | async-start | bytes 2621440 | tf_op jit(solution)/shard_map/cond/branch_1_fun/all_to_all | solution.py:470
  161.4 6.5 %copy-start.5 = (bf16[8,2,2,256,256]{4,3,2,1,0:T(8,128)(2,1)S(1)}, bf16[8,2,2,256,256]{4,3,2,1,0:T(8,128)(2,1)}, u32[]{:S(2)}) copy-start(bf16[8,2,2,256,256]{4,3,2,1,0:T(8,128)(2,1)} %get-tuple-element.92.weighed) | copy-start | bytes 12582916 | tf_op jit(solution)/shard_map/cond
  161.4 18.1 %copy-start.26 = (bf16[80,128]{1,0:T(8,128)(2,1)S(1)}, bf16[80,128]{1,0:T(8,128)(2,1)}, u32[]{:S(2)}) copy-start(bf16[80,128]{1,0:T(8,128)(2,1)} %get-tuple-element.90.chosen) | copy-start | bytes 61444 | tf_op jit(solution)/shard_map/cond
  180.1 14.6 %all-to-all-start.1 = ((f32[8,160,128]{2,1,0:T(8,128)}), f32[8,160,128]{2,1,0:T(8,128)S(1)}, u32[]{:S(2)}, u32[]{:S(2)}) async-start(f32[8,160,128]{2,1,0:T(8,128)} %backward.10), calls=%async_computation.1 | async-start | bytes 1310720 | tf_op jit(solution)/shard_map/cond/branch_1_fun/all_to_all | solution.py:470
  183.7 29.0 %collective-permute-start = (f32[20,80,128]{2,1,0:T(8,128)S(1)}, f32[20,80,128]{2,1,0:T(8,128)S(1)}, u32[]{:S(2)}, u32[]{:S(2)}) collective-permute-start(f32[20,80,128]{2,1,0:T(8,128)S(1)} %pack_rows.3.refs_3_), channel_id=1, source_target_pairs={{0,1},{1,2},{2,3},{4,5},{5,6},{6,7},{8,9},{9,10},{10,11},{12,13},{... | collective-permute-start | bytes 2457608 | tf_op jit(solution)/shard_map/cond/branch_1_fun/ppermute | solution.py:466
  195.1 14.6 %all-to-all-start.2 = ((f32[8,160,128]{2,1,0:T(8,128)}), f32[8,160,128]{2,1,0:T(8,128)S(1)}, u32[]{:S(2)}, u32[]{:S(2)}) async-start(f32[8,160,128]{2,1,0:T(8,128)} %backward.11), calls=%async_computation.2 | async-start | bytes 1310720 | tf_op jit(solution)/shard_map/cond/branch_1_fun/all_to_all | solution.py:470
  198.7 24.1 %collective-permute-start.1 = (f32[20,80,128]{2,1,0:T(8,128)S(1)}, f32[20,80,128]{2,1,0:T(8,128)}, u32[]{:S(2)}, u32[]{:S(2)}) collective-permute-start(f32[20,80,128]{2,1,0:T(8,128)S(1)} %pack_rows.3.refs_3_), channel_id=1, source_target_pairs={{1,0},{2,1},{3,2},{5,4},{6,5},{7,6},{9,8},{10,9},{11,10},{13,12},{... | collective-permute-start | bytes 2457608 | tf_op jit(solution)/shard_map/cond/branch_1_fun/ppermute | solution.py:466
  200.0 32.1 %collective-permute-start.2 = (f32[10,80,128]{2,1,0:T(8,128)S(1)}, f32[10,80,128]{2,1,0:T(8,128)S(1)}, u32[]{:S(2)}, u32[]{:S(2)}) collective-permute-start(f32[10,80,128]{2,1,0:T(8,128)S(1)} %pack_rows.4.refs_2_), channel_id=1, source_target_pairs={{0,1},{1,2},{2,3},{4,5},{5,6},{6,7},{8,9},{9,10},{10,11},{12,13},{... | collective-permute-start | bytes 1228808 | tf_op jit(solution)/shard_map/cond/branch_1_fun/ppermute | solution.py:466
  204.6 27.4 %collective-permute-start.3 = (f32[10,80,128]{2,1,0:T(8,128)S(1)}, f32[10,80,128]{2,1,0:T(8,128)}, u32[]{:S(2)}, u32[]{:S(2)}) collective-permute-start(f32[10,80,128]{2,1,0:T(8,128)S(1)} %pack_rows.4.refs_2_), channel_id=1, source_target_pairs={{1,0},{2,1},{3,2},{5,4},{6,5},{7,6},{9,8},{10,9},{11,10},{13,12},{... | collective-permute-start | bytes 1228808 | tf_op jit(solution)/shard_map/cond/branch_1_fun/ppermute | solution.py:466
  209.8 10.8 %copy-start.11 = (f32[8,2,128,128]{3,2,1,0:T(8,128)S(1)}, f32[8,2,128,128]{3,2,1,0:T(8,128)}, u32[]{:S(2)}) copy-start(f32[8,2,128,128]{3,2,1,0:T(8,128)} %get-tuple-element.99.refs_0_) | copy-start | bytes 3145732 | tf_op jit(solution)/shard_map/cond
  210.1 29.7 %collective-permute-start.4 = (f32[10,80,128]{2,1,0:T(8,128)S(1)}, f32[10,80,128]{2,1,0:T(8,128)S(1)}, u32[]{:S(2)}, u32[]{:S(2)}) collective-permute-start(f32[10,80,128]{2,1,0:T(8,128)S(1)} %pack_rows.5.refs_2_), channel_id=1, source_target_pairs={{0,1},{1,2},{2,3},{4,5},{5,6},{6,7},{8,9},{9,10},{10,11},{12,13},{... | collective-permute-start | bytes 1228808 | tf_op jit(solution)/shard_map/cond/branch_1_fun/ppermute | solution.py:466
  212.6 27.2 %collective-permute-start.5 = (f32[10,80,128]{2,1,0:T(8,128)S(1)}, f32[10,80,128]{2,1,0:T(8,128)S(1)}, u32[]{:S(2)}, u32[]{:S(2)}) collective-permute-start(f32[10,80,128]{2,1,0:T(8,128)S(1)} %pack_rows.5.refs_2_), channel_id=1, source_target_pairs={{1,0},{2,1},{3,2},{5,4},{6,5},{7,6},{9,8},{10,9},{11,10},{13,12},{... | collective-permute-start | bytes 1228808 | tf_op jit(solution)/shard_map/cond/branch_1_fun/ppermute | solution.py:466
  213.9 6.6 %copy-start.7 = (bf16[32,256,256]{2,1,0:T(8,128)(2,1)S(1)}, bf16[32,256,256]{2,1,0:T(8,128)(2,1)}, u32[]{:S(2)}) copy-start(bf16[32,256,256]{2,1,0:T(8,128)(2,1)} %get-tuple-element.89.refs_2_.refs_1_) | copy-start | bytes 12582916 | tf_op jit(solution)/shard_map/cond
  214.0 8.8 %copy-start.9 = (bf16[32,256,256]{2,1,0:T(8,128)(2,1)S(1)}, bf16[32,256,256]{2,1,0:T(8,128)(2,1)}, u32[]{:S(2)}) copy-start(bf16[32,256,256]{2,1,0:T(8,128)(2,1)} %get-tuple-element.98.refs_2_.refs_3_) | copy-start | bytes 12582916 | tf_op jit(solution)/shard_map/cond
  (7 other events, 29.5 us)

commit v3 on v2

--- a/solution.py
+++ b/solution.py
@@ -11,6 +11,7 @@
 F32 = jnp.float32
 BF16 = jnp.bfloat16
 MIB = 1024 * 1024
+UNROLL = 2
 
 
 def params(mebibytes=16):
@@ -41,10 +42,10 @@
     return both[:rows] + (both[rows:] + dot(first[:rows], second[1]))
 
 
-def sandwich(green, middle, turn):
+def sandwich(green, middle):
     rows = green.shape[0] // 2
     first = dot_stacked(green, middle)
-    out = dot(stack(*split(first), *split(turn(first))), green, transposed=True)
+    out = dot(stack(*split(first), *split(turn_halves(first))), green, transposed=True)
     real, real_low, imag, imag_low = (out[i * rows : (i + 1) * rows] for i in range(4))
     return beside(real[:, :rows] + (real[:, rows:] + real_low[:, :rows]), imag[:, :rows] + (imag[:, rows:] + imag_low[:, :rows]))
 
@@ -52,6 +53,16 @@
 def turn_halves(value):
     width = value.shape[1] // 2
     return beside(value[:, width:], -value[:, :width])
+
+
+def packed_sandwich(green, middle, turned, spread):
+    rows, inner = green.shape[0] // 2, middle[0].shape[0]
+    out = dot(stack(*middle, *turned), green, transposed=True)
+    real, real_low, imag, imag_low = (out[i * inner : (i + 1) * inner] for i in range(4))
+    inside = beside(real[:, :rows] + (real[:, rows:] + real_low[:, :rows]), imag[:, :rows] + (imag[:, rows:] + imag_low[:, :rows]))
+    high, low = (spread(part, beside(-part[:, rows:], part[:, :rows])) for part in split(inside))
+    both = dot(green, high)
+    return both[:rows] + (both[rows:] + dot(green[:rows], low))
 
 
 def lane_of(value):
@@ -102,18 +113,18 @@
 
 def whole_term(green, middle):
     pairs = [stack(part, beside(-part[:, part.shape[1] // 2 :], part[:, : part.shape[1] // 2])) for part in split(middle)]
-    return sandwich(stack(*split(green)), pairs, turn_halves)
+    return sandwich(stack(*split(green)), pairs)
 
 
 def packed_term(green, middle_ref, index, size, extra):
-    width = green.shape[1] // 2
-    share = width // (2 * extra)
+    half = green.shape[1] // 4
+    share = half // extra
     middle = beside(middle_ref[index], middle_ref[size + index // share])
-    pairs = []
-    for part, turned in zip(split(middle), split(-turn_packed(middle, extra))):
-        half = width // 2
-        pairs.append(stack(part[:half], turned[:half], *([part[half:], turned[half:]] * share)))
-    return sandwich(green, pairs, functools.partial(turn_packed, extra=extra))
+
+    def spread(part, turned):
+        return stack(part[:half], turned[:half], *([part[half:], turned[half:]] * share))
+
+    return packed_sandwich(green, split(middle), split(turn_packed(middle, extra)), spread)
 
 
 def matrix_spec(step, offset, width, lead):
@@ -133,12 +144,8 @@
     return pl.BlockSpec(memory_space=pl.ANY)
 
 
-def cost(energies, count, width):
-    return pl.CostEstimate(
-        flops=energies * count * width**2,
-        bytes_accessed=energies * count * width,
-        transcendentals=0,
-    )
+def cost(micros):
+    return pl.CostEstimate(flops=int(micros * 0.3 * 1.15e9), bytes_accessed=int(micros * 0.3 * 3.69e6), transcendentals=0)
 
 
 def own_terms_kernel(step, green, sigma, out):
@@ -155,7 +162,7 @@
         out_specs=matrix_spec(step, 0, width, 0),
         out_shape=jax.ShapeDtypeStruct((energies, 2, width, width), F32),
         compiler_params=params(60),
-        cost_estimate=cost(energies, 1, width),
+        cost_estimate=cost(0.35 * energies),
         name="own_terms",
     )(green, sigma)
 
@@ -183,7 +190,7 @@
             jax.ShapeDtypeStruct((groups, size, 2 * rows, width), F32),
         ],
         compiler_params=params(60),
-        cost_estimate=cost(size, 2, width),
+        cost_estimate=cost(0.75 * size),
         name="side_terms",
     )(total, lower, upper, before, after)
 
@@ -214,7 +221,7 @@
         out_shape=jax.ShapeDtypeStruct(shape, F32),
         input_output_aliases={0: 0} if aliased else {},
         compiler_params=params(),
-        cost_estimate=cost(size, count, width),
+        cost_estimate=cost(0.3 * count * size),
         name="whole_again",
     )(*([result] * aliased), base, *greens, *middles)
 
@@ -254,7 +261,7 @@
         out_shape=jax.ShapeDtypeStruct(shape, F32),
         input_output_aliases={0: 0} if aliased else {},
         compiler_params=params(),
-        cost_estimate=cost(size, count, width),
+        cost_estimate=cost(0.3 * count * size),
         name="packed_again",
     )(*([result] * aliased), *bases, *greens, *middles)
 
@@ -281,9 +288,7 @@
         out_specs=[pl.BlockSpec((step, 2 * width, 2 * width), lambda i: (i, 0, 0))] * count,
         out_shape=[jax.ShapeDtypeStruct((energies, 2 * width, 2 * width), BF16)] * count,
         compiler_params=params(60),
-        cost_estimate=pl.CostEstimate(
-            flops=count * energies * 16 * width**3, bytes_accessed=count * energies * 16 * width**2, transcendentals=0
-        ),
+        cost_estimate=cost(0.13 * count * energies),
         name="pack_green",
     )(places, *greens)
 
@@ -306,9 +311,7 @@
         out_specs=whole,
         out_shape=jax.ShapeDtypeStruct((height // rows, cap, width), F32),
         compiler_params=params(),
-        cost_estimate=pl.CostEstimate(
-            flops=height // rows * 4 * cap * width**2, bytes_accessed=2 * groups * height * width * 4, transcendentals=0
-        ),
+        cost_estimate=cost(1.5),
         name="pack_rows",
     )(chosen, part)
 
@@ -318,12 +321,16 @@
     return both[:size] + (both[size:] + dot(table[:size], value[1]))
 
 
-def forward_kernel(first, groups, rows, tables, weight_ref, *refs):
-    inputs, out = refs[: len(first)], refs[-1]
+def convolve_kernel(first, second, groups, rows, extra, forth, back, weight_ref, final_ref, *refs):
+    inputs, outputs, scratch = refs[: len(first)], refs[len(first) : len(first) + len(second)], refs[len(first) + len(second) :]
     total, double, width = weight_ref.shape
     half = total // 2
+    local = total // groups
+    share = width // (2 * extra) if extra else 0
     weight = weight_ref.reshape(total * double, width)
     arrived = [ref.reshape(groups * size * double, width) for ref, (_, size) in zip(inputs, first)]
+    spans = [(size + size // share) * rows if extra else size * double for _, size in second]
+    leaving = [ref.reshape(groups * span, width) for ref, span in zip(outputs, spans)]
 
     def load(row, p):
         pieces = [
@@ -333,128 +340,92 @@
         ]
         return stack(*pieces)
 
+    def store_whole(row, real, imag):
+        kept = final_ref[pl.ds(row, 1), :] * (1.0 / total)
+        for p, value in enumerate((-imag * kept, real * kept)):
+            for j in range(groups):
+                for c, (begin, size) in enumerate(second):
+                    at = j * local + begin
+                    leaving[c][pl.ds(j * spans[c] + p * rows + row, size, stride=double), :] = value[at : at + size]
+
+    def store_packed(row, real, imag, spare):
+        value = beside(-imag, real) * (1.0 / total)
+        both = dot(stack(*split(value)), final_ref[...])
+        both = both[:total] + both[total:]
+        spare[...] = both[:, width:]
+        quarter = [spare[pl.ds(q, total // share, stride=share), :] for q in range(share)]
+        lane = lane_of(quarter[0]) // (2 * extra)
+        narrow = quarter[0]
+        for q in range(1, share):
+            narrow = jnp.where(lane == q, quarter[q], narrow)
+        for j in range(groups):
+            for c, (begin, size) in enumerate(second):
+                at = j * local + begin
+                leaving[c][pl.ds(j * spans[c] + row, size, stride=rows), :] = both[at : at + size, :width]
+                leaving[c][pl.ds(j * spans[c] + size * rows + row, size // share, stride=rows), :] = narrow[
+                    at // share : (at + size) // share
+                ]
+
     def two_rows(pair, carry):
         at = (2 * pair, 2 * pair + 1)
         values = [[load(row, p) for row in at] for p in (0, 1)]
+        backs = []
         for odd in (0, 1):
             sign = 1.0 - 2.0 * odd
             folded = [beside(*[value[:half] + sign * value[half:] for value in part]) for part in values]
-            spectrum = apply_table(tables[odd], split(stack(*folded)), total)
+            spectrum = apply_table(forth[odd], split(stack(*folded)), total)
             real, imag = spectrum[:half], spectrum[half:]
             weights = [
                 beside(*[weight[pl.ds(odd * double + p * rows + row, half, stride=2 * double), :] for row in at]) for p in (0, 1)
             ]
             weighed = split(stack(real * weights[0] - imag * weights[1], real * weights[1] + imag * weights[0]))
-            for part in (0, 1):
-                out[pair, odd, part] = weighed[part]
+            backs.append(apply_table(back[odd], weighed, total))
+        early, late = backs[0] + backs[1], backs[0] - backs[1]
+        for index, row in enumerate(at):
+            lanes = slice(index * width, (index + 1) * width)
+            real = stack(early[:half, lanes], late[:half, lanes])
+            imag = stack(early[half:, lanes], late[half:, lanes])
+            if extra:
+                store_packed(row, real, imag, scratch[index])
+            else:
+                store_whole(row, real, imag)
         return carry
 
-    lax.fori_loop(0, rows // 2, two_rows, 0)
-
-
-def forward(arrived, weights, first):
+    lax.fori_loop(0, rows // 2, two_rows, 0, unroll=UNROLL)
+
+
+def convolve(arrived, weights, final, first, second, extra):
     groups, _, double, width = arrived[0].shape
     total = weights.shape[0]
-    whole = pl.BlockSpec(memory_space=pltpu.VMEM)
-    shape = (double // 4, 2, 2, total, 2 * width)
-    return pl.pallas_call(
-        functools.partial(forward_kernel, first, groups, double // 2),
-        in_specs=[whole] * (2 + len(first)),
-        out_specs=whole,
-        out_shape=jax.ShapeDtypeStruct(shape, BF16),
-        compiler_params=params(60),
-        cost_estimate=pl.CostEstimate(
-            flops=6 * total * total * double * width, bytes_accessed=3 * total * double * width * 4, transcendentals=0
-        ),
-        name="forward",
-    )(transform_tables(total, None), weights, *arrived)
-
-
-def backward_kernel(size, groups, extra, tables, weighed, final_ref, out_ref, *scratch):
-    pairs, _, _, total, double = weighed.shape
-    width = double // 2
-    rows = 2 * pairs
-    count = groups * size
-    share = width // (2 * extra) if extra else 0
-    span = (size + size // share) * rows if extra else size * 2 * rows
-    out = out_ref.reshape(groups * span, width)
-
-    def store_whole(row, real, imag):
-        kept = final_ref[pl.ds(row, 1), :] * (1.0 / total)
-        for p, value in enumerate((-imag * kept, real * kept)):
-            for j in range(groups):
-                out[pl.ds(j * span + p * rows + row, size, stride=2 * rows), :] = value[j * size : (j + 1) * size]
-
-    def store_packed(row, real, imag):
-        value = beside(-imag, real) * (1.0 / total)
-        both = dot(stack(*split(value)), final_ref[...])
-        both = both[:count] + both[count:]
-        scratch[0][...] = both[:, width:]
-        quarter = [scratch[0][pl.ds(q, count // share, stride=share), :] for q in range(share)]
-        lane = lane_of(quarter[0]) // (2 * extra)
-        narrow = quarter[0]
-        for q in range(1, share):
-            narrow = jnp.where(lane == q, quarter[q], narrow)
-        for j in range(groups):
-            out[pl.ds(j * span + row, size, stride=rows), :] = both[j * size : (j + 1) * size, :width]
-            short = size // share
-            out[pl.ds(j * span + size * rows + row, short, stride=rows), :] = narrow[j * short : (j + 1) * short]
-
-    def two_rows(pair, carry):
-        backs = [apply_table(tables[odd], (weighed[pair, odd, 0], weighed[pair, odd, 1]), count) for odd in (0, 1)]
-        early, late = backs[0] + backs[1], backs[0] - backs[1]
-        for index in (0, 1):
-            lanes = slice(index * width, (index + 1) * width)
-            real = stack(early[: count // 2, lanes], late[: count // 2, lanes])
-            imag = stack(early[count // 2 :, lanes], late[count // 2 :, lanes])
-            (store_packed if extra else store_whole)(2 * pair + index, real, imag)
-        return carry
-
-    lax.fori_loop(0, pairs, two_rows, 0)
-
-
-def backward(weighed, final, begin, size, groups, extra):
-    pairs, _, _, total, double = weighed.shape
-    width = double // 2
-    rows = 2 * pairs
-    local = total // groups
-    chosen = [j * local + begin + l for j in range(groups // 2) for l in range(size)]
+    rows = double // 2
     if extra:
         share = width // (2 * extra)
-        shape = (groups, (size + size // share) * rows, width)
-        scratch = [pltpu.VMEM((groups * size, width), F32)]
+        shapes = [(groups, (size + size // share) * rows, width) for _, size in second]
+        scratch = [pltpu.VMEM((total, width), F32)] * 2
     else:
-        shape = (groups, size, 2 * rows, width)
+        shapes = [(groups, size, double, width) for _, size in second]
         scratch = []
     whole = pl.BlockSpec(memory_space=pltpu.VMEM)
     return pl.pallas_call(
-        functools.partial(backward_kernel, size, groups, extra),
-        in_specs=[whole] * 3,
-        out_specs=whole,
-        out_shape=jax.ShapeDtypeStruct(shape, F32),
+        functools.partial(convolve_kernel, first, second, groups, rows, extra),
+        in_specs=[whole] * (4 + len(first)),
+        out_specs=[whole] * len(second),
+        out_shape=[jax.ShapeDtypeStruct(shape, F32) for shape in shapes],
         scratch_shapes=scratch,
-        compiler_params=params(28),
-        cost_estimate=pl.CostEstimate(
-            flops=6 * total * groups * size * 2 * rows * width,
-            bytes_accessed=(total + groups * size) * 2 * rows * width * 4,
-            transcendentals=0,
-        ),
-        name="backward",
-    )(transform_tables(total, chosen), weighed, final)
-
-
-def transform_tables(total, chosen):
+        compiler_params=params(60),
+        cost_estimate=cost(0.3 * total / groups + 7.0),
+        name="convolve",
+    )(transform_tables(total, False), transform_tables(total, True), weights, final, *arrived)
+
+
+def transform_tables(total, back):
     half = total // 2
     tables = []
     for odd in (0, 1):
         phase = (2 * np.arange(half)[:, None] + odd) * np.arange(half)[None, :] % total
         cosine, sine = np.cos(2.0 * np.pi / total * phase), np.sin(2.0 * np.pi / total * phase)
-        if chosen is None:
-            table = np.block([[cosine, sine], [-sine, cosine]])
-        else:
-            cosine, sine = cosine.T[chosen], sine.T[chosen]
-            table = np.block([[cosine, -sine], [sine, cosine]])
-        tables.append(table.astype(np.float32))
+        table = np.block([[cosine, sine], [-sine, cosine]])
+        tables.append((table.T if back else table).astype(np.float32))
     high = [table.astype(jnp.bfloat16) for table in tables]
     low = [(table - part.astype(np.float32)).astype(jnp.bfloat16) for table, part in zip(tables, high)]
     return jnp.asarray(np.stack([np.concatenate(parts, axis=0) for parts in zip(high, low)]))
@@ -499,13 +470,13 @@
     extra = width // 8
     cap = width // 2 + extra
     first = chunks_of([energies // 4] * 4)
-    second = chunks_of([energies // 2] + [energies // 4] * 2)
+    second = chunks_of([energies // 2] * 2)
 
     mine = pattern[0].astype(F32)
     sent = [sigma_lesser[0, at : at + size].reshape(2 * size * width, width) for at, size in first]
     edge = sent[0].shape[0]
     sent[0] = stack(sent[0], jnp.broadcast_to(mine, (8, width)))
-    own = own_terms(green_diag, sigma_lesser, step)
+    own = own_terms(green_diag, sigma_lesser, 2 * step)
     halos, bases, arrived = [neighbours(part, slabs) for part in sent[:2]], [], []
     patterns = jnp.stack([mine, halos[0][0][edge], halos[0][1][edge]])
     ranks = jnp.cumsum(patterns, axis=1).astype(jnp.int32) - 1
@@ -525,30 +496,31 @@
     chosen = ((ranks[0][None, :] == jnp.arange(cap)[:, None]) & (mine[None, :] > 0)).astype(BF16)
     own_rows = lax.dynamic_slice_in_dim(mine, lax.axis_index("energy") * rows, rows)
     mask = own_rows[:, None] * mine[None, :]
-    weighed = forward(arrived, screened.reshape(total, 2 * rows, width), first)
+    weights = screened.reshape(total, 2 * rows, width)
+    parts = convolve(arrived, weights, places[0], first, second, extra)
 
     def within(begin, size):
         return [base for base, (at, _) in zip(bases, first) if begin <= at < begin + size]
 
-    def packed_rest(weighed):
-        packed, halos = [], []
-        parts = [backward(weighed, places[0], at, size, groups, extra) for at, size in second]
-        for index, part in enumerate(parts):
-            part = exchange(tied(part, packed[-1]) if index else part)
-            packed.append(pack_rows(chosen, part if index else tied(part, parts), rows))
+    def packed_rest(parts, weights, *arrived):
+        packed, halos, partials = [], [], []
+        for index, (part, (at, size)) in enumerate(zip(parts, second)):
+            part = exchange(tied(part, (packed[0], partials[: index - 1])) if index else part)
+            packed.append(pack_rows(chosen, part, rows))
             halos.append(neighbours(packed[-1], slabs))
-        partials = [
-            packed_again(None, within(at, size), packed_greens[:1], [part], at, size, step, (size, 2, width, width), extra)
-            for part, (at, size) in zip(packed, second)
-        ]
+            partials.append(
+                packed_again(
+                    None, within(at, size), packed_greens[:1], packed[-1:], at, size, 2 * step, (size, 2, width, width), extra
+                )
+            )
         result = None
         for partial, halo, (at, size) in zip(partials, halos, second):
-            result = packed_again(result, [partial], packed_greens[1:], halo, at, size, step, green_lower.shape, extra)
+            result = packed_again(result, [partial], packed_greens[1:], halo, at, size, 2 * step, green_lower.shape, extra)
         return result
 
-    def whole_rest(weighed):
+    def whole_rest(parts, weights, *arrived):
         base = jnp.concatenate(bases, axis=0)
-        middles = [exchange(backward(weighed, mask, at, size, groups, 0)) for at, size in second]
+        middles = [exchange(part) for part in convolve(arrived, weights, mask, first, second, 0)]
         halos = [neighbours(part, slabs) for part in middles]
         partials = [
             whole_again(None, base, at, [green_diag], [part], at, step, (size, 2, width, width))
@@ -559,7 +531,7 @@
             result = whole_again(result, partial, 0, [green_lower, green_upper], halo, at, step, green_lower.shape)
         return result
 
-    return lax.cond(fits, packed_rest, whole_rest, weighed)
+    return lax.cond(fits, packed_rest, whole_rest, parts, weights, *arrived)
 
 
 def solution(mesh):

time: 246 us -> 230 us (0.935)
  Pallas kernels: 111 us -> 86.1 us
  blocking collectives: 9.45 us -> 31.4 us
  starting transfers between devices: 63.8 us -> 52 us
    all_to_all x0 -> x1, blocking collectives: none -> 21.7 us  [exchange(): lax.all_to_all(value, 'energy', split_axis=0, concat_axis=0, tiled=True)]
    pallas_call x4 -> x1, Pallas kernels: 31.4 us -> 18.1 us  [convolve(): pl.pallas_call(functools.partial(convolve_kernel, first, second, groups,...]
    pallas_call x6 -> x4, Pallas kernels: 30.2 us -> 20.8 us  [packed_again(): pl.pallas_call(functools.partial(packed_again_kernel, step, places, count...]
    all_to_all x7 -> x5, waiting for transfers between devices: 28.6 us -> 22.7 us  [exchange(): lax.all_to_all(value, 'energy', split_axis=0, concat_axis=0, tiled=True)]
    ppermute x14 -> x12, starting transfers between devices: 38.2 us -> 32.3 us  [neighbours(): return (lax.ppermute(value, 'slab', up), lax.ppermute(value, 'slab', down))]
    all_to_all x7 -> x5, starting transfers between devices: 25.5 us -> 19.7 us  [exchange(): lax.all_to_all(value, 'energy', split_axis=0, concat_axis=0, tiled=True)]
    ppermute x14 -> x12, waiting for transfers between devices: 21.7 us -> 27.2 us  [neighbours(): return (lax.ppermute(value, 'slab', up), lax.ppermute(value, 'slab', down))]
  transfers between devices with their start and end apart: 21 -> 17, of which waited for: 10 -> 10; matrix products, arithmetic and copies ran while one was open for 1% -> 2% of each run, Pallas kernels for 35% -> 27%
where the time goes in v3:
time: 230 us; the launch traced here: 229 us
  Pallas kernels  86.1 us (37%)
  starting transfers between devices  52 us (23%)
  waiting for transfers between devices  49.9 us (22%)
  blocking collectives  31.4 us (14%)
  local copies, waits for them, and re-layouts  5 us (2%)
  other arithmetic  3.71 us (2%)
    ppermute x12, starting transfers between devices, neighbours(): return (lax.ppermute(value, 'slab', up), lax.ppermute(value, 'slab', down))  32.3 us
    ppermute x12, waiting for transfers between devices, neighbours(): return (lax.ppermute(value, 'slab', up), lax.ppermute(value, 'slab', down))  27.2 us
    pallas_call x4, Pallas kernels, side_terms(): pl.pallas_call(functools.partial(side_terms_kernel, step), grid=(size //...  24.3 us
    all_to_all x5, waiting for transfers between devices, exchange(): lax.all_to_all(value, 'energy', split_axis=0, concat_axis=0, tiled=True)  22.7 us
    all_to_all x1, blocking collectives, exchange(): lax.all_to_all(value, 'energy', split_axis=0, concat_axis=0, tiled=True)  21.7 us
    pallas_call x4, Pallas kernels, packed_again(): pl.pallas_call(functools.partial(packed_again_kernel, step, places, count...  20.8 us
    all_to_all x5, starting transfers between devices, exchange(): lax.all_to_all(value, 'energy', split_axis=0, concat_axis=0, tiled=True)  19.7 us
    pallas_call x1, Pallas kernels, convolve(): pl.pallas_call(functools.partial(convolve_kernel, first, second, groups,...  18.1 us
  transfers between devices with their start and end apart: 17, of which 10 were waited for; matrix products, arithmetic and copies ran while one was open for 2% of the time, Pallas kernels for 27%

profile of v3, /device:TPU:0, one launch (start us, length us, event | category | flops | bytes accessed | tf_op | source)
XLA Modules:
  0.0 229.0 jit_solution(8695986163625928057)
XLA Ops:
  0.0 3.9 %fusion.13 = (f32[1,8,2,128,128]{4,3,2,1,0:T(8,128)}, f32[1,8,2,128,128]{4,3,2,1,0:T(8,128)}, f32[1,8,2,128,128]{4,3,2,1,0:T(8,128)}, f32[1,8,2,128,128]{4,3,2,1,0:T(8,128)S(1)}) fusion(f32[1,32,2,128,128]{4,3,2,1,0:T(8,128)} %sigma.1), kind=kLoop, calls=%fused_computation.60 | loop fusion | bytes 8388608 | tf_op jit(solution)/shard_map/slice | solution.py:476
  4.0 5.0 %collective-permute-start.12 = (f32[2056,128]{1,0:T(8,128)S(1)}, f32[2056,128]{1,0:T(8,128)S(1)}, u32[]{:S(2)}, u32[]{:S(2)}) collective-permute-start(f32[2056,128]{1,0:T(8,128)S(1)} %pad_maximum_fusion), channel_id=1, source_target_pairs={{0,1},{1,2},{2,3},{4,5},{5,6},{6,7},{8,9},{9,10},{10,11},{12,13},{... | collective-permute-start | bytes 3158024 | tf_op jit(solution)/shard_map/ppermute | solution.py:437
  10.3 5.5 %collective-permute-start.8 = (f32[2048,128]{1,0:T(8,128)}, f32[2048,128]{1,0:T(8,128)}, u32[]{:S(2)}, u32[]{:S(2)}) collective-permute-start(f32[2048,128]{1,0:T(8,128)} %bitcast.1), channel_id=1, source_target_pairs={{0,1},{1,2},{2,3},{4,5},{5,6},{6,7},{8,9},{9,10},{10,11},{12,13},{... | collective-permute-start | bytes 3145736 | tf_op jit(solution)/shard_map/ppermute | solution.py:437
  17.2 9.4 %own_terms.1.total = f32[32,2,128,128]{3,2,1,0:T(8,128)} custom-call(f32[1,32,2,128,128]{4,3,2,1,0:T(8,128)} %refs_0_.1, f32[1,32,2,128,128]{4,3,2,1,0:T(8,128)} %sigma.1), custom_call_target="tpu_custom_call" | custom-call | flops 3864000000 | bytes 12398400 | tf_op jit(solution)/shard_map/own_terms/pallas_call | solution.py:158
  26.6 5.9 %collective-permute-done.12.before = f32[2056,128]{1,0:T(8,128)S(1)} collective-permute-done((f32[2056,128]{1,0:T(8,128)S(1)}, f32[2056,128]{1,0:T(8,128)S(1)}, u32[]{:S(2)}, u32[]{:S(2)}) %collective-permute-start.12) | collective-permute-done | bytes 1052704 | tf_op jit(solution)/shard_map/ppermute | solution.py:437
  32.6 4.5 %collective-permute-done.13.after = f32[2056,128]{1,0:T(8,128)S(1)} collective-permute-done((f32[2056,128]{1,0:T(8,128)S(1)}, f32[2056,128]{1,0:T(8,128)S(1)}, u32[]{:S(2)}, u32[]{:S(2)}) %collective-permute-start.13) | collective-permute-done | bytes 1052704 | tf_op jit(solution)/shard_map/ppermute | solution.py:437
  37.1 4.4 %collective-permute-start.14 = (f32[2048,128]{1,0:T(8,128)}, f32[2048,128]{1,0:T(8,128)}, u32[]{:S(2)}, u32[]{:S(2)}) collective-permute-start(f32[2048,128]{1,0:T(8,128)} %bitcast.33), channel_id=1, source_target_pairs={{0,1},{1,2},{2,3},{4,5},{5,6},{6,7},{8,9},{9,10},{10,11},{12,13},{... | collective-permute-start | bytes 3145736 | tf_op jit(solution)/shard_map/ppermute | solution.py:437
  43.2 5.8 %side_terms.4 = (f32[8,2,128,128]{3,2,1,0:T(8,128)S(1)}, f32[8,8,32,128]{3,2,1,0:T(8,128)}) custom-call(f32[32,2,128,128]{3,2,1,0:T(8,128)} %own_terms.1.total, f32[1,32,2,128,128]{4,3,2,1,0:T(8,128)} %lower.7, f32[1,32,2,128,128]{4,3,2,1,0:T(8,128)} %upper.7, f32[2056,128]{1,0:T(8,128)} %copy-done.12, f32[2056,128]{1,0:T(8,128)} %copy-done.13), custom_call_target="tpu_custom_call" | custom-call | flops 2070000000 | bytes 6641999 | tf_op jit(solution)/shard_map/side_terms/pallas_call | solution.py:183
  49.0 3.7 %all-to-all-start.4 = ((f32[8,8,32,128]{3,2,1,0:T(8,128)}), f32[8,8,32,128]{3,2,1,0:T(8,128)S(1)}, u32[]{:S(2)}, u32[]{:S(2)}) async-start(f32[8,8,32,128]{3,2,1,0:T(8,128)} %get-tuple-element.126), calls=%async_computation.4 | async-start | bytes 2097152 | tf_op jit(solution)/shard_map/all_to_all | solution.py:441
  54.6 12.2 %pack_green.1 = (bf16[32,256,256]{2,1,0:T(8,128)(2,1)}, bf16[32,256,256]{2,1,0:T(8,128)(2,1)}, bf16[32,256,256]{2,1,0:T(8,128)(2,1)}) custom-call(bf16[3,256,256]{2,1,0:T(8,128)(2,1)} %add_convert_fusion.place, f32[1,32,2,128,128]{4,3,2,1,0:T(8,128)} %refs_0_.1, f32[1,32,2,128,128]{4,3,2,1,0:T(8,128)} %lower.7, f32[1,32,2,128,128]{4,3,2,1,0:T(8,128)} %upper.7), custom_call_target="tpu_custom_call" | custom-call | flops 4305600000 | bytes 13815360 | tf_op jit(solution)/shard_map/pack_green/pallas_call | solution.py:284
  68.2 6.4 %side_terms.5 = (f32[8,2,128,128]{3,2,1,0:T(8,128)}, f32[8,8,32,128]{3,2,1,0:T(8,128)}) custom-call(f32[32,2,128,128]{3,2,1,0:T(8,128)} %own_terms.1.total, f32[1,32,2,128,128]{4,3,2,1,0:T(8,128)} %lower.7, f32[1,32,2,128,128]{4,3,2,1,0:T(8,128)} %upper.7, f32[2048,128]{1,0:T(8,128)} %collective-permute-done.8.before, f32[2048,128]{1,0:T(8,128)} %collective-permute-done.9.after), custom_call_target="tpu_custom_call" | custom-call | flops 2070000000 | bytes 6641999 | tf_op jit(solution)/shard_map/side_terms/pallas_call | solution.py:183
  74.6 4.2 %all-to-all-start.5 = ((f32[8,8,32,128]{3,2,1,0:T(8,128)}), f32[8,8,32,128]{3,2,1,0:T(8,128)}, u32[]{:S(2)}, u32[]{:S(2)}) async-start(f32[8,8,32,128]{3,2,1,0:T(8,128)} %get-tuple-element.132), calls=%async_computation.5 | async-start | bytes 2097152 | tf_op jit(solution)/shard_map/all_to_all | solution.py:441
  78.8 4.6 %collective-permute-start.10 = (f32[2048,128]{1,0:T(8,128)}, f32[2048,128]{1,0:T(8,128)S(1)}, u32[]{:S(2)}, u32[]{:S(2)}) collective-permute-start(f32[2048,128]{1,0:T(8,128)} %bitcast), channel_id=1, source_target_pairs={{0,1},{1,2},{2,3},{4,5},{5,6},{6,7},{8,9},{9,10},{10,11},{12,13},{... | collective-permute-start | bytes 3145736 | tf_op jit(solution)/shard_map/ppermute | solution.py:437
  84.8 6.1 %side_terms.7 = (f32[8,2,128,128]{3,2,1,0:T(8,128)}, f32[8,8,32,128]{3,2,1,0:T(8,128)}) custom-call(f32[32,2,128,128]{3,2,1,0:T(8,128)} %own_terms.1.total, f32[1,32,2,128,128]{4,3,2,1,0:T(8,128)} %lower.7, f32[1,32,2,128,128]{4,3,2,1,0:T(8,128)} %upper.7, f32[2048,128]{1,0:T(8,128)} %collective-permute-done.14.before, f32[2048,128]{1,0:T(8,128)} %collective-permute-done.15.after), custom_call_target="tpu_custom_call" | custom-call | flops 2070000000 | bytes 6641999 | tf_op jit(solution)/shard_map/side_terms/pallas_call | solution.py:183
  90.8 3.4 %all-to-all-done.5.refs_1_ = f32[8,8,32,128]{3,2,1,0:T(8,128)} async-done(((f32[8,8,32,128]{3,2,1,0:T(8,128)}), f32[8,8,32,128]{3,2,1,0:T(8,128)}, u32[]{:S(2)}, u32[]{:S(2)}) %all-to-all-start.5) | async-done | bytes 1048608 | tf_op jit(solution)/shard_map/all_to_all | solution.py:441
  94.2 4.2 %all-to-all-start.6 = ((f32[8,8,32,128]{3,2,1,0:T(8,128)}), f32[8,8,32,128]{3,2,1,0:T(8,128)}, u32[]{:S(2)}, u32[]{:S(2)}) async-start(f32[8,8,32,128]{3,2,1,0:T(8,128)} %get-tuple-element.143), calls=%async_computation.6 | async-start | bytes 2097152 | tf_op jit(solution)/shard_map/all_to_all | solution.py:441
  98.5 8.1 %collective-permute-done.10.before = f32[2048,128]{1,0:T(8,128)S(1)} collective-permute-done((f32[2048,128]{1,0:T(8,128)}, f32[2048,128]{1,0:T(8,128)S(1)}, u32[]{:S(2)}, u32[]{:S(2)}) %collective-permute-start.10) | collective-permute-done | bytes 1048608 | tf_op jit(solution)/shard_map/ppermute | solution.py:437
  106.6 4.1 %collective-permute-done.11.after = f32[2048,128]{1,0:T(8,128)S(1)} collective-permute-done((f32[2048,128]{1,0:T(8,128)}, f32[2048,128]{1,0:T(8,128)S(1)}, u32[]{:S(2)}, u32[]{:S(2)}) %collective-permute-start.11) | collective-permute-done | bytes 1048608 | tf_op jit(solution)/shard_map/ppermute | solution.py:437
  111.7 6.0 %side_terms.6 = (f32[8,2,128,128]{3,2,1,0:T(8,128)}, f32[8,8,32,128]{3,2,1,0:T(8,128)}) custom-call(f32[32,2,128,128]{3,2,1,0:T(8,128)} %own_terms.1.total, f32[1,32,2,128,128]{4,3,2,1,0:T(8,128)} %lower.7, f32[1,32,2,128,128]{4,3,2,1,0:T(8,128)} %upper.7, f32[2048,128]{1,0:T(8,128)} %copy-done.14, f32[2048,128]{1,0:T(8,128)} %copy-done.15), custom_call_target="tpu_custom_call" | custom-call | flops 2070000000 | bytes 6641999 | tf_op jit(solution)/shard_map/side_terms/pallas_call | solution.py:183
  117.7 3.9 %all-to-all-start.7 = ((f32[8,8,32,128]{3,2,1,0:T(8,128)}), f32[8,8,32,128]{3,2,1,0:T(8,128)S(1)}, u32[]{:S(2)}, u32[]{:S(2)}) async-start(f32[8,8,32,128]{3,2,1,0:T(8,128)} %get-tuple-element.144), calls=%async_computation.7 | async-start | bytes 2097152 | tf_op jit(solution)/shard_map/all_to_all | solution.py:441
  123.1 9.7 %pmax.7 = f32[]{:T(128)} all-reduce(f32[]{:T(128)} %convert_reduce_fusion), channel_id=1, replica_groups=mesh['energy'=8,'slab'=4] {'slab'}, use_global_device_ids=true, to_apply=%region_2.3 | all-reduce | flops 1 | bytes 8 | tf_op jit(solution)/shard_map/pmax | solution.py:495
  133.4 3.6 %all-to-all-done.7.refs_3_ = f32[8,8,32,128]{3,2,1,0:T(8,128)S(1)} async-done(((f32[8,8,32,128]{3,2,1,0:T(8,128)}), f32[8,8,32,128]{3,2,1,0:T(8,128)S(1)}, u32[]{:S(2)}, u32[]{:S(2)}) %all-to-all-start.7) | async-done | bytes 1048608 | tf_op jit(solution)/shard_map/all_to_all | solution.py:441
  137.0 18.1 %convolve.3 = (f32[8,320,128]{2,1,0:T(8,128)}, f32[8,320,128]{2,1,0:T(8,128)}) custom-call(bf16[2,512,256]{2,1,0:T(8,128)(2,1)} %constant.137.clone.forth, bf16[2,512,256]{2,1,0:T(8,128)(2,1)} %constant.138.clone.back, f32[256,32,128]{2,1,0:T(8,128)} %bitcast.35, bf16[256,256]{1,0:T(8,128)(2,1)} %and_convert_fusion.final_ref, f32[8,8,32,128]{3,2,1,0:T(8,128)} %copy-done.16, ...), custom_call_target="tpu_custom_call" | custom-call | flops 5727000064 | bytes 18376200 | tf_op jit(solution)/shard_map/convolve/pallas_call | solution.py:409
  155.2 73.9 %conditional.1 = (f32[1,32,2,128,128]{4,3,2,1,0:T(8,128)}) conditional(s32[]{:T(128)} %convert_element_type.39, (f32[8,2,128,128]{3,2,1,0:T(8,128)S(1)}, f32[8,2,128,128]{3,2,1,0:T(8,128)}, f32[8,2,128,128]{3,2,1,0:T(8,128)}, f32[8,2,128,128]{3,2,1,0:T(8,128)}, s32[]{:T(128)}, /*index=5*/f32[128]{0:T(128)S(1)}, bf16[2,512,256]{2,1,0:T(8,128)(2,1)}, ...), branch_computations={%region_3.4_spmd, %region_4.5_spmd} | conditional | flops 15663002624 | bytes 169804768 | solution.py:534
  155.2 21.7 %all_to_all.37.part = f32[8,320,128]{2,1,0:T(8,128)S(1)} all-to-all(f32[8,320,128]{2,1,0:T(8,128)} %get-tuple-element.96), channel_id=1, replica_groups=mesh['energy'=8,'slab'=4] {'energy'}, dimensions={0} | all-to-all | bytes 2621440 | tf_op jit(solution)/shard_map/cond/branch_1_fun/all_to_all | solution.py:441
  177.4 3.6 %all-to-all-start.1 = ((f32[8,320,128]{2,1,0:T(8,128)}), f32[8,320,128]{2,1,0:T(8,128)S(1)}, u32[]{:S(2)}, u32[]{:S(2)}) async-start(f32[8,320,128]{2,1,0:T(8,128)} %get-tuple-element.102), calls=%async_computation.1 | async-start | bytes 2621440 | tf_op jit(solution)/shard_map/cond/branch_1_fun/all_to_all | solution.py:441
  184.8 14.3 %all-to-all-done.1.part = f32[8,320,128]{2,1,0:T(8,128)S(1)} async-done(((f32[8,320,128]{2,1,0:T(8,128)}), f32[8,320,128]{2,1,0:T(8,128)S(1)}, u32[]{:S(2)}, u32[]{:S(2)}) %all-to-all-start.1) | async-done | bytes 1310752 | tf_op jit(solution)/shard_map/cond/branch_1_fun/all_to_all | solution.py:441
  203.5 4.9 %packed_again.4.refs_0_ = f32[16,2,128,128]{3,2,1,0:T(8,128)S(1)} custom-call(f32[8,2,128,128]{3,2,1,0:T(8,128)} %copy-done.7, f32[8,2,128,128]{3,2,1,0:T(8,128)} %get-tuple-element.93.refs_1_, bf16[32,256,256]{2,1,0:T(8,128)(2,1)} %get-tuple-element.94.refs_2_, f32[20,80,128]{2,1,0:T(8,128)S(1)} %pack_rows.2.refs_3_), custom_call_target="tpu_custom_call" | custom-call | flops 1656000000 | bytes 5313600 | tf_op jit(solution)/shard_map/cond/branch_1_fun/packed_again/pallas_call | solution.py:253
  208.6 7.1 %packed_again.5.refs_0_ = f32[1,32,2,128,128]{4,3,2,1,0:T(8,128)} custom-call(f32[16,2,128,128]{3,2,1,0:T(8,128)S(1)} %packed_again.4.refs_0_, bf16[32,256,256]{2,1,0:T(8,128)(2,1)S(1)} %copy-done.5, bf16[32,256,256]{2,1,0:T(8,128)(2,1)S(1)} %copy-done.6, f32[20,80,128]{2,1,0:T(8,128)S(1)} %collective-permute-done.refs_3_, ...), custom_call_target="tpu_custom_call" | custom-call | flops 3312000000 | bytes 10627200 | tf_op jit(solution)/shard_map/cond/branch_1_fun/packed_again/pallas_call | solution.py:253
  215.7 2.9 %packed_again.6.refs_1_ = f32[16,2,128,128]{3,2,1,0:T(8,128)S(1)} custom-call(f32[8,2,128,128]{3,2,1,0:T(8,128)S(1)} %copy-done.9, f32[8,2,128,128]{3,2,1,0:T(8,128)S(1)} %copy-done.11, bf16[32,256,256]{2,1,0:T(8,128)(2,1)S(1)} %copy-done.4, f32[20,80,128]{2,1,0:T(8,128)S(1)} %pack_rows.3.refs_3_), custom_call_target="tpu_custom_call" | custom-call | flops 1656000000 | bytes 5313600 | tf_op jit(solution)/shard_map/cond/branch_1_fun/packed_again/pallas_call | solution.py:253
  219.0 4.2 %collective-permute-done.3.refs_5_ = f32[20,80,128]{2,1,0:T(8,128)S(1)} collective-permute-done((f32[20,80,128]{2,1,0:T(8,128)S(1)}, f32[20,80,128]{2,1,0:T(8,128)S(1)}, u32[]{:S(2)}, u32[]{:S(2)}) %collective-permute-start.3) | collective-permute-done | bytes 819232 | tf_op jit(solution)/shard_map/cond/branch_1_fun/ppermute | solution.py:437
  223.2 5.8 %packed_again.7 = f32[1,32,2,128,128]{4,3,2,1,0:T(8,128)} custom-call(f32[1,32,2,128,128]{4,3,2,1,0:T(8,128)} %packed_again.5.refs_0_, f32[16,2,128,128]{3,2,1,0:T(8,128)S(1)} %packed_again.6.refs_1_, bf16[32,256,256]{2,1,0:T(8,128)(2,1)S(1)} %copy-done.5, bf16[32,256,256]{2,1,0:T(8,128)(2,1)S(1)} %copy-done.6, ...), custom_call_target="tpu_custom_call", output_to_operand_aliasing={{}: (0, {})} | custom-call | flops 3312000000 | bytes 10627200 | tf_op jit(solution)/shard_map/cond/branch_1_fun/packed_again/pallas_call | solution.py:253
  (70 shorter events, 20.4 us)
Async XLA Ops:
  0.0 3.9 %copy-start.18 = (s32[1,128]{1,0:T(1,128)S(1)}, s32[1,128]{1,0:T(1,128)}, u32[]{:S(2)}) copy-start(s32[1,128]{1,0:T(1,128)} %param.17) | copy-start | bytes 1540
  4.0 28.6 %collective-permute-start.12 = (f32[2056,128]{1,0:T(8,128)S(1)}, f32[2056,128]{1,0:T(8,128)S(1)}, u32[]{:S(2)}, u32[]{:S(2)}) collective-permute-start(f32[2056,128]{1,0:T(8,128)S(1)} %pad_maximum_fusion), channel_id=1, source_target_pairs={{0,1},{1,2},{2,3},{4,5},{5,6},{6,7},{8,9},{9,10},{10,11},{12,13},{... | collective-permute-start | bytes 3158024 | tf_op jit(solution)/shard_map/ppermute | solution.py:437
  9.0 28.1 %collective-permute-start.13 = (f32[2056,128]{1,0:T(8,128)S(1)}, f32[2056,128]{1,0:T(8,128)S(1)}, u32[]{:S(2)}, u32[]{:S(2)}) collective-permute-start(f32[2056,128]{1,0:T(8,128)S(1)} %pad_maximum_fusion), channel_id=1, source_target_pairs={{1,0},{2,1},{3,2},{5,4},{6,5},{7,6},{9,8},{10,9},{11,10},{13,12},{... | collective-permute-start | bytes 3158024 | tf_op jit(solution)/shard_map/ppermute | solution.py:437
  10.3 56.5 %collective-permute-start.8 = (f32[2048,128]{1,0:T(8,128)}, f32[2048,128]{1,0:T(8,128)}, u32[]{:S(2)}, u32[]{:S(2)}) collective-permute-start(f32[2048,128]{1,0:T(8,128)} %bitcast.1), channel_id=1, source_target_pairs={{0,1},{1,2},{2,3},{4,5},{5,6},{6,7},{8,9},{9,10},{10,11},{12,13},{... | collective-permute-start | bytes 3145736 | tf_op jit(solution)/shard_map/ppermute | solution.py:437
  15.8 51.0 %collective-permute-start.9 = (f32[2048,128]{1,0:T(8,128)}, f32[2048,128]{1,0:T(8,128)}, u32[]{:S(2)}, u32[]{:S(2)}) collective-permute-start(f32[2048,128]{1,0:T(8,128)} %bitcast.1), channel_id=1, source_target_pairs={{1,0},{2,1},{3,2},{5,4},{6,5},{7,6},{9,8},{10,9},{11,10},{13,12},{... | collective-permute-start | bytes 3145736 | tf_op jit(solution)/shard_map/ppermute | solution.py:437
  32.6 10.6 %copy-start.12 = (f32[2056,128]{1,0:T(8,128)}, f32[2056,128]{1,0:T(8,128)S(1)}, u32[]{:S(2)}) copy-start(f32[2056,128]{1,0:T(8,128)S(1)} %collective-permute-done.12.before) | copy-start | bytes 3158020
  37.1 6.1 %copy-start.13 = (f32[2056,128]{1,0:T(8,128)}, f32[2056,128]{1,0:T(8,128)S(1)}, u32[]{:S(2)}) copy-start(f32[2056,128]{1,0:T(8,128)S(1)} %collective-permute-done.13.after) | copy-start | bytes 3158020
  37.1 47.7 %collective-permute-start.14 = (f32[2048,128]{1,0:T(8,128)}, f32[2048,128]{1,0:T(8,128)}, u32[]{:S(2)}, u32[]{:S(2)}) collective-permute-start(f32[2048,128]{1,0:T(8,128)} %bitcast.33), channel_id=1, source_target_pairs={{0,1},{1,2},{2,3},{4,5},{5,6},{6,7},{8,9},{9,10},{10,11},{12,13},{... | collective-permute-start | bytes 3145736 | tf_op jit(solution)/shard_map/ppermute | solution.py:437
  41.5 43.3 %collective-permute-start.15 = (f32[2048,128]{1,0:T(8,128)}, f32[2048,128]{1,0:T(8,128)}, u32[]{:S(2)}, u32[]{:S(2)}) collective-permute-start(f32[2048,128]{1,0:T(8,128)} %bitcast.34), channel_id=1, source_target_pairs={{1,0},{2,1},{3,2},{5,4},{6,5},{7,6},{9,8},{10,9},{11,10},{13,12},{... | collective-permute-start | bytes 3145736 | tf_op jit(solution)/shard_map/ppermute | solution.py:437
  49.0 19.1 %all-to-all-start.4 = ((f32[8,8,32,128]{3,2,1,0:T(8,128)}), f32[8,8,32,128]{3,2,1,0:T(8,128)S(1)}, u32[]{:S(2)}, u32[]{:S(2)}) async-start(f32[8,8,32,128]{3,2,1,0:T(8,128)} %get-tuple-element.126), calls=%async_computation.4 | async-start | bytes 2097152 | tf_op jit(solution)/shard_map/all_to_all | solution.py:441
  68.1 6.4 %copy-start.16 = (f32[8,8,32,128]{3,2,1,0:T(8,128)}, f32[8,8,32,128]{3,2,1,0:T(8,128)S(1)}, u32[]{:S(2)}) copy-start(f32[8,8,32,128]{3,2,1,0:T(8,128)S(1)} %all-to-all-done.4.refs_0_) | copy-start | bytes 3145732
  74.6 19.7 %all-to-all-start.5 = ((f32[8,8,32,128]{3,2,1,0:T(8,128)}), f32[8,8,32,128]{3,2,1,0:T(8,128)}, u32[]{:S(2)}, u32[]{:S(2)}) async-start(f32[8,8,32,128]{3,2,1,0:T(8,128)} %get-tuple-element.132), calls=%async_computation.5 | async-start | bytes 2097152 | tf_op jit(solution)/shard_map/all_to_all | solution.py:441
  78.8 27.8 %collective-permute-start.10 = (f32[2048,128]{1,0:T(8,128)}, f32[2048,128]{1,0:T(8,128)S(1)}, u32[]{:S(2)}, u32[]{:S(2)}) collective-permute-start(f32[2048,128]{1,0:T(8,128)} %bitcast), channel_id=1, source_target_pairs={{0,1},{1,2},{2,3},{4,5},{5,6},{6,7},{8,9},{9,10},{10,11},{12,13},{... | collective-permute-start | bytes 3145736 | tf_op jit(solution)/shard_map/ppermute | solution.py:437
  83.5 27.2 %collective-permute-start.11 = (f32[2048,128]{1,0:T(8,128)}, f32[2048,128]{1,0:T(8,128)S(1)}, u32[]{:S(2)}, u32[]{:S(2)}) collective-permute-start(f32[2048,128]{1,0:T(8,128)} %bitcast), channel_id=1, source_target_pairs={{1,0},{2,1},{3,2},{5,4},{6,5},{7,6},{9,8},{10,9},{11,10},{13,12},{... | collective-permute-start | bytes 3145736 | tf_op jit(solution)/shard_map/ppermute | solution.py:437
  94.2 23.5 %all-to-all-start.6 = ((f32[8,8,32,128]{3,2,1,0:T(8,128)}), f32[8,8,32,128]{3,2,1,0:T(8,128)}, u32[]{:S(2)}, u32[]{:S(2)}) async-start(f32[8,8,32,128]{3,2,1,0:T(8,128)} %get-tuple-element.143), calls=%async_computation.6 | async-start | bytes 2097152 | tf_op jit(solution)/shard_map/all_to_all | solution.py:441
  106.6 4.1 %copy-start.14 = (f32[2048,128]{1,0:T(8,128)}, f32[2048,128]{1,0:T(8,128)S(1)}, u32[]{:S(2)}) copy-start(f32[2048,128]{1,0:T(8,128)S(1)} %collective-permute-done.10.before) | copy-start | bytes 3145732
  110.7 1.0 copy-start.15
  117.7 19.3 %all-to-all-start.7 = ((f32[8,8,32,128]{3,2,1,0:T(8,128)}), f32[8,8,32,128]{3,2,1,0:T(8,128)S(1)}, u32[]{:S(2)}, u32[]{:S(2)}) async-start(f32[8,8,32,128]{3,2,1,0:T(8,128)} %get-tuple-element.144), calls=%async_computation.7 | async-start | bytes 2097152 | tf_op jit(solution)/shard_map/all_to_all | solution.py:441
  137.0 18.1 %copy-start.17 = (f32[8,8,32,128]{3,2,1,0:T(8,128)S(1)}, f32[8,8,32,128]{3,2,1,0:T(8,128)}, u32[]{:S(2)}) copy-start(f32[8,8,32,128]{3,2,1,0:T(8,128)} %copy-done.16) | copy-start | bytes 3145732
  155.2 22.2 %copy-start.7 = (f32[8,2,128,128]{3,2,1,0:T(8,128)}, f32[8,2,128,128]{3,2,1,0:T(8,128)S(1)}, u32[]{:S(2)}) copy-start(f32[8,2,128,128]{3,2,1,0:T(8,128)S(1)} %get-tuple-element.92.refs_0_) | copy-start | bytes 3145732 | tf_op jit(solution)/shard_map/cond
  177.4 21.7 %all-to-all-start.1 = ((f32[8,320,128]{2,1,0:T(8,128)}), f32[8,320,128]{2,1,0:T(8,128)S(1)}, u32[]{:S(2)}, u32[]{:S(2)}) async-start(f32[8,320,128]{2,1,0:T(8,128)} %get-tuple-element.102), calls=%async_computation.1 | async-start | bytes 2621440 | tf_op jit(solution)/shard_map/cond/branch_1_fun/all_to_all | solution.py:441
  181.0 27.5 %collective-permute-start = (f32[20,80,128]{2,1,0:T(8,128)S(1)}, f32[20,80,128]{2,1,0:T(8,128)S(1)}, u32[]{:S(2)}, u32[]{:S(2)}) collective-permute-start(f32[20,80,128]{2,1,0:T(8,128)S(1)} %pack_rows.2.refs_3_), channel_id=1, source_target_pairs={{0,1},{1,2},{2,3},{4,5},{5,6},{6,7},{8,9},{9,10},{10,11},{12,13},{... | collective-permute-start | bytes 2457608 | tf_op jit(solution)/shard_map/cond/branch_1_fun/ppermute | solution.py:437
  183.5 25.0 %collective-permute-start.1 = (f32[20,80,128]{2,1,0:T(8,128)S(1)}, f32[20,80,128]{2,1,0:T(8,128)}, u32[]{:S(2)}, u32[]{:S(2)}) collective-permute-start(f32[20,80,128]{2,1,0:T(8,128)S(1)} %pack_rows.2.refs_3_), channel_id=1, source_target_pairs={{1,0},{2,1},{3,2},{5,4},{6,5},{7,6},{9,8},{10,9},{11,10},{13,12},{... | collective-permute-start | bytes 2457608 | tf_op jit(solution)/shard_map/cond/branch_1_fun/ppermute | solution.py:437
  199.7 19.3 %collective-permute-start.2 = (f32[20,80,128]{2,1,0:T(8,128)S(1)}, f32[20,80,128]{2,1,0:T(8,128)S(1)}, u32[]{:S(2)}, u32[]{:S(2)}) collective-permute-start(f32[20,80,128]{2,1,0:T(8,128)S(1)} %pack_rows.3.refs_3_), channel_id=1, source_target_pairs={{0,1},{1,2},{2,3},{4,5},{5,6},{6,7},{8,9},{9,10},{10,11},{12,13},{... | collective-permute-start | bytes 2457608 | tf_op jit(solution)/shard_map/cond/branch_1_fun/ppermute | solution.py:437
  202.2 21.0 %collective-permute-start.3 = (f32[20,80,128]{2,1,0:T(8,128)S(1)}, f32[20,80,128]{2,1,0:T(8,128)S(1)}, u32[]{:S(2)}, u32[]{:S(2)}) collective-permute-start(f32[20,80,128]{2,1,0:T(8,128)S(1)} %pack_rows.3.refs_3_), channel_id=1, source_target_pairs={{1,0},{2,1},{3,2},{5,4},{6,5},{7,6},{9,8},{10,9},{11,10},{13,12},{... | collective-permute-start | bytes 2457608 | tf_op jit(solution)/shard_map/cond/branch_1_fun/ppermute | solution.py:437
  203.5 5.0 %copy-start.5 = (bf16[32,256,256]{2,1,0:T(8,128)(2,1)S(1)}, bf16[32,256,256]{2,1,0:T(8,128)(2,1)}, u32[]{:S(2)}) copy-start(bf16[32,256,256]{2,1,0:T(8,128)(2,1)} %get-tuple-element.97.refs_1_.refs_2_) | copy-start | bytes 12582916 | tf_op jit(solution)/shard_map/cond
  203.5 5.0 %copy-start.6 = (bf16[32,256,256]{2,1,0:T(8,128)(2,1)S(1)}, bf16[32,256,256]{2,1,0:T(8,128)(2,1)}, u32[]{:S(2)}) copy-start(bf16[32,256,256]{2,1,0:T(8,128)(2,1)} %get-tuple-element.98.refs_2_.refs_3_) | copy-start | bytes 12582916 | tf_op jit(solution)/shard_map/cond
  208.5 7.2 %copy-start.4 = (bf16[32,256,256]{2,1,0:T(8,128)(2,1)S(1)}, bf16[32,256,256]{2,1,0:T(8,128)(2,1)}, u32[]{:S(2)}) copy-start(bf16[32,256,256]{2,1,0:T(8,128)(2,1)} %get-tuple-element.94.refs_2_) | copy-start | bytes 12582916 | tf_op jit(solution)/shard_map/cond
  208.5 7.2 %copy-start.9 = (f32[8,2,128,128]{3,2,1,0:T(8,128)S(1)}, f32[8,2,128,128]{3,2,1,0:T(8,128)}, u32[]{:S(2)}) copy-start(f32[8,2,128,128]{3,2,1,0:T(8,128)} %get-tuple-element.99.refs_0_) | copy-start | bytes 3145732 | tf_op jit(solution)/shard_map/cond
  208.6 7.2 %copy-start.11 = (f32[8,2,128,128]{3,2,1,0:T(8,128)S(1)}, f32[8,2,128,128]{3,2,1,0:T(8,128)}, u32[]{:S(2)}) copy-start(f32[8,2,128,128]{3,2,1,0:T(8,128)} %get-tuple-element.100.refs_1_) | copy-start | bytes 3145732 | tf_op jit(solution)/shard_map/cond

commit v4 on v3

--- a/solution.py
+++ b/solution.py
@@ -11,7 +11,6 @@
 F32 = jnp.float32
 BF16 = jnp.bfloat16
 MIB = 1024 * 1024
-UNROLL = 2
 
 
 def params(mebibytes=16):
@@ -103,12 +102,11 @@
     ref[lead + (index, 1)] = value[:, width:]
 
 
-def store_rows(ref, index, value):
-    groups, _, double, width = ref.shape
-    rows = double // 2
+def store_by_rows(ref, index, value):
+    groups, _, rows, _, width = ref.shape
     for r in range(groups):
         for p in (0, 1):
-            ref[r, index, p * rows : (p + 1) * rows, :] = value[r * rows : (r + 1) * rows, p * width : (p + 1) * width]
+            ref[r, p, :, index, :] = value[r * rows : (r + 1) * rows, p * width : (p + 1) * width]
 
 
 def whole_term(green, middle):
@@ -173,7 +171,7 @@
         value = value + whole_term(load_matrix(lower, index), load_flat(before, index))
         value = value + whole_term(load_matrix(upper, index), load_flat(after, index))
         store_matrix(out, index, value)
-        store_rows(send, index, value)
+        store_by_rows(send, index, value)
 
 
 def side_terms(total, lower, upper, before, after, begin, size, groups, step):
@@ -184,10 +182,13 @@
         functools.partial(side_terms_kernel, step),
         grid=(size // step,),
         in_specs=[matrix_spec(step, at, width, 0)] + [matrix_spec(step, at, width, 1)] * 2 + [flat_spec(step, width)] * 2,
-        out_specs=[matrix_spec(step, 0, width, 0), rows_spec(step, groups, rows, width)],
+        out_specs=[
+            matrix_spec(step, 0, width, 0),
+            pl.BlockSpec((groups, 2, rows, step, width), lambda i: (0, 0, 0, i, 0)),
+        ],
         out_shape=[
             jax.ShapeDtypeStruct((size, 2, width, width), F32),
-            jax.ShapeDtypeStruct((groups, size, 2 * rows, width), F32),
+            jax.ShapeDtypeStruct((groups, 2, rows, size, width), F32),
         ],
         compiler_params=params(60),
         cost_estimate=cost(0.75 * size),
@@ -321,24 +322,19 @@
     return both[:size] + (both[size:] + dot(table[:size], value[1]))
 
 
-def convolve_kernel(first, second, groups, rows, extra, forth, back, weight_ref, final_ref, *refs):
-    inputs, outputs, scratch = refs[: len(first)], refs[len(first) : len(first) + len(second)], refs[len(first) + len(second) :]
-    total, double, width = weight_ref.shape
-    half = total // 2
+def convolve_kernel(first, second, rows, extra, forth, back, weight_ref, final_ref, *refs):
+    arrived, outputs, scratch = refs[: len(first)], refs[len(first) : len(first) + len(second)], refs[len(first) + len(second) :]
+    groups, _, here, _, width = arrived[0].shape
+    half = weight_ref.shape[3]
+    total = 2 * half
+    double = 2 * rows
     local = total // groups
     share = width // (2 * extra) if extra else 0
-    weight = weight_ref.reshape(total * double, width)
-    arrived = [ref.reshape(groups * size * double, width) for ref, (_, size) in zip(inputs, first)]
     spans = [(size + size // share) * rows if extra else size * double for _, size in second]
     leaving = [ref.reshape(groups * span, width) for ref, span in zip(outputs, spans)]
 
     def load(row, p):
-        pieces = [
-            arrived[c][pl.ds(j * size * double + p * rows + row, size, stride=double), :]
-            for j in range(groups)
-            for c, (_, size) in enumerate(first)
-        ]
-        return stack(*pieces)
+        return stack(*[arrived[c][j, p, row] for j in range(groups) for c in range(len(first))])
 
     def store_whole(row, real, imag):
         kept = final_ref[pl.ds(row, 1), :] * (1.0 / total)
@@ -366,7 +362,7 @@
                     at // share : (at + size) // share
                 ]
 
-    def two_rows(pair, carry):
+    for pair in range(here // 2):
         at = (2 * pair, 2 * pair + 1)
         values = [[load(row, p) for row in at] for p in (0, 1)]
         backs = []
@@ -375,9 +371,7 @@
             folded = [beside(*[value[:half] + sign * value[half:] for value in part]) for part in values]
             spectrum = apply_table(forth[odd], split(stack(*folded)), total)
             real, imag = spectrum[:half], spectrum[half:]
-            weights = [
-                beside(*[weight[pl.ds(odd * double + p * rows + row, half, stride=2 * double), :] for row in at]) for p in (0, 1)
-            ]
+            weights = [beside(*[weight_ref[row, p, odd] for row in at]) for p in (0, 1)]
             weighed = split(stack(real * weights[0] - imag * weights[1], real * weights[1] + imag * weights[0]))
             backs.append(apply_table(back[odd], weighed, total))
         early, late = backs[0] + backs[1], backs[0] - backs[1]
@@ -385,35 +379,40 @@
             lanes = slice(index * width, (index + 1) * width)
             real = stack(early[:half, lanes], late[:half, lanes])
             imag = stack(early[half:, lanes], late[half:, lanes])
+            place = pl.program_id(0) * here + row
             if extra:
-                store_packed(row, real, imag, scratch[index])
+                store_packed(place, real, imag, scratch[row])
             else:
-                store_whole(row, real, imag)
-        return carry
-
-    lax.fori_loop(0, rows // 2, two_rows, 0, unroll=UNROLL)
+                store_whole(place, real, imag)
 
 
 def convolve(arrived, weights, final, first, second, extra):
-    groups, _, double, width = arrived[0].shape
-    total = weights.shape[0]
-    rows = double // 2
+    groups, _, rows, _, width = arrived[0].shape
+    half = weights.shape[3]
+    total = 2 * half
+    here = min(rows, 4)
     if extra:
         share = width // (2 * extra)
         shapes = [(groups, (size + size // share) * rows, width) for _, size in second]
-        scratch = [pltpu.VMEM((total, width), F32)] * 2
+        scratch = [pltpu.VMEM((total, width), F32)] * here
     else:
-        shapes = [(groups, size, double, width) for _, size in second]
+        shapes = [(groups, size, 2 * rows, width) for _, size in second]
         scratch = []
-    whole = pl.BlockSpec(memory_space=pltpu.VMEM)
-    return pl.pallas_call(
-        functools.partial(convolve_kernel, first, second, groups, rows, extra),
-        in_specs=[whole] * (4 + len(first)),
-        out_specs=[whole] * len(second),
+
+    def fixed(shape):
+        return pl.BlockSpec(shape, lambda i: (0,) * len(shape))
+
+    return pl.pallas_call(
+        functools.partial(convolve_kernel, first, second, rows, extra),
+        grid=(rows // here,),
+        in_specs=[fixed((2, 2 * total, total))] * 2
+        + [pl.BlockSpec((here, 2, 2, half, width), lambda i: (i, 0, 0, 0, 0)), fixed(final.shape)]
+        + [pl.BlockSpec((groups, 2, here, size, width), lambda i: (0, 0, i, 0, 0)) for _, size in first],
+        out_specs=[fixed(shape) for shape in shapes],
         out_shape=[jax.ShapeDtypeStruct(shape, F32) for shape in shapes],
         scratch_shapes=scratch,
         compiler_params=params(60),
-        cost_estimate=cost(0.3 * total / groups + 7.0),
+        cost_estimate=cost(0.2 * total / groups + 4.0),
         name="convolve",
     )(transform_tables(total, False), transform_tables(total, True), weights, final, *arrived)
 
@@ -477,6 +476,7 @@
     edge = sent[0].shape[0]
     sent[0] = stack(sent[0], jnp.broadcast_to(mine, (8, width)))
     own = own_terms(green_diag, sigma_lesser, 2 * step)
+    weights = tied(screened[0], own).reshape(total // 2, 2, 2, rows, width).transpose(3, 2, 1, 0, 4)
     halos, bases, arrived = [neighbours(part, slabs) for part in sent[:2]], [], []
     patterns = jnp.stack([mine, halos[0][0][edge], halos[0][1][edge]])
     ranks = jnp.cumsum(patterns, axis=1).astype(jnp.int32) - 1
@@ -485,10 +485,8 @@
     for index, (at, size) in enumerate(first):
         if index + 2 < len(first):
             halos.append(neighbours(tied(sent[index + 2], (halos[index], own)), slabs))
-        halo = halos[index]
-        if index:
-            halo = tied(halo, (arrived[max(index - 2, 0)], packed_greens))
-        base, send = side_terms(own, green_lower, green_upper, *halo, at, size, groups, step)
+        halo = tied(halos[index], (arrived[max(index - 2, 0)], packed_greens) if index else weights)
+        base, send = side_terms(own, green_lower, green_upper, *halo, at, size, groups, 2 * step)
         bases.append(base)
         arrived.append(exchange(send))
 
@@ -496,7 +494,6 @@
     chosen = ((ranks[0][None, :] == jnp.arange(cap)[:, None]) & (mine[None, :] > 0)).astype(BF16)
     own_rows = lax.dynamic_slice_in_dim(mine, lax.axis_index("energy") * rows, rows)
     mask = own_rows[:, None] * mine[None, :]
-    weights = screened.reshape(total, 2 * rows, width)
     parts = convolve(arrived, weights, places[0], first, second, extra)
 
     def within(begin, size):
@@ -506,7 +503,7 @@
         packed, halos, partials = [], [], []
         for index, (part, (at, size)) in enumerate(zip(parts, second)):
             part = exchange(tied(part, (packed[0], partials[: index - 1])) if index else part)
-            packed.append(pack_rows(chosen, part, rows))
+            packed.append(pack_rows(chosen, tied(part, partials) if index else part, rows))
             halos.append(neighbours(packed[-1], slabs))
             partials.append(
                 packed_again(

time: 230 us -> 241 us (1.048)
  blocking collectives: 31.4 us -> 44.4 us
  waiting for transfers between devices: 49.9 us -> 37.1 us
  local copies, waits for them, and re-layouts: 5 us -> 11.6 us
  starting transfers between devices: 52 us -> 54.8 us
    pmax x1, blocking collectives: 9.71 us -> 22 us  [local(): fits = lax.pmax(tied(jnp.sum(mine), bases[-1]), 'slab') <= cap]
    all_to_all x5, waiting for transfers between devices: 22.7 us -> 11.4 us  [exchange(): lax.all_to_all(value, 'energy', split_axis=0, concat_axis=0, tiled=True)]
    reshape x0 -> x1, local copies, waits for them, and re-layouts: none -> 6.6 us  [local(): tied(screened[0], own).reshape(total // 2, 2, 2, rows, width)]
    pallas_call x1, Pallas kernels: 18.1 us -> 12.8 us  [convolve(): pl.pallas_call(functools.partial(convolve_kernel, first, second, rows, ex...]
    pallas_call x4, Pallas kernels: 24.3 us -> 27.7 us  [side_terms(): pl.pallas_call(functools.partial(side_terms_kernel, step), grid=(size //...]
    ppermute x12, starting transfers between devices: 32.3 us -> 34.9 us  [neighbours(): return (lax.ppermute(value, 'slab', up), lax.ppermute(value, 'slab', down))]
  transfers between devices with their start and end apart: 17 -> 17, of which waited for: 10 -> 9; matrix products, arithmetic and copies ran while one was open for 2% -> 4% of each run, Pallas kernels for 27% -> 28%
where the time goes in v4:
time: 241 us; the launch traced here: 239 us
  Pallas kernels  86.2 us (36%)
  starting transfers between devices  54.8 us (23%)
  blocking collectives  44.4 us (18%)
  waiting for transfers between devices  37.1 us (15%)
  local copies, waits for them, and re-layouts  11.6 us (5%)
  other arithmetic  3.79 us (2%)
    ppermute x12, starting transfers between devices, neighbours(): return (lax.ppermute(value, 'slab', up), lax.ppermute(value, 'slab', down))  34.9 us
    pallas_call x4, Pallas kernels, side_terms(): pl.pallas_call(functools.partial(side_terms_kernel, step), grid=(size //...  27.7 us
    ppermute x12, waiting for transfers between devices, neighbours(): return (lax.ppermute(value, 'slab', up), lax.ppermute(value, 'slab', down))  25.7 us
    all_to_all x1, blocking collectives, exchange(): lax.all_to_all(value, 'energy', split_axis=0, concat_axis=0, tiled=True)  22.4 us
    pmax x1, blocking collectives, local(): fits = lax.pmax(tied(jnp.sum(mine), bases[-1]), 'slab') <= cap  22 us
    pallas_call x4, Pallas kernels, packed_again(): pl.pallas_call(functools.partial(packed_again_kernel, step, places, count...  21.8 us
    all_to_all x5, starting transfers between devices, exchange(): lax.all_to_all(value, 'energy', split_axis=0, concat_axis=0, tiled=True)  19.9 us
    pallas_call x1, Pallas kernels, convolve(): pl.pallas_call(functools.partial(convolve_kernel, first, second, rows, ex...  12.8 us
  transfers between devices with their start and end apart: 17, of which 9 were waited for; matrix products, arithmetic and copies ran while one was open for 4% of the time, Pallas kernels for 28%

profile of v4, /device:TPU:0, one launch (start us, length us, event | category | flops | bytes accessed | tf_op | source)
XLA Modules:
  0.0 239.1 jit_solution(17017485013036807070)
XLA Ops:
  0.0 3.9 %fusion.13 = (f32[1,8,2,128,128]{4,3,2,1,0:T(8,128)}, f32[1,8,2,128,128]{4,3,2,1,0:T(8,128)}, f32[1,8,2,128,128]{4,3,2,1,0:T(8,128)}, f32[1,8,2,128,128]{4,3,2,1,0:T(8,128)S(1)}) fusion(f32[1,32,2,128,128]{4,3,2,1,0:T(8,128)} %sigma.1), kind=kLoop, calls=%fused_computation.61 | loop fusion | bytes 8388608 | tf_op jit(solution)/shard_map/slice | solution.py:475
  4.0 5.0 %collective-permute-start.12 = (f32[2056,128]{1,0:T(8,128)S(1)}, f32[2056,128]{1,0:T(8,128)S(1)}, u32[]{:S(2)}, u32[]{:S(2)}) collective-permute-start(f32[2056,128]{1,0:T(8,128)S(1)} %pad_maximum_fusion), channel_id=1, source_target_pairs={{0,1},{1,2},{2,3},{4,5},{5,6},{6,7},{8,9},{9,10},{10,11},{12,13},{... | collective-permute-start | bytes 3158024 | tf_op jit(solution)/shard_map/ppermute | solution.py:436
  10.3 5.6 %collective-permute-start.8 = (f32[2048,128]{1,0:T(8,128)}, f32[2048,128]{1,0:T(8,128)}, u32[]{:S(2)}, u32[]{:S(2)}) collective-permute-start(f32[2048,128]{1,0:T(8,128)} %bitcast.1), channel_id=1, source_target_pairs={{0,1},{1,2},{2,3},{4,5},{5,6},{6,7},{8,9},{9,10},{10,11},{12,13},{... | collective-permute-start | bytes 3145736 | tf_op jit(solution)/shard_map/ppermute | solution.py:436
  17.2 9.4 %own_terms.1.total = f32[32,2,128,128]{3,2,1,0:T(8,128)} custom-call(f32[1,32,2,128,128]{4,3,2,1,0:T(8,128)} %refs_0_.1, f32[1,32,2,128,128]{4,3,2,1,0:T(8,128)} %sigma.1), custom_call_target="tpu_custom_call" | custom-call | flops 3864000000 | bytes 12398400 | tf_op jit(solution)/shard_map/own_terms/pallas_call | solution.py:156
  26.6 6.6 %copy.17 = f32[128,2,2,16,128]{4,0,1,2,3:T(8,128)} copy(f32[128,2,2,16,128]{4,3,2,1,0:T(8,128)} %bitcast.36) | data formatting | bytes 8388608 | tf_op jit(solution)/shard_map/reshape | solution.py:479
  33.3 3.8 %collective-permute-done.13.after = f32[2056,128]{1,0:T(8,128)S(1)} collective-permute-done((f32[2056,128]{1,0:T(8,128)S(1)}, f32[2056,128]{1,0:T(8,128)S(1)}, u32[]{:S(2)}, u32[]{:S(2)}) %collective-permute-start.13) | collective-permute-done | bytes 1052704 | tf_op jit(solution)/shard_map/ppermute | solution.py:436
  37.1 4.4 %collective-permute-start.14 = (f32[2048,128]{1,0:T(8,128)}, f32[2048,128]{1,0:T(8,128)}, u32[]{:S(2)}, u32[]{:S(2)}) collective-permute-start(f32[2048,128]{1,0:T(8,128)} %bitcast.18), channel_id=1, source_target_pairs={{0,1},{1,2},{2,3},{4,5},{5,6},{6,7},{8,9},{9,10},{10,11},{12,13},{... | collective-permute-start | bytes 3145736 | tf_op jit(solution)/shard_map/ppermute | solution.py:436
  43.2 6.6 %side_terms.4 = (f32[8,2,128,128]{3,2,1,0:T(8,128)S(1)}, f32[8,2,16,8,128]{4,3,2,1,0:T(8,128)}) custom-call(f32[32,2,128,128]{3,2,1,0:T(8,128)} %own_terms.1.total, f32[1,32,2,128,128]{4,3,2,1,0:T(8,128)} %lower.7, f32[1,32,2,128,128]{4,3,2,1,0:T(8,128)} %upper.7, f32[2056,128]{1,0:T(8,128)} %copy-done.12, f32[2056,128]{1,0:T(8,128)} %copy-done.13), custom_call_target="tpu_custom_call" | custom-call | flops 2070000000 | bytes 6641999 | tf_op jit(solution)/shard_map/side_terms/pallas_call | solution.py:181
  49.8 4.0 %all-to-all-start.4 = ((f32[8,2,16,8,128]{4,3,2,1,0:T(8,128)}), f32[8,2,16,8,128]{4,3,2,1,0:T(8,128)S(1)}, u32[]{:S(2)}, u32[]{:S(2)}) async-start(f32[8,2,16,8,128]{4,3,2,1,0:T(8,128)} %get-tuple-element.133), calls=%async_computation.4 | async-start | bytes 2097152 | tf_op jit(solution)/shard_map/all_to_all | solution.py:440
  55.6 12.3 %pack_green.1 = (bf16[32,256,256]{2,1,0:T(8,128)(2,1)}, bf16[32,256,256]{2,1,0:T(8,128)(2,1)}, bf16[32,256,256]{2,1,0:T(8,128)(2,1)}) custom-call(bf16[3,256,256]{2,1,0:T(8,128)(2,1)} %add_convert_fusion.place, f32[1,32,2,128,128]{4,3,2,1,0:T(8,128)} %refs_0_.1, f32[1,32,2,128,128]{4,3,2,1,0:T(8,128)} %lower.7, f32[1,32,2,128,128]{4,3,2,1,0:T(8,128)} %upper.7), custom_call_target="tpu_custom_call" | custom-call | flops 4305600000 | bytes 13815360 | tf_op jit(solution)/shard_map/pack_green/pallas_call | solution.py:285
  69.2 7.3 %side_terms.5 = (f32[8,2,128,128]{3,2,1,0:T(8,128)}, f32[8,2,16,8,128]{4,3,2,1,0:T(8,128)}) custom-call(f32[32,2,128,128]{3,2,1,0:T(8,128)} %own_terms.1.total, f32[1,32,2,128,128]{4,3,2,1,0:T(8,128)} %lower.7, f32[1,32,2,128,128]{4,3,2,1,0:T(8,128)} %upper.7, f32[2048,128]{1,0:T(8,128)} %collective-permute-done.8.before, ...), custom_call_target="tpu_custom_call" | custom-call | flops 2070000000 | bytes 6641999 | tf_op jit(solution)/shard_map/side_terms/pallas_call | solution.py:181
  76.5 4.3 %all-to-all-start.5 = ((f32[8,2,16,8,128]{4,3,2,1,0:T(8,128)}), f32[8,2,16,8,128]{4,3,2,1,0:T(8,128)}, u32[]{:S(2)}, u32[]{:S(2)}) async-start(f32[8,2,16,8,128]{4,3,2,1,0:T(8,128)} %get-tuple-element.139), calls=%async_computation.5 | async-start | bytes 2097152 | tf_op jit(solution)/shard_map/all_to_all | solution.py:440
  80.7 4.6 %collective-permute-start.10 = (f32[2048,128]{1,0:T(8,128)}, f32[2048,128]{1,0:T(8,128)S(1)}, u32[]{:S(2)}, u32[]{:S(2)}) collective-permute-start(f32[2048,128]{1,0:T(8,128)} %bitcast), channel_id=1, source_target_pairs={{0,1},{1,2},{2,3},{4,5},{5,6},{6,7},{8,9},{9,10},{10,11},{12,13},{... | collective-permute-start | bytes 3145736 | tf_op jit(solution)/shard_map/ppermute | solution.py:436
  86.7 6.9 %side_terms.7 = (f32[8,2,128,128]{3,2,1,0:T(8,128)}, f32[8,2,16,8,128]{4,3,2,1,0:T(8,128)}) custom-call(f32[32,2,128,128]{3,2,1,0:T(8,128)} %own_terms.1.total, f32[1,32,2,128,128]{4,3,2,1,0:T(8,128)} %lower.7, f32[1,32,2,128,128]{4,3,2,1,0:T(8,128)} %upper.7, f32[2048,128]{1,0:T(8,128)} %collective-permute-done.14.before, ...), custom_call_target="tpu_custom_call" | custom-call | flops 2070000000 | bytes 6641999 | tf_op jit(solution)/shard_map/side_terms/pallas_call | solution.py:181
  96.2 4.2 %all-to-all-start.6 = ((f32[8,2,16,8,128]{4,3,2,1,0:T(8,128)}), f32[8,2,16,8,128]{4,3,2,1,0:T(8,128)}, u32[]{:S(2)}, u32[]{:S(2)}) async-start(f32[8,2,16,8,128]{4,3,2,1,0:T(8,128)} %get-tuple-element.150), calls=%async_computation.6 | async-start | bytes 2097152 | tf_op jit(solution)/shard_map/all_to_all | solution.py:440
  100.4 8.1 %collective-permute-done.10.before = f32[2048,128]{1,0:T(8,128)S(1)} collective-permute-done((f32[2048,128]{1,0:T(8,128)}, f32[2048,128]{1,0:T(8,128)S(1)}, u32[]{:S(2)}, u32[]{:S(2)}) %collective-permute-start.10) | collective-permute-done | bytes 1048608 | tf_op jit(solution)/shard_map/ppermute | solution.py:436
  108.5 4.1 %collective-permute-done.11.after = f32[2048,128]{1,0:T(8,128)S(1)} collective-permute-done((f32[2048,128]{1,0:T(8,128)}, f32[2048,128]{1,0:T(8,128)S(1)}, u32[]{:S(2)}, u32[]{:S(2)}) %collective-permute-start.11) | collective-permute-done | bytes 1048608 | tf_op jit(solution)/shard_map/ppermute | solution.py:436
  113.6 6.9 %side_terms.6 = (f32[8,2,128,128]{3,2,1,0:T(8,128)}, f32[8,2,16,8,128]{4,3,2,1,0:T(8,128)}) custom-call(f32[32,2,128,128]{3,2,1,0:T(8,128)} %own_terms.1.total, f32[1,32,2,128,128]{4,3,2,1,0:T(8,128)} %lower.7, f32[1,32,2,128,128]{4,3,2,1,0:T(8,128)} %upper.7, f32[2048,128]{1,0:T(8,128)} %copy-done.14, f32[2048,128]{1,0:T(8,128)} %copy-done.15), custom_call_target="tpu_custom_call" | custom-call | flops 2070000000 | bytes 6641999 | tf_op jit(solution)/shard_map/side_terms/pallas_call | solution.py:181
  120.5 3.9 %all-to-all-start.7 = ((f32[8,2,16,8,128]{4,3,2,1,0:T(8,128)}), f32[8,2,16,8,128]{4,3,2,1,0:T(8,128)S(1)}, u32[]{:S(2)}, u32[]{:S(2)}) async-start(f32[8,2,16,8,128]{4,3,2,1,0:T(8,128)} %get-tuple-element.151), calls=%async_computation.7 | async-start | bytes 2097152 | tf_op jit(solution)/shard_map/all_to_all | solution.py:440
  126.0 22.0 %pmax.7 = f32[]{:T(128)} all-reduce(f32[]{:T(128)} %convert_reduce_fusion), channel_id=1, replica_groups=mesh['energy'=8,'slab'=4] {'slab'}, use_global_device_ids=true, to_apply=%region_2.3 | all-reduce | flops 1 | bytes 8 | tf_op jit(solution)/shard_map/pmax | solution.py:493
  148.7 12.8 %convolve.3 = (f32[8,320,128]{2,1,0:T(8,128)}, f32[8,320,128]{2,1,0:T(8,128)}) custom-call(bf16[2,512,256]{2,1,0:T(8,128)(2,1)} %constant.137.clone.forth, bf16[2,512,256]{2,1,0:T(8,128)(2,1)} %constant.138.clone.back, f32[16,2,2,128,128]{4,3,2,1,0:T(8,128)} %bitcast.37, bf16[256,256]{1,0:T(8,128)(2,1)} %and_convert_fusion.final_ref, ...), custom_call_target="tpu_custom_call" | custom-call | flops 3588000000 | bytes 11512800 | tf_op jit(solution)/shard_map/convolve/pallas_call | solution.py:405
  161.5 77.4 %conditional.1 = (f32[1,32,2,128,128]{4,3,2,1,0:T(8,128)}) conditional(s32[]{:T(128)} %convert_element_type.39, (f32[8,2,128,128]{3,2,1,0:T(8,128)S(1)}, f32[8,2,128,128]{3,2,1,0:T(8,128)}, f32[8,2,128,128]{3,2,1,0:T(8,128)}, f32[8,2,128,128]{3,2,1,0:T(8,128)}, s32[]{:T(128)}, /*index=5*/f32[128]{0:T(128)S(1)}, bf16[2,512,256]{2,1,0:T(8,128)(2,1)}, ...), branch_computations={%region_3.4_spmd, %region_4.5_spmd} | conditional | flops 13524001792 | bytes 162941344 | solution.py:531
  161.5 22.4 %all_to_all.37.part = f32[8,320,128]{2,1,0:T(8,128)S(1)} all-to-all(f32[8,320,128]{2,1,0:T(8,128)} %get-tuple-element.96), channel_id=1, replica_groups=mesh['energy'=8,'slab'=4] {'energy'}, dimensions={0} | all-to-all | bytes 2621440 | tf_op jit(solution)/shard_map/cond/branch_1_fun/all_to_all | solution.py:440
  185.4 3.6 %all-to-all-start.1 = ((f32[8,320,128]{2,1,0:T(8,128)}), f32[8,320,128]{2,1,0:T(8,128)S(1)}, u32[]{:S(2)}, u32[]{:S(2)}) async-start(f32[8,320,128]{2,1,0:T(8,128)} %get-tuple-element.102), calls=%async_computation.1 | async-start | bytes 2621440 | tf_op jit(solution)/shard_map/cond/branch_1_fun/all_to_all | solution.py:440
  189.0 4.2 %collective-permute-start = (f32[20,80,128]{2,1,0:T(8,128)}, f32[20,80,128]{2,1,0:T(8,128)}, u32[]{:S(2)}, u32[]{:S(2)}) collective-permute-start(f32[20,80,128]{2,1,0:T(8,128)} %pack_rows.2.refs_3_), channel_id=1, source_target_pairs={{0,1},{1,2},{2,3},{4,5},{5,6},{6,7},{8,9},{9,10},{10,11},{12,13},{... | collective-permute-start | bytes 2457608 | tf_op jit(solution)/shard_map/cond/branch_1_fun/ppermute | solution.py:436
  194.5 5.0 %packed_again.4.refs_0_ = f32[16,2,128,128]{3,2,1,0:T(8,128)S(1)} custom-call(f32[8,2,128,128]{3,2,1,0:T(8,128)} %copy-done.7, f32[8,2,128,128]{3,2,1,0:T(8,128)} %get-tuple-element.93.refs_1_, bf16[32,256,256]{2,1,0:T(8,128)(2,1)} %get-tuple-element.94.refs_2_, f32[20,80,128]{2,1,0:T(8,128)} %pack_rows.2.refs_3_), custom_call_target="tpu_custom_call" | custom-call | flops 1656000000 | bytes 5313600 | tf_op jit(solution)/shard_map/cond/branch_1_fun/packed_again/pallas_call | solution.py:254
  199.5 7.6 %all-to-all-done.1.part = f32[8,320,128]{2,1,0:T(8,128)S(1)} async-done(((f32[8,320,128]{2,1,0:T(8,128)}), f32[8,320,128]{2,1,0:T(8,128)S(1)}, u32[]{:S(2)}, u32[]{:S(2)}) %all-to-all-start.1) | async-done | bytes 1310752 | tf_op jit(solution)/shard_map/cond/branch_1_fun/all_to_all | solution.py:440
  207.7 3.4 %collective-permute-start.2 = (f32[20,80,128]{2,1,0:T(8,128)S(1)}, f32[20,80,128]{2,1,0:T(8,128)S(1)}, u32[]{:S(2)}, u32[]{:S(2)}) collective-permute-start(f32[20,80,128]{2,1,0:T(8,128)S(1)} %pack_rows.3.refs_3_), channel_id=1, source_target_pairs={{0,1},{1,2},{2,3},{4,5},{5,6},{6,7},{8,9},{9,10},{10,11},{12,13},{... | collective-permute-start | bytes 2457608 | tf_op jit(solution)/shard_map/cond/branch_1_fun/ppermute | solution.py:436
  212.4 4.1 %collective-permute-done.1.refs_4_ = f32[20,80,128]{2,1,0:T(8,128)} collective-permute-done((f32[20,80,128]{2,1,0:T(8,128)}, f32[20,80,128]{2,1,0:T(8,128)}, u32[]{:S(2)}, u32[]{:S(2)}) %collective-permute-start.1) | collective-permute-done | bytes 819232 | tf_op jit(solution)/shard_map/cond/branch_1_fun/ppermute | solution.py:436
  216.5 8.0 %packed_again.5.refs_0_ = f32[1,32,2,128,128]{4,3,2,1,0:T(8,128)} custom-call(f32[16,2,128,128]{3,2,1,0:T(8,128)S(1)} %packed_again.4.refs_0_, bf16[32,256,256]{2,1,0:T(8,128)(2,1)} %get-tuple-element.97.refs_1_.refs_2_, bf16[32,256,256]{2,1,0:T(8,128)(2,1)} %get-tuple-element.98.refs_2_.refs_3_, f32[20,80,128]{2,1,0:T(8,128)} %collective-permute-done.refs_3_, ...), custom_call_target="tpu_custom_call" | custom-call | flops 3312000000 | bytes 10627200 | tf_op jit(solution)/shard_map/cond/branch_1_fun/packed_again/pallas_call | solution.py:254
  228.1 5.0 %collective-permute-done.3.refs_5_ = f32[20,80,128]{2,1,0:T(8,128)S(1)} collective-permute-done((f32[20,80,128]{2,1,0:T(8,128)S(1)}, f32[20,80,128]{2,1,0:T(8,128)S(1)}, u32[]{:S(2)}, u32[]{:S(2)}) %collective-permute-start.3) | collective-permute-done | bytes 819232 | tf_op jit(solution)/shard_map/cond/branch_1_fun/ppermute | solution.py:436
  233.1 5.8 %packed_again.7 = f32[1,32,2,128,128]{4,3,2,1,0:T(8,128)} custom-call(f32[1,32,2,128,128]{4,3,2,1,0:T(8,128)} %packed_again.5.refs_0_, f32[16,2,128,128]{3,2,1,0:T(8,128)S(1)} %packed_again.6.refs_1_, bf16[32,256,256]{2,1,0:T(8,128)(2,1)S(1)} %copy-done.5, bf16[32,256,256]{2,1,0:T(8,128)(2,1)S(1)} %copy-done.6, ...), custom_call_target="tpu_custom_call", output_to_operand_aliasing={{}: (0, {})} | custom-call | flops 3312000000 | bytes 10627200 | tf_op jit(solution)/shard_map/cond/branch_1_fun/packed_again/pallas_call | solution.py:254
  (71 shorter events, 22.0 us)
Async XLA Ops:
  0.0 3.9 %copy-start.18 = (s32[1,128]{1,0:T(1,128)S(1)}, s32[1,128]{1,0:T(1,128)}, u32[]{:S(2)}) copy-start(s32[1,128]{1,0:T(1,128)} %param.17) | copy-start | bytes 1540
  4.0 29.2 %collective-permute-start.12 = (f32[2056,128]{1,0:T(8,128)S(1)}, f32[2056,128]{1,0:T(8,128)S(1)}, u32[]{:S(2)}, u32[]{:S(2)}) collective-permute-start(f32[2056,128]{1,0:T(8,128)S(1)} %pad_maximum_fusion), channel_id=1, source_target_pairs={{0,1},{1,2},{2,3},{4,5},{5,6},{6,7},{8,9},{9,10},{10,11},{12,13},{... | collective-permute-start | bytes 3158024 | tf_op jit(solution)/shard_map/ppermute | solution.py:436
  9.0 28.1 %collective-permute-start.13 = (f32[2056,128]{1,0:T(8,128)S(1)}, f32[2056,128]{1,0:T(8,128)S(1)}, u32[]{:S(2)}, u32[]{:S(2)}) collective-permute-start(f32[2056,128]{1,0:T(8,128)S(1)} %pad_maximum_fusion), channel_id=1, source_target_pairs={{1,0},{2,1},{3,2},{5,4},{6,5},{7,6},{9,8},{10,9},{11,10},{13,12},{... | collective-permute-start | bytes 3158024 | tf_op jit(solution)/shard_map/ppermute | solution.py:436
  10.3 57.6 %collective-permute-start.8 = (f32[2048,128]{1,0:T(8,128)}, f32[2048,128]{1,0:T(8,128)}, u32[]{:S(2)}, u32[]{:S(2)}) collective-permute-start(f32[2048,128]{1,0:T(8,128)} %bitcast.1), channel_id=1, source_target_pairs={{0,1},{1,2},{2,3},{4,5},{5,6},{6,7},{8,9},{9,10},{10,11},{12,13},{... | collective-permute-start | bytes 3145736 | tf_op jit(solution)/shard_map/ppermute | solution.py:436
  15.9 52.0 %collective-permute-start.9 = (f32[2048,128]{1,0:T(8,128)}, f32[2048,128]{1,0:T(8,128)}, u32[]{:S(2)}, u32[]{:S(2)}) collective-permute-start(f32[2048,128]{1,0:T(8,128)} %bitcast.1), channel_id=1, source_target_pairs={{1,0},{2,1},{3,2},{5,4},{6,5},{7,6},{9,8},{10,9},{11,10},{13,12},{... | collective-permute-start | bytes 3145736 | tf_op jit(solution)/shard_map/ppermute | solution.py:436
  33.3 9.9 %copy-start.12 = (f32[2056,128]{1,0:T(8,128)}, f32[2056,128]{1,0:T(8,128)S(1)}, u32[]{:S(2)}) copy-start(f32[2056,128]{1,0:T(8,128)S(1)} %collective-permute-done.12.before) | copy-start | bytes 3158020
  37.1 6.1 %copy-start.13 = (f32[2056,128]{1,0:T(8,128)}, f32[2056,128]{1,0:T(8,128)S(1)}, u32[]{:S(2)}) copy-start(f32[2056,128]{1,0:T(8,128)S(1)} %collective-permute-done.13.after) | copy-start | bytes 3158020
  37.1 49.6 %collective-permute-start.14 = (f32[2048,128]{1,0:T(8,128)}, f32[2048,128]{1,0:T(8,128)}, u32[]{:S(2)}, u32[]{:S(2)}) collective-permute-start(f32[2048,128]{1,0:T(8,128)} %bitcast.18), channel_id=1, source_target_pairs={{0,1},{1,2},{2,3},{4,5},{5,6},{6,7},{8,9},{9,10},{10,11},{12,13},{... | collective-permute-start | bytes 3145736 | tf_op jit(solution)/shard_map/ppermute | solution.py:436
  41.5 45.2 %collective-permute-start.15 = (f32[2048,128]{1,0:T(8,128)}, f32[2048,128]{1,0:T(8,128)}, u32[]{:S(2)}, u32[]{:S(2)}) collective-permute-start(f32[2048,128]{1,0:T(8,128)} %bitcast.18), channel_id=1, source_target_pairs={{1,0},{2,1},{3,2},{5,4},{6,5},{7,6},{9,8},{10,9},{11,10},{13,12},{... | collective-permute-start | bytes 3145736 | tf_op jit(solution)/shard_map/ppermute | solution.py:436
  49.8 19.4 %all-to-all-start.4 = ((f32[8,2,16,8,128]{4,3,2,1,0:T(8,128)}), f32[8,2,16,8,128]{4,3,2,1,0:T(8,128)S(1)}, u32[]{:S(2)}, u32[]{:S(2)}) async-start(f32[8,2,16,8,128]{4,3,2,1,0:T(8,128)} %get-tuple-element.133), calls=%async_computation.4 | async-start | bytes 2097152 | tf_op jit(solution)/shard_map/all_to_all | solution.py:440
  69.2 7.3 %copy-start.16 = (f32[8,2,16,8,128]{4,3,2,1,0:T(8,128)}, f32[8,2,16,8,128]{4,3,2,1,0:T(8,128)S(1)}, u32[]{:S(2)}) copy-start(f32[8,2,16,8,128]{4,3,2,1,0:T(8,128)S(1)} %all-to-all-done.4.refs_0_) | copy-start | bytes 3145732
  76.5 19.7 %all-to-all-start.5 = ((f32[8,2,16,8,128]{4,3,2,1,0:T(8,128)}), f32[8,2,16,8,128]{4,3,2,1,0:T(8,128)}, u32[]{:S(2)}, u32[]{:S(2)}) async-start(f32[8,2,16,8,128]{4,3,2,1,0:T(8,128)} %get-tuple-element.139), calls=%async_computation.5 | async-start | bytes 2097152 | tf_op jit(solution)/shard_map/all_to_all | solution.py:440
  80.7 27.8 %collective-permute-start.10 = (f32[2048,128]{1,0:T(8,128)}, f32[2048,128]{1,0:T(8,128)S(1)}, u32[]{:S(2)}, u32[]{:S(2)}) collective-permute-start(f32[2048,128]{1,0:T(8,128)} %bitcast), channel_id=1, source_target_pairs={{0,1},{1,2},{2,3},{4,5},{5,6},{6,7},{8,9},{9,10},{10,11},{12,13},{... | collective-permute-start | bytes 3145736 | tf_op jit(solution)/shard_map/ppermute | solution.py:436
  85.4 27.2 %collective-permute-start.11 = (f32[2048,128]{1,0:T(8,128)}, f32[2048,128]{1,0:T(8,128)S(1)}, u32[]{:S(2)}, u32[]{:S(2)}) collective-permute-start(f32[2048,128]{1,0:T(8,128)} %bitcast), channel_id=1, source_target_pairs={{1,0},{2,1},{3,2},{5,4},{6,5},{7,6},{9,8},{10,9},{11,10},{13,12},{... | collective-permute-start | bytes 3145736 | tf_op jit(solution)/shard_map/ppermute | solution.py:436
  96.2 24.4 %all-to-all-start.6 = ((f32[8,2,16,8,128]{4,3,2,1,0:T(8,128)}), f32[8,2,16,8,128]{4,3,2,1,0:T(8,128)}, u32[]{:S(2)}, u32[]{:S(2)}) async-start(f32[8,2,16,8,128]{4,3,2,1,0:T(8,128)} %get-tuple-element.150), calls=%async_computation.6 | async-start | bytes 2097152 | tf_op jit(solution)/shard_map/all_to_all | solution.py:440
  108.5 4.1 %copy-start.14 = (f32[2048,128]{1,0:T(8,128)}, f32[2048,128]{1,0:T(8,128)S(1)}, u32[]{:S(2)}) copy-start(f32[2048,128]{1,0:T(8,128)S(1)} %collective-permute-done.10.before) | copy-start | bytes 3145732
  112.6 1.0 copy-start.15
  120.5 28.1 %all-to-all-start.7 = ((f32[8,2,16,8,128]{4,3,2,1,0:T(8,128)}), f32[8,2,16,8,128]{4,3,2,1,0:T(8,128)S(1)}, u32[]{:S(2)}, u32[]{:S(2)}) async-start(f32[8,2,16,8,128]{4,3,2,1,0:T(8,128)} %get-tuple-element.151), calls=%async_computation.7 | async-start | bytes 2097152 | tf_op jit(solution)/shard_map/all_to_all | solution.py:440
  148.6 12.9 %copy-start.17 = (f32[8,2,16,8,128]{4,3,2,1,0:T(8,128)S(1)}, f32[8,2,16,8,128]{4,3,2,1,0:T(8,128)}, u32[]{:S(2)}) copy-start(f32[8,2,16,8,128]{4,3,2,1,0:T(8,128)} %copy-done.16) | copy-start | bytes 3145732
  161.5 23.9 %copy-start.7 = (f32[8,2,128,128]{3,2,1,0:T(8,128)}, f32[8,2,128,128]{3,2,1,0:T(8,128)S(1)}, u32[]{:S(2)}) copy-start(f32[8,2,128,128]{3,2,1,0:T(8,128)S(1)} %get-tuple-element.92.refs_0_) | copy-start | bytes 3145732 | tf_op jit(solution)/shard_map/cond
  185.4 21.7 %all-to-all-start.1 = ((f32[8,320,128]{2,1,0:T(8,128)}), f32[8,320,128]{2,1,0:T(8,128)S(1)}, u32[]{:S(2)}, u32[]{:S(2)}) async-start(f32[8,320,128]{2,1,0:T(8,128)} %get-tuple-element.102), calls=%async_computation.1 | async-start | bytes 2621440 | tf_op jit(solution)/shard_map/cond/branch_1_fun/all_to_all | solution.py:440
  189.0 23.4 %collective-permute-start = (f32[20,80,128]{2,1,0:T(8,128)}, f32[20,80,128]{2,1,0:T(8,128)}, u32[]{:S(2)}, u32[]{:S(2)}) collective-permute-start(f32[20,80,128]{2,1,0:T(8,128)} %pack_rows.2.refs_3_), channel_id=1, source_target_pairs={{0,1},{1,2},{2,3},{4,5},{5,6},{6,7},{8,9},{9,10},{10,11},{12,13},{... | collective-permute-start | bytes 2457608 | tf_op jit(solution)/shard_map/cond/branch_1_fun/ppermute | solution.py:436
  193.2 23.3 %collective-permute-start.1 = (f32[20,80,128]{2,1,0:T(8,128)}, f32[20,80,128]{2,1,0:T(8,128)}, u32[]{:S(2)}, u32[]{:S(2)}) collective-permute-start(f32[20,80,128]{2,1,0:T(8,128)} %pack_rows.2.refs_3_), channel_id=1, source_target_pairs={{1,0},{2,1},{3,2},{5,4},{6,5},{7,6},{9,8},{10,9},{11,10},{13,12},{... | collective-permute-start | bytes 2457608 | tf_op jit(solution)/shard_map/cond/branch_1_fun/ppermute | solution.py:436
  207.7 20.4 %collective-permute-start.2 = (f32[20,80,128]{2,1,0:T(8,128)S(1)}, f32[20,80,128]{2,1,0:T(8,128)S(1)}, u32[]{:S(2)}, u32[]{:S(2)}) collective-permute-start(f32[20,80,128]{2,1,0:T(8,128)S(1)} %pack_rows.3.refs_3_), channel_id=1, source_target_pairs={{0,1},{1,2},{2,3},{4,5},{5,6},{6,7},{8,9},{9,10},{10,11},{12,13},{... | collective-permute-start | bytes 2457608 | tf_op jit(solution)/shard_map/cond/branch_1_fun/ppermute | solution.py:436
  211.1 22.0 %collective-permute-start.3 = (f32[20,80,128]{2,1,0:T(8,128)S(1)}, f32[20,80,128]{2,1,0:T(8,128)S(1)}, u32[]{:S(2)}, u32[]{:S(2)}) collective-permute-start(f32[20,80,128]{2,1,0:T(8,128)S(1)} %pack_rows.3.refs_3_), channel_id=1, source_target_pairs={{1,0},{2,1},{3,2},{5,4},{6,5},{7,6},{9,8},{10,9},{11,10},{13,12},{... | collective-permute-start | bytes 2457608 | tf_op jit(solution)/shard_map/cond/branch_1_fun/ppermute | solution.py:436
  216.5 8.0 %copy-start.4 = (bf16[32,256,256]{2,1,0:T(8,128)(2,1)S(1)}, bf16[32,256,256]{2,1,0:T(8,128)(2,1)}, u32[]{:S(2)}) copy-start(bf16[32,256,256]{2,1,0:T(8,128)(2,1)} %get-tuple-element.94.refs_2_) | copy-start | bytes 12582916 | tf_op jit(solution)/shard_map/cond
  216.5 8.0 %copy-start.9 = (f32[8,2,128,128]{3,2,1,0:T(8,128)S(1)}, f32[8,2,128,128]{3,2,1,0:T(8,128)}, u32[]{:S(2)}) copy-start(f32[8,2,128,128]{3,2,1,0:T(8,128)} %get-tuple-element.99.refs_0_) | copy-start | bytes 3145732 | tf_op jit(solution)/shard_map/cond
  216.5 8.0 %copy-start.11 = (f32[8,2,128,128]{3,2,1,0:T(8,128)S(1)}, f32[8,2,128,128]{3,2,1,0:T(8,128)}, u32[]{:S(2)}) copy-start(f32[8,2,128,128]{3,2,1,0:T(8,128)} %get-tuple-element.100.refs_1_) | copy-start | bytes 3145732 | tf_op jit(solution)/shard_map/cond
  224.5 8.5 %copy-start.5 = (bf16[32,256,256]{2,1,0:T(8,128)(2,1)S(1)}, bf16[32,256,256]{2,1,0:T(8,128)(2,1)}, u32[]{:S(2)}) copy-start(bf16[32,256,256]{2,1,0:T(8,128)(2,1)} %get-tuple-element.97.refs_1_.refs_2_) | copy-start | bytes 12582916 | tf_op jit(solution)/shard_map/cond
  224.6 8.5 %copy-start.6 = (bf16[32,256,256]{2,1,0:T(8,128)(2,1)S(1)}, bf16[32,256,256]{2,1,0:T(8,128)(2,1)}, u32[]{:S(2)}) copy-start(bf16[32,256,256]{2,1,0:T(8,128)(2,1)} %get-tuple-element.98.refs_2_.refs_3_) | copy-start | bytes 12582916 | tf_op jit(solution)/shard_map/cond
